TPU v7x, 256 devices: a whole 4x4x8 slice. The times are simulated.
256 devices in a mesh: dp: 8 (over y, core), expert: 32 (over z, x).
Axes of the slice: x: 4, y: 4, z: 8, core: 2. Of those that a mesh axis runs over, the one named last changes fastest.
Arguments:
- tokens: bfloat16 [32768, 2048], P(('dp', 'expert')), may hold values from -6 to 6
- cotangent: bfloat16 [32768, 2048], P(('dp', 'expert')), may hold values from -1.5 to 1.5
- routes: int32 [32768, 1], P(('dp', 'expert')), may hold values from 0 to 31; in each aligned block of 128 rows (0 to 127, 128 to 255, ...) at most 5 rows name the same one
- gates: bfloat16 [32768, 1], P(('dp', 'expert')), may hold values from 0.049804688 to 0.59765625
- loss_mask: int32 [32768], P(('dp', 'expert')), may hold values 0 or 1
- w_gate: bfloat16 [32, 1536, 2048], P('expert', 'dp'), may hold values from -0.125 to 0.125
- w_up: bfloat16 [32, 1536, 2048], P('expert', 'dp'), may hold values from -0.125 to 0.125
- w_down: bfloat16 [32, 1536, 2048], P('expert', 'dp'), may hold values from -0.15625 to 0.15625
Outputs:
- grad_tokens: bfloat16 [32768, 2048], P(('dp', 'expert'))
- grad_gates: float32 [32768, 1], P(('dp', 'expert'))
- grad_w_gate: bfloat16 [32, 1536, 2048], P('expert', 'dp')
- grad_w_up: bfloat16 [32, 1536, 2048], P('expert', 'dp')
- grad_w_down: bfloat16 [32, 1536, 2048], P('expert', 'dp')
Inputs may be any that keep to these rules, and one draw needn't show every extreme that they name: `routes`: each row names 1 expert. Within the 128 rows of one device, no expert is named by more than 5 rows, a bound that some block reaches.
All inputs are finite; a program needn't handle non-finite values. No bound on the sum of `loss_mask` on one device may be relied on, other than what follows from the above.
Results may differ from a plain program's by a relative error of at most 0.02.
Values may be sent and summed in bfloat16 or wider, within the bound.
No kernel may reach another device: no remote copies, remote signals or barrier semaphores. Data moves between devices by JAX's collectives and lax.ppermute only.
A program may use at most 128 MiB of HBM per device.

v0:
```python
import jax
import jax.numpy as jnp
from jax import lax
from jax.sharding import PartitionSpec as P


def buffer_positions(route_rows, groups, slots, experts):
    flat_routes = route_rows.reshape(groups, -1)
    picked = (
        flat_routes[:, :, None] == jnp.arange(experts, dtype=jnp.int32)[None, None, :]
    ).astype(jnp.int32)
    before = jnp.cumsum(picked, axis=1) - picked
    slot_rank = jnp.sum(before * picked, axis=2)
    group_id = jnp.arange(groups, dtype=jnp.int32)[:, None]
    slot_place = flat_routes * (groups * slots) + group_id * slots + slot_rank
    return slot_place.reshape(-1)


def fill_rows(rows_x, rows_dy, slot_gates, slot_place, top_count, buffer_rows):
    slot_count = slot_place.shape[0]
    source = (
        jnp.full((buffer_rows,), slot_count, jnp.int32)
        .at[slot_place]
        .set(jnp.arange(slot_count, dtype=jnp.int32))
    )
    owner_row = source // top_count
    zero_row = jnp.zeros((1, rows_x.shape[1]), rows_x.dtype)
    buf_x = jnp.concatenate([rows_x, zero_row], axis=0)[owner_row]
    buf_dy = jnp.concatenate([rows_dy, zero_row], axis=0)[owner_row]
    flat_gates = jnp.concatenate(
        [slot_gates.reshape(-1), jnp.zeros((1,), slot_gates.dtype)], axis=0
    )
    buf_gate = flat_gates[source]
    return (buf_x, buf_dy, buf_gate)


def expert_grads(rows_x, rows_dy, rows_gate, w_gate, w_up, w_down):
    pre_gate = jnp.einsum("slcd,lfd->slcf", rows_x, w_gate, preferred_element_type=jnp.float32)
    pre_up = jnp.einsum("slcd,lfd->slcf", rows_x, w_up, preferred_element_type=jnp.float32)
    back_proj = jnp.einsum("slcd,lfd->slcf", rows_dy, w_down, preferred_element_type=jnp.float32)
    sigmoid_gate = jax.nn.sigmoid(pre_gate)
    activated = pre_gate * sigmoid_gate
    hidden = (activated * pre_up).astype(jnp.bfloat16)
    weight = rows_gate.astype(jnp.float32)[..., None]
    d_hidden = weight * back_proj
    d_pre_gate = (
        d_hidden * pre_up * sigmoid_gate * (1.0 + pre_gate * (1.0 - sigmoid_gate))
    ).astype(jnp.bfloat16)
    d_pre_up = (d_hidden * activated).astype(jnp.bfloat16)
    scaled_dy = (weight * rows_dy.astype(jnp.float32)).astype(jnp.bfloat16)
    gate_part = jnp.sum(hidden.astype(jnp.float32) * back_proj, axis=3).astype(jnp.bfloat16)
    grad_down = jnp.einsum(
        "slcf,slcd->lfd", hidden, scaled_dy, preferred_element_type=jnp.float32
    ).astype(jnp.bfloat16)
    grad_gate = jnp.einsum(
        "slcf,slcd->lfd", d_pre_gate, rows_x, preferred_element_type=jnp.float32
    ).astype(jnp.bfloat16)
    grad_up = jnp.einsum(
        "slcf,slcd->lfd", d_pre_up, rows_x, preferred_element_type=jnp.float32
    ).astype(jnp.bfloat16)
    row_part = jnp.einsum("slcf,lfd->slcd", d_pre_gate, w_gate, preferred_element_type=jnp.float32)
    row_part = (
        row_part + jnp.einsum("slcf,lfd->slcd", d_pre_up, w_up, preferred_element_type=jnp.float32)
    ).astype(jnp.bfloat16)
    return (row_part, gate_part, grad_gate, grad_up, grad_down)


def shards(tokens, cotangent, routes, gates, loss_mask, w_gate, w_up, w_down):
    local_count = w_gate.shape[0]
    expert_ranks = lax.axis_size("expert")
    experts = local_count * expert_ranks
    top_count = routes.shape[1]
    own_tokens = tokens.shape[0]
    model_width = tokens.shape[1]
    capacity = max(2, 5 * own_tokens * top_count // (4 * experts))
    masked = jnp.where((loss_mask == 1)[:, None], cotangent, jnp.zeros_like(cotangent))
    groups = lax.axis_size("dp")
    col_x, col_dy, col_gates = (
        lax.all_gather(tokens, "dp", axis=0, tiled=True),
        lax.all_gather(masked, "dp", axis=0, tiled=True),
        lax.all_gather(gates, "dp", axis=0, tiled=True),
    )
    col_routes = lax.all_gather(routes, "dp", axis=0, tiled=True)
    slot_place = buffer_positions(col_routes, groups, capacity, experts)
    buffer_rows = experts * groups * capacity
    buf_x, buf_dy, buf_gate = fill_rows(
        col_x, col_dy, col_gates, slot_place, top_count, buffer_rows
    )
    send_shape = (expert_ranks, local_count, groups * capacity)
    arrived_x, arrived_dy, arrived_gate = (
        lax.all_to_all(
            buf_x.reshape(send_shape + (model_width,)),
            "expert",
            split_axis=0,
            concat_axis=0,
            tiled=True,
        ),
        lax.all_to_all(
            buf_dy.reshape(send_shape + (model_width,)),
            "expert",
            split_axis=0,
            concat_axis=0,
            tiled=True,
        ),
        lax.all_to_all(
            buf_gate.reshape(send_shape), "expert", split_axis=0, concat_axis=0, tiled=True
        ),
    )
    row_part, gate_part, grad_gate, grad_up, grad_down = expert_grads(
        arrived_x, arrived_dy, arrived_gate, w_gate, w_up, w_down
    )
    back_rows, back_gate = (
        lax.all_to_all(row_part, "expert", split_axis=0, concat_axis=0, tiled=True),
        lax.all_to_all(gate_part, "expert", split_axis=0, concat_axis=0, tiled=True),
    )
    flat_rows = back_rows.reshape(buffer_rows, model_width)
    flat_gate = back_gate.reshape(buffer_rows)
    slot_rows = jnp.sum(
        flat_rows[slot_place]
        .astype(jnp.float32)
        .reshape(groups * own_tokens, top_count, model_width),
        axis=1,
    )
    slot_gate = flat_gate[slot_place].astype(jnp.float32).reshape(groups * own_tokens, top_count)
    token_rows, token_gate = (
        lax.psum_scatter(
            slot_rows.astype(jnp.bfloat16), "dp", scatter_dimension=0, tiled=True
        ).astype(jnp.float32),
        lax.psum_scatter(
            slot_gate.astype(jnp.bfloat16), "dp", scatter_dimension=0, tiled=True
        ).astype(jnp.float32),
    )
    return (token_rows.astype(jnp.bfloat16), token_gate, grad_gate, grad_up, grad_down)


def solution(mesh):
    placed = (
        P(("dp", "expert"), None),
        P(("dp", "expert"), None),
        P(("dp", "expert"), None),
        P(("dp", "expert"), None),
        P(("dp", "expert")),
        P("expert", "dp", None),
        P("expert", "dp", None),
        P("expert", "dp", None),
    )
    return jax.shard_map(
        shards,
        mesh=mesh,
        in_specs=placed,
        out_specs=(
            P(("dp", "expert"), None),
            P(("dp", "expert"), None),
            P("expert", "dp", None),
            P("expert", "dp", None),
            P("expert", "dp", None),
        ),
        check_vma=False,
    )
```

profile of v0, /device:TPU:2, one launch (start us, length us, event | category | flops | bytes accessed | tf_op | source)
XLA Modules:
  0.0 532.1 jit_solution(6425582840578835937)
XLA Ops:
  7.2 0.0 all-gather.5.cloned.1.call-start
  7.2 0.7 all-gather.5.cloned.1.call-update
  7.9 10.9 %all_gather.13 = s32[1024,1]{0,1:T(1,128)S(1)} all-gather(s32[128,1]{0,1:T(1,128)} %param.10), channel_id=1, replica_groups=mesh['dp'=8,'expert'=32] {'dp'}, dimensions={0}, use_global_device_ids=true | all-gather | bytes 4608 | tf_op jit(solution)/shard_map/all_gather | solution.py:83
  18.8 0.1 copy.19
  18.9 2.5 select_reduce_fusion
  21.5 8.2 %all_gather.12 = bf16[1024,1]{0,1:T(2,128)(2,1)S(1)} all-gather(bf16[128,1]{0,1:T(2,128)(2,1)} %param.11), channel_id=1, replica_groups=mesh['dp'=8,'expert'=32] {'dp'}, dimensions={0}, use_global_device_ids=true | all-gather | bytes 2304 | tf_op jit(solution)/shard_map/all_gather | solution.py:81
  29.8 0.1 add.49
  29.9 4.3 scatter_custom_fusion
  34.2 8.0 %gather_fusion = bf16[1280]{0:T(1024)(128)(2,1)S(1)} fusion(bf16[1025]{0:T(1024)(128)(2,1)S(1)} %pad_maximum_fusion, s32[2048]{0:T(1024)S(1)} %pad_clamp_fusion), kind=kCustom, calls=%fused_computation | custom fusion | bytes 10240 | tf_op jit(solution)/shard_map/gather | solution.py:33
  42.2 0.7 reshape.183
  42.9 11.6 %all-to-all-start = ((bf16[32,1,40]{2,1,0:T(2,128)(2,1)}), bf16[32,1,40]{2,1,0:T(2,128)(2,1)S(1)}, u32[]{:S(2)}, u32[]{:S(2)}) async-start(bf16[32,1,40]{2,1,0:T(2,128)(2,1)} %reshape.183), calls=%async_computation | async-start | bytes 32768 | tf_op jit(solution)/shard_map/all_to_all | solution.py:105
  54.5 0.0 all-gather.5.cloned.1.call-done
  54.6 4.7 concatenate.11
  59.3 13.5 %gather_fusion.2 = bf16[1280,2048]{1,0:T(8,128)(2,1)} fusion(bf16[1025,2048]{1,0:T(8,128)(2,1)} %concatenate.11, s32[2048]{0:T(1024)S(1)} %pad_clamp_fusion), kind=kCustom, calls=%fused_computation.2 | custom fusion | bytes 10490880 | tf_op jit(solution)/shard_map/gather | solution.py:28
  72.9 10.0 %all-to-all-start.2 = ((bf16[32,1,40,2048]{3,2,1,0:T(8,128)(2,1)}), bf16[32,1,40,2048]{3,2,1,0:T(8,128)(2,1)}, u32[]{:S(2)}, u32[]{:S(2)}) async-start(bf16[32,1,40,2048]{3,2,1,0:T(8,128)(2,1)} %bitcast.140), calls=%async_computation.2 | async-start | bytes 10485760 | tf_op jit(solution)/shard_map/all_to_all | solution.py:91
  82.8 0.0 all-gather.3.cloned.1.call-start
  82.9 0.9 broadcast_select_fusion
  83.8 0.0 all-gather.3.cloned.1.call-update
  83.8 36.6 %all-gather.3.cloned.1.call-done = bf16[1024,2048]{1,0:T(8,128)(2,1)} async-done(((bf16[128,2048]{1,0:T(8,128)(2,1)}), bf16[1024,2048]{1,0:T(8,128)(2,1)}) %all-gather.3.cloned.1.call-update) | async-done | bytes 4194320 | tf_op jit(solution)/shard_map/all_gather | solution.py:80
  120.5 4.7 concatenate.10
  125.2 13.6 %gather_fusion.1 = bf16[1280,2048]{1,0:T(8,128)(2,1)} fusion(bf16[1025,2048]{1,0:T(8,128)(2,1)} %concatenate.10, s32[2048]{0:T(1024)S(1)} %pad_clamp_fusion), kind=kCustom, calls=%fused_computation.1 | custom fusion | bytes 10490880 | tf_op jit(solution)/shard_map/gather | solution.py:29
  138.8 63.9 %all-to-all-done.2 = bf16[32,1,40,2048]{3,2,1,0:T(8,128)(2,1)} async-done(((bf16[32,1,40,2048]{3,2,1,0:T(8,128)(2,1)}), bf16[32,1,40,2048]{3,2,1,0:T(8,128)(2,1)}, u32[]{:S(2)}, u32[]{:S(2)}) %all-to-all-start.2) | async-done | bytes 5242912 | tf_op jit(solution)/shard_map/all_to_all | solution.py:91
  202.7 7.0 %all-to-all-start.1 = ((bf16[32,1,40,2048]{3,2,1,0:T(8,128)(2,1)}), bf16[32,1,40,2048]{3,2,1,0:T(8,128)(2,1)}, u32[]{:S(2)}, u32[]{:S(2)}) async-start(bf16[32,1,40,2048]{3,2,1,0:T(8,128)(2,1)} %bitcast.141), calls=%async_computation.1 | async-start | bytes 10485760 | tf_op jit(solution)/shard_map/all_to_all | solution.py:98
  209.8 5.2 fusion.45
  215.0 110.5 %all-to-all-done.1 = bf16[32,1,40,2048]{3,2,1,0:T(8,128)(2,1)} async-done(((bf16[32,1,40,2048]{3,2,1,0:T(8,128)(2,1)}), bf16[32,1,40,2048]{3,2,1,0:T(8,128)(2,1)}, u32[]{:S(2)}, u32[]{:S(2)}) %all-to-all-start.1) | async-done | bytes 5242912 | tf_op jit(solution)/shard_map/all_to_all | solution.py:98
  325.5 4.2 fusion.42
  329.6 5.5 %multiply_reduce_fusion = (bf16[32,40]{1,0:T(8,128)(2,1)S(1)}, bf16[32,1,40,192]{3,2,0,1:T(8,128)(2,1)}, bf16[32,1,40,192]{3,2,0,1:T(8,128)(2,1)S(1)}, bf16[32,40,192]{2,1,0:T(8,128)(2,1)S(1)}) fusion(f32[32,1,40,192]{3,2,0,1:T(8,128)S(1)} %fusion.42, f32[32,1,40,192]{3,2,0,1:T(8,128)S(1)} %copy-done.6, f32[32,40]{1,0:T(8,128)S(1)} %bitcast.143, ...), kind=kOutput, calls=%fused_computation.34 | convolution fusion | flops 1011301120 | bytes 9477632 | tf_op jit(solution)/shard_map/slcd,lfd->slcf/dot_general | solution.py:38
  335.2 0.6 copy.25
  335.8 9.7 %all-to-all-start.4 = ((bf16[32,1,40]{2,1,0:T(2,128)(2,1)}), bf16[32,1,40]{2,1,0:T(2,128)(2,1)S(1)}, u32[]{:S(2)}, u32[]{:S(2)}) async-start(bf16[32,1,40]{2,1,0:T(2,128)(2,1)} %copy.25), calls=%async_computation.5 | async-start | bytes 32768 | tf_op jit(solution)/shard_map/all_to_all | solution.py:114
  345.5 1.5 fusion.52
  347.1 3.9 fusion
  350.9 3.0 all-to-all-done.4
  354.0 6.8 %all-to-all-start.3 = ((bf16[32,1,40,2048]{3,2,1,0:T(8,128)(2,1)}), bf16[32,1,40,2048]{3,2,1,0:T(8,128)(2,1)}, u32[]{:S(2)}, u32[]{:S(2)}) async-start(bf16[32,1,40,2048]{3,2,1,0:T(8,128)(2,1)} %fusion), calls=%async_computation.3 | async-start | bytes 10485760 | tf_op jit(solution)/shard_map/all_to_all | solution.py:113
  360.8 0.0 reduce-scatter.7.cloned.1.call-start
  360.8 0.1 reduce.2
  360.9 0.1 reshape.122
  361.0 6.8 %gather_fusion.4 = bf16[1024]{0:T(1024)(128)(2,1)S(1)} fusion(bf16[1280]{0:T(1024)(128)(2,1)S(1)} %reshape.122, s32[1024]{0:T(1024)S(1)} %broadcast_clamp_fusion), kind=kCustom, calls=%fused_computation.4 | custom fusion | bytes 8192 | tf_op jit(solution)/shard_map/gather | solution.py:124
  367.8 0.9 reshape.184
  368.7 0.0 reduce-scatter.7.cloned.1.call-update
  368.7 0.3 reduce-scatter.5.cloned.1.call-start
  369.0 109.4 %all-to-all-done.3 = bf16[32,1,40,2048]{3,2,1,0:T(8,128)(2,1)} async-done(((bf16[32,1,40,2048]{3,2,1,0:T(8,128)(2,1)}), bf16[32,1,40,2048]{3,2,1,0:T(8,128)(2,1)}, u32[]{:S(2)}, u32[]{:S(2)}) %all-to-all-start.3) | async-done | bytes 5242912 | tf_op jit(solution)/shard_map/all_to_all | solution.py:113
  478.4 12.0 %gather_fusion.3 = bf16[1024,2048]{1,0:T(8,128)(2,1)} fusion(bf16[1280,2048]{1,0:T(8,128)(2,1)} %bitcast.34, s32[1024]{0:T(1024)S(1)} %broadcast_clamp_fusion), kind=kCustom, calls=%fused_computation.3 | custom fusion | bytes 8392704 | tf_op jit(solution)/shard_map/gather | solution.py:119
  490.4 4.6 fusion.33
  495.0 5.0 fusion.36
  500.1 4.8 fusion.39
  504.9 0.8 copy.27
  505.7 0.5 convert_element_type.91
  506.2 19.3 %reduce-scatter.5.cloned.1.call-done = bf16[128,2048]{1,0:T(8,128)(2,1)} async-done(((bf16[1024,2048]{1,0:T(8,128)(2,1)}), bf16[128,2048]{1,0:T(8,128)(2,1)}) %reduce-scatter.5.cloned.1.call-update) | async-done | bytes 524304 | tf_op jit(solution)/shard_map/reduce_scatter | solution.py:126
  (30 shorter events, 0.2 us)
Async XLA Ops:
  7.2 322.5 %copy-start = (bf16[1,192,2048]{2,1,0:T(8,128)(2,1)S(1)}, bf16[1,192,2048]{2,1,0:T(8,128)(2,1)}, u32[]{:S(2)}) copy-start(bf16[1,192,2048]{2,1,0:T(8,128)(2,1)} %param.13) | copy-start | bytes 2359300
  7.2 47.4 %all-gather.5.cloned.1.call-start = ((), (), s32[]{:S(2)}) async-start(), calls=%async_computation.8 | async-start | bytes 4718592 | tf_op jit(solution)/shard_map/all_gather | solution.py:79
  42.9 29.9 %all-to-all-start = ((bf16[32,1,40]{2,1,0:T(2,128)(2,1)}), bf16[32,1,40]{2,1,0:T(2,128)(2,1)S(1)}, u32[]{:S(2)}, u32[]{:S(2)}) async-start(bf16[32,1,40]{2,1,0:T(2,128)(2,1)} %reshape.183), calls=%async_computation | async-start | bytes 32768 | tf_op jit(solution)/shard_map/all_to_all | solution.py:105
  72.9 10.0 %copy-start.5 = (s32[128]{0:T(128)S(1)}, s32[128]{0:T(128)}, u32[]{:S(2)}) copy-start(s32[128]{0:T(128)} %param.12) | copy-start | bytes 1540
  72.9 10.1 %copy-start.3 = (bf16[128,2048]{1,0:T(8,128)(2,1)S(1)}, bf16[128,2048]{1,0:T(8,128)(2,1)}, u32[]{:S(2)}) copy-start(bf16[128,2048]{1,0:T(8,128)(2,1)} %param.9) | copy-start | bytes 1572868
  72.9 129.8 %all-to-all-start.2 = ((bf16[32,1,40,2048]{3,2,1,0:T(8,128)(2,1)}), bf16[32,1,40,2048]{3,2,1,0:T(8,128)(2,1)}, u32[]{:S(2)}, u32[]{:S(2)}) async-start(bf16[32,1,40,2048]{3,2,1,0:T(8,128)(2,1)} %bitcast.140), calls=%async_computation.2 | async-start | bytes 10485760 | tf_op jit(solution)/shard_map/all_to_all | solution.py:91
  82.8 37.6 %all-gather.3.cloned.1.call-start = ((), (), s32[]{:S(2)}) async-start(), calls=%async_computation.7 | async-start | bytes 4718592 | tf_op jit(solution)/shard_map/all_gather | solution.py:80
  202.7 7.1 %copy-start.2 = (bf16[1,192,2048]{2,1,0:T(8,128)(2,1)S(1)}, bf16[1,192,2048]{2,1,0:T(8,128)(2,1)}, u32[]{:S(2)}) copy-start(bf16[1,192,2048]{2,1,0:T(8,128)(2,1)} %param.14) | copy-start | bytes 2359300
  202.7 122.8 %all-to-all-start.1 = ((bf16[32,1,40,2048]{3,2,1,0:T(8,128)(2,1)}), bf16[32,1,40,2048]{3,2,1,0:T(8,128)(2,1)}, u32[]{:S(2)}, u32[]{:S(2)}) async-start(bf16[32,1,40,2048]{3,2,1,0:T(8,128)(2,1)} %bitcast.141), calls=%async_computation.1 | async-start | bytes 10485760 | tf_op jit(solution)/shard_map/all_to_all | solution.py:98
  209.7 115.7 %copy-start.4 = (bf16[1,192,2048]{2,1,0:T(8,128)(2,1)S(1)}, bf16[1,192,2048]{2,1,0:T(8,128)(2,1)}, u32[]{:S(2)}) copy-start(bf16[1,192,2048]{2,1,0:T(8,128)(2,1)} %param.15) | copy-start | bytes 2359300
  325.5 4.2 copy-start.6
  335.8 18.2 %all-to-all-start.4 = ((bf16[32,1,40]{2,1,0:T(2,128)(2,1)}), bf16[32,1,40]{2,1,0:T(2,128)(2,1)S(1)}, u32[]{:S(2)}, u32[]{:S(2)}) async-start(bf16[32,1,40]{2,1,0:T(2,128)(2,1)} %copy.25), calls=%async_computation.5 | async-start | bytes 32768 | tf_op jit(solution)/shard_map/all_to_all | solution.py:114
  354.0 124.5 %all-to-all-start.3 = ((bf16[32,1,40,2048]{3,2,1,0:T(8,128)(2,1)}), bf16[32,1,40,2048]{3,2,1,0:T(8,128)(2,1)}, u32[]{:S(2)}, u32[]{:S(2)}) async-start(bf16[32,1,40,2048]{3,2,1,0:T(8,128)(2,1)} %fusion), calls=%async_computation.3 | async-start | bytes 10485760 | tf_op jit(solution)/shard_map/all_to_all | solution.py:113
  360.8 144.1 %reduce-scatter.7.cloned.1.call-start = ((), (), s32[]{:S(2)}) async-start(), calls=%async_computation.10 | async-start | bytes 294912
  368.7 156.8 %reduce-scatter.5.cloned.1.call-start = ((), (), s32[]{:S(2)}) async-start(), calls=%async_computation.9 | async-start | bytes 4718592 | tf_op jit(solution)/shard_map/reduce_scatter | solution.py:126
  495.0 5.0 copy-start.7
  500.1 25.5 %copy-start.1 = (bf16[1,192,2048]{2,1,0:T(8,128)(2,1)S(1)}, bf16[1,192,2048]{2,1,0:T(8,128)(2,1)}, u32[]{:S(2)}) copy-start(bf16[1,192,2048]{2,1,0:T(8,128)(2,1)} %param.13) | copy-start | bytes 2359300
Sparse Core Ops, SparseCore 0:
  9.9 37.6 all-gather.4
  86.1 34.3 all-gather.2
  368.9 33.6 reduce-scatter.6
  490.6 34.9 reduce-scatter.4
where the time goes:
time: 533 us; the launch traced here: 532 us
  waiting for transfers between devices  344 us (65%)
  local copies, waits for them, and re-layouts  71.1 us (13%)
  starting transfers between devices  45.5 us (9%)
  matrix products  34.7 us (7%)
  blocking collectives  19.1 us (4%)
  between operations  14 us (3%)
    all_to_all x1, waiting for transfers between devices, shards(): lax.all_to_all(buf_dy.reshape(send_shape + (model_width,)), 'expert', spl...  110 us
    all_to_all x1, waiting for transfers between devices, shards(): lax.all_to_all(row_part, 'expert', split_axis=0, concat_axis=0, tiled=True)  109 us
    all_to_all x1, waiting for transfers between devices, shards(): lax.all_to_all(buf_x.reshape(send_shape + (model_width,)), 'expert', spli...  63.9 us
    all_gather x1, waiting for transfers between devices, shards(): lax.all_gather(masked, 'dp', axis=0, tiled=True)  36.6 us
    reduce_scatter x1, waiting for transfers between devices, shards(): lax.psum_scatter(slot_rows.astype(jnp.bfloat16), 'dp', scatter_dimension=...  19.3 us
    gather x1, local copies, waits for them, and re-layouts, fill_rows(): buf_dy = jnp.concatenate([rows_dy, zero_row], axis=0)[owner_row]  13.6 us
    gather x1, local copies, waits for them, and re-layouts, fill_rows(): buf_x = jnp.concatenate([rows_x, zero_row], axis=0)[owner_row]  13.5 us
    gather x1, local copies, waits for them, and re-layouts, shards(): flat_rows[slot_place].astype(jnp.float32)  12 us
  transfers between devices with their start and end apart: 9, of which 6 were waited for; matrix products, arithmetic and copies ran while one was open for 19% of the time, Pallas kernels for 0%

commit v1 on v0

v1 whole, which is shorter than its diff:
```python
import functools
import math

import jax
import jax.numpy as jnp
from jax import lax
from jax.experimental import pallas as pl
from jax.experimental.pallas import tpu as pltpu
from jax.sharding import Mesh, PartitionSpec as P

SLOTS = 5
BF = jnp.bfloat16
F32 = jnp.float32
LIMIT = 56 * 1024 * 1024


def dot(a, b, dims=((1,), (0,))):
    return lax.dot_general(a, b, (dims, ((), ())), preferred_element_type=F32)


def iota(shape, axis):
    return lax.broadcasted_iota(jnp.int32, shape, axis)


def params():
    return pltpu.CompilerParams(vmem_limit_bytes=LIMIT)


def vmem(count):
    return [pl.BlockSpec(memory_space=pltpu.VMEM)] * count


def places(routes_row, experts):
    tokens = routes_row.shape[1]
    picked = iota((experts, tokens), 0) == routes_row
    hot = jnp.where(picked, 1.0, 0.0).astype(BF)
    earlier = jnp.where(iota((tokens, tokens), 0) < iota((tokens, tokens), 1), 1.0, 0.0).astype(BF)
    before = dot(hot, earlier)
    rank = jnp.sum(jnp.where(picked, before, 0.0), axis=0, keepdims=True).astype(jnp.int32)
    return routes_row, rank


def main_rows(expert, rank, half):
    return jnp.where(rank < SLOTS - 1, expert * 8 + half * 4 + rank, -1)


def last_rows(expert, rank, piece):
    return jnp.where(rank == SLOTS - 1, expert * 8 + piece, -1)


def one_hot(rows, target):
    return iota((rows, target.shape[1]), 0) == target


def pack_tokens(routes_ref, gates_ref, mask_ref, x_ref, dy_ref, px_ref, pdy_ref):
    width = x_ref.shape[1]
    rows = px_ref.shape[0]
    half, piece = width // 2, width // 8
    expert, rank = places(routes_ref[...], rows // 8)
    weight = jnp.where(mask_ref[...] == 1, gates_ref[...].astype(F32), 0.0)
    for src, dst, scale in ((x_ref, px_ref, None), (dy_ref, pdy_ref, weight)):
        def spread(target):
            value = 1.0 if scale is None else scale
            return jnp.where(one_hot(rows, target), value, 0.0).astype(BF)

        main = dot(spread(main_rows(expert, rank, 0)), src[:, :half])
        main += dot(spread(main_rows(expert, rank, 1)), src[:, half:])
        dst[:, :half] = main.astype(BF)
        last = jnp.zeros((rows, piece), F32)
        for k in range(8):
            last += dot(spread(last_rows(expert, rank, k)), src[:, k * piece : (k + 1) * piece])
        dst[:, half : half + piece] = last.astype(BF)


def unpack_tokens(routes_ref, gates_ref, r_ref, out_ref, gate_ref):
    width = out_ref.shape[1]
    rows = r_ref.shape[0]
    half, piece = width // 2, width // 8
    expert, rank = places(routes_ref[...], rows // 8)

    def spread(target):
        return jnp.where(one_hot(rows, target), 1.0, 0.0).astype(BF)

    across = ((0,), (0,))
    mains = [dot(spread(main_rows(expert, rank, h)), r_ref[:, :half], across) for h in (0, 1)]
    for k in range(8):
        last = dot(spread(last_rows(expert, rank, k)), r_ref[:, half : half + piece], across)
        at = (k % 4) * piece
        out_ref[:, k * piece : (k + 1) * piece] = (mains[k // 4][:, at : at + piece] + last).astype(BF)
    lanes = r_ref[:, half + piece :]
    summed = dot(lanes, spread(expert * 8 + rank), across)
    gate_ref[...] = summed[0:1, :] / gates_ref[...].astype(F32)


def main_order(rows):
    at = iota((rows, rows), 1)
    inner = at % (rows // 2)
    return iota((rows, rows), 0) == (inner // 4) * 8 + (at // (rows // 2)) * 4 + inner % 4


def last_order(rows):
    at = iota((rows, rows), 1)
    return iota((rows, rows), 0) == (at % (rows // 8)) * 8 + at // (rows // 8)


def expert_rows(xs, dys, weights, outs, x_ref, dy_ref, act_refs, wgu, wd, pre, back, dcat):
    rows = xs[0].shape[0]
    width = x_ref.shape[1]
    half, piece = width // 2, width // 8
    units = weights[0].shape[0]
    both = 2 * units
    four = rows // 2
    lone = rows // 8
    block = four + lone
    for i, (gate_w, up_w, down_w) in enumerate((weights[:3], weights[3:])):
        wgu[i * units : (i + 1) * units] = gate_w[...]
        wgu[both + i * units : both + (i + 1) * units] = up_w[...]
        wd[i * units : (i + 1) * units] = down_w[...]
    order = jnp.where(main_order(rows), 1.0, 0.0).astype(BF)
    order_last = jnp.where(last_order(rows), 1.0, 0.0).astype(BF)
    across = ((0,), (0,))
    lanes_of = ((1,), (1,))
    for parts, dst in ((xs, x_ref), (dys, dy_ref)):
        for b in range(4):
            if b < 3:
                got_main, got_last = parts[b][:, :half], parts[b][:, half : half + piece]
            else:
                got = jnp.concatenate([parts[3][...], parts[4][...]], axis=0)
                got_main, got_last = got[:, :half], got[:, half : half + piece]
            main = dot(order, got_main, across).astype(BF)
            last = dot(order_last, got_last, across).astype(BF)
            at = b * block
            dst[at : at + four, :half] = main[:four]
            dst[at : at + four, half:] = main[four:]
            for k in range(8):
                dst[at + four : at + block, k * piece : (k + 1) * piece] = last[k * lone : (k + 1) * lone]
    pre[...] = dot(x_ref[...], wgu[...], lanes_of)
    back[...] = dot(dy_ref[...], wd[...], lanes_of)
    hid_ref = act_refs[0]
    total = 4 * block
    step = math.gcd(block, 32)
    gates = []
    for r in range(0, total, step):
        at = slice(r, r + step)
        gate, up, bp = pre[at, :both], pre[at, both:], back[at, :]
        sig = jax.nn.sigmoid(gate)
        silu = gate * sig
        hidden = (silu * up).astype(BF)
        hid_ref[at, :] = hidden
        dcat[at, :both] = (bp * up * sig * (1.0 + gate * (1.0 - sig))).astype(BF)
        dcat[at, both:] = (bp * silu).astype(BF)
        gates.append(jnp.sum(hidden.astype(F32) * bp, axis=1, keepdims=True))
    act_refs[1][...] = dcat[...]
    for b in range(4):
        at = b * block
        part = dot(dcat[at : at + block, :], wgu[...]).astype(BF)
        stacked = jnp.concatenate([part[:four, :half], part[:four, half:]], axis=0)
        outs[b][:, :half] = dot(order, stacked).astype(BF)
        stacked = jnp.concatenate([part[four:, k * piece : (k + 1) * piece] for k in range(8)], axis=0)
        outs[b][:, half : half + piece] = dot(order_last, stacked).astype(BF)
        column = jnp.concatenate(gates[at // step : (at + block) // step], axis=0)
        column = jnp.broadcast_to(column.astype(BF), (block, 128))
        main = dot(order[:, :four], column[:four])
        pick = iota((rows, lone), 0) == iota((rows, lone), 1) * 8 + 4
        main += dot(jnp.where(pick, 1.0, 0.0).astype(BF), column[four:])
        outs[b][:, half + piece :] = main.astype(BF)


def call_expert_rows(xs, dys, weights):
    rows, packed = xs[0].shape
    units, width = weights[0].shape
    total = 4 * (rows // 2 + rows // 8)

    def body(*refs):
        ins, rest = refs[:16], refs[16:]
        outs, rest = rest[:8], rest[8:]
        expert_rows(ins[:5], ins[5:10], ins[10:16], outs[:4], outs[4], outs[5], outs[6:8], *rest)

    return pl.pallas_call(
        body,
        out_shape=[jax.ShapeDtypeStruct((rows, packed + 128), BF)] * 4
        + [jax.ShapeDtypeStruct((total, width), BF)] * 2
        + [jax.ShapeDtypeStruct((total, 2 * units), BF), jax.ShapeDtypeStruct((total, 4 * units), BF)],
        in_specs=vmem(16),
        out_specs=vmem(8),
        scratch_shapes=[
            pltpu.VMEM((4 * units, width), BF),
            pltpu.VMEM((2 * units, width), BF),
            pltpu.VMEM((total, 4 * units), F32),
            pltpu.VMEM((total, 2 * units), F32),
            pltpu.VMEM((total, 4 * units), BF),
        ],
        compiler_params=params(),
        cost_estimate=pl.CostEstimate(
            flops=10 * 2 * total * units * width, bytes_accessed=24 * total * width, transcendentals=total * 2 * units
        ),
    )(*xs, *dys, *weights)


def grad_block(own, has_more, units, *refs):
    hid_ref, d_ref, x_ref, dy_ref = refs[:4]
    more = refs[4 : 4 + 3 * has_more]
    outs = refs[4 + 3 * has_more :]
    both = 2 * units
    first = 0 if own else units
    across = ((0,), (0,))
    down = dot(hid_ref[...], dy_ref[...], across)[first : first + units]
    pair = dot(d_ref[...], x_ref[...], across)
    gate = pair[first : first + units]
    up = pair[both + first : both + first + units]
    for i, value in enumerate((gate, up, down)):
        if has_more:
            value = value + more[i][...].astype(F32)
        outs[i][...] = value.astype(BF)


def call_grads(own, hid, d, x, dy, more):
    total, width = x.shape
    units = hid.shape[1] // 2
    cols = 512
    full = lambda a: pl.BlockSpec(a.shape, lambda j: (0, 0))
    piece = lambda rows: pl.BlockSpec((rows, cols), lambda j: (0, j))
    return pl.pallas_call(
        functools.partial(grad_block, own, bool(more), units),
        grid=(width // cols,),
        out_shape=[jax.ShapeDtypeStruct((units, width), BF)] * 3,
        in_specs=[full(hid), full(d), piece(total), piece(total)] + [piece(units)] * len(more),
        out_specs=[piece(units)] * 3,
        compiler_params=params(),
        cost_estimate=pl.CostEstimate(
            flops=6 * 2 * total * units * width, bytes_accessed=4 * total * width + 12 * units * width, transcendentals=0
        ),
    )(hid, d, x, dy, *more)


def along(v, axis, size, by):
    return lax.ppermute(v, axis, [(i, (i + by) % size) for i in range(size)])


def shards(tokens, cotangent, routes, gates, loss_mask, w_gate, w_up, w_down):
    experts = lax.axis_size("z") * lax.axis_size("x")
    ring = lax.axis_size("y")
    count, width = tokens.shape
    packed = width // 2 + width // 8
    rows = experts * 8
    flip = lambda v: along(v, "core", 2, 1)
    mine = [w_gate[0], w_up[0], w_down[0]]
    theirs = [flip(w) for w in mine]
    routes_row = routes.reshape(1, count)
    gates_row = gates.reshape(1, count)
    mask_row = loss_mask.reshape(1, count)
    px, pdy = pl.pallas_call(
        pack_tokens,
        out_shape=[jax.ShapeDtypeStruct((rows, packed), BF)] * 2,
        in_specs=vmem(5),
        out_specs=vmem(2),
        compiler_params=params(),
    )(routes_row, gates_row, mask_row, tokens, cotangent)

    def dispatch(v):
        chunks = v.reshape(experts, 8, v.shape[1])
        return lax.all_to_all(chunks, ("z", "x"), 0, 0, tiled=True).reshape(v.shape)

    def gather(v):
        low, high = along(v, "y", ring, 1), along(v, "y", ring, -1)
        cut = rows // 2
        return [v, low, high, along(low[:cut], "y", ring, 1), along(high[cut:], "y", ring, -1)]

    xs = gather(dispatch(px))
    dys = gather(dispatch(pdy))
    *parts, x_all, dy_all, hid, d = call_expert_rows(xs, dys, mine + theirs)
    home = parts[0].astype(F32)
    for part, by in zip(parts[1:], (-1, 1, 2)):
        home = home + along(part, "y", ring, by).astype(F32)
    given = call_grads(False, hid, d, x_all, dy_all, [])
    taken = [flip(g) for g in given]
    returned = dispatch(home.astype(BF))
    grads = call_grads(True, hid, d, x_all, dy_all, taken)
    grad_tokens, grad_gates = pl.pallas_call(
        unpack_tokens,
        out_shape=[jax.ShapeDtypeStruct((count, width), BF), jax.ShapeDtypeStruct((1, count), F32)],
        in_specs=vmem(3),
        out_specs=vmem(2),
        compiler_params=params(),
    )(routes_row, gates_row, returned)
    return (grad_tokens, grad_gates.reshape(count, 1), *[g[None] for g in grads])


def solution(mesh):
    devices = mesh.devices
    fine = Mesh(devices.reshape(devices.shape[0] // 2, 2, -1, 4), ("y", "core", "z", "x"))
    row = P(("y", "core", "z", "x"))
    weight = P(("z", "x"), ("y", "core"))
    return jax.shard_map(
        shards,
        mesh=fine,
        in_specs=(row,) * 5 + (weight,) * 3,
        out_specs=(row,) * 2 + (weight,) * 3,
        check_vma=False,
    )
```

time: 533 us -> 178 us (0.33)
  waiting for transfers between devices: 344 us -> 68.9 us
  local copies, waits for them, and re-layouts: 71.1 us -> 2.62 us
  Pallas kernels: 0 us -> 36.3 us
  matrix products: 34.7 us -> 0 us
  between operations: 14 us -> 0.86 us
  blocking collectives: 19.1 us -> 31.4 us
  starting transfers between devices: 45.5 us -> 34 us
    all_to_all x5 -> x2, waiting for transfers between devices: 287 us -> 15 us  [dispatch(): return lax.all_to_all(chunks, ('z', 'x'), 0, 0, tiled=True).reshape(v.shape)]
    gather x6 -> x0, local copies, waits for them, and re-layouts: 54.8 us -> none  [the longest x1 13.6 us: fill_rows(): buf_dy = jnp.concatenate([rows_dy, zero_row], axis=0)[owner_row]]
    ppermute x0 -> x17, waiting for transfers between devices: none -> 53.9 us  [along(): return lax.ppermute(v, axis, [(i, (i + by) % size) for i in range(size)])]
    all_gather x2 -> x0, waiting for transfers between devices: 36.7 us -> none  [the longest x1 36.6 us: shards(): lax.all_gather(masked, 'dp', axis=0, tiled=True)]
    pallas_call x0 -> x5, Pallas kernels: none -> 36.3 us  [the longest x2 15.3 us: call_grads(): pl.pallas_call(functools.partial(grad_block, own, bool(more), units), gri...]
    dot_general x8 -> x0, matrix products: 34.7 us -> none  [the longest x1 5.52 us: expert_grads(): jnp.einsum('slcd,lfd->slcf', rows_x, w_gate, preferred_element_type=jnp.f...]
    all_to_all x0 -> x1, blocking collectives: none -> 31.4 us  [dispatch(): return lax.all_to_all(chunks, ('z', 'x'), 0, 0, tiled=True).reshape(v.shape)]
    all_to_all x5 -> x2, starting transfers between devices: 45.1 us -> 17.1 us  [dispatch(): return lax.all_to_all(chunks, ('z', 'x'), 0, 0, tiled=True).reshape(v.shape)]
  transfers between devices with their start and end apart: 9 -> 19, of which waited for: 6 -> 11; matrix products, arithmetic and copies ran while one was open for 19% -> 0% of each run, Pallas kernels for 0% -> 9%
where the time goes in v1:
time: 178 us; the launch traced here: 176 us
  waiting for transfers between devices  68.9 us (39%)
  Pallas kernels  36.3 us (20%)
  starting transfers between devices  34 us (19%)
  blocking collectives  31.4 us (18%)
  local copies, waits for them, and re-layouts  2.62 us (1%)
  other arithmetic  2.37 us (1%)
    ppermute x17, waiting for transfers between devices, along(): return lax.ppermute(v, axis, [(i, (i + by) % size) for i in range(size)])  53.9 us
    all_to_all x1, blocking collectives, dispatch(): return lax.all_to_all(chunks, ('z', 'x'), 0, 0, tiled=True).reshape(v.shape)  31.4 us
    all_to_all x2, starting transfers between devices, dispatch(): return lax.all_to_all(chunks, ('z', 'x'), 0, 0, tiled=True).reshape(v.shape)  17.1 us
    ppermute x17, starting transfers between devices, along(): return lax.ppermute(v, axis, [(i, (i + by) % size) for i in range(size)])  16.8 us
    pallas_call x2, Pallas kernels, call_grads(): pl.pallas_call(functools.partial(grad_block, own, bool(more), units), gri...  15.3 us
    all_to_all x2, waiting for transfers between devices, dispatch(): return lax.all_to_all(chunks, ('z', 'x'), 0, 0, tiled=True).reshape(v.shape)  15 us
    pallas_call x1, Pallas kernels, call_expert_rows(): pl.pallas_call(body, out_shape=[jax.ShapeDtypeStruct((rows, packed + 128)...  15 us
  transfers between devices with their start and end apart: 19, of which 11 were waited for; matrix products, arithmetic and copies ran while one was open for 0% of the time, Pallas kernels for 9%

profile of v1, /device:TPU:2, one launch (start us, length us, event | category | flops | bytes accessed | tf_op | source)
XLA Modules:
  0.0 176.4 jit_solution(1061437017926139519)
XLA Ops:
  0.6 3.5 %shard_map.119 = (bf16[256,1280]{1,0:T(8,128)(2,1)}, bf16[256,1280]{1,0:T(8,128)(2,1)}) custom-call(s32[1,128]{1,0:T(1,128)} %bitcast.26, bf16[1,128]{1,0:T(2,128)(2,1)} %bitcast.28, s32[1,128]{1,0:T(1,128)} %bitcast.30, bf16[128,2048]{1,0:T(8,128)(2,1)} %x_ref.1, bf16[128,2048]{1,0:T(8,128)(2,1)} %dy_ref.1), custom_call_target="tpu_custom_call" | custom-call | tf_op jit(solution)/shard_map/pallas_call | solution.py:252
  4.1 31.4 %all_to_all.15 = bf16[32,8,1280]{2,1,0:T(8,128)(2,1)S(1)} all-to-all(bf16[32,8,1280]{2,1,0:T(8,128)(2,1)} %bitcast.25), channel_id=1, replica_groups=mesh['y'=4,'core'=2,'z'=8,'x'=4] {'z','x'}, dimensions={0} | all-to-all | bytes 1310720 | tf_op jit(solution)/shard_map/all_to_all | solution.py:262
  35.5 5.6 %all-to-all-start.1 = ((bf16[32,8,1280]{2,1,0:T(8,128)(2,1)}), bf16[32,8,1280]{2,1,0:T(8,128)(2,1)S(1)}, u32[]{:S(2)}, u32[]{:S(2)}) async-start(bf16[32,8,1280]{2,1,0:T(8,128)(2,1)} %bitcast.24), calls=%async_computation.1 | async-start | bytes 1310720 | tf_op jit(solution)/shard_map/all_to_all | solution.py:262
  41.1 3.1 %collective-permute-start.1 = (bf16[256,1280]{1,0:T(8,128)(2,1)S(1)}, bf16[256,1280]{1,0:T(8,128)(2,1)S(1)}, u32[]{:S(2)}, u32[]{:S(2)}) collective-permute-start(bf16[256,1280]{1,0:T(8,128)(2,1)S(1)} %bitcast.18), channel_id=1, source_target_pairs={{0,192},{64,0},{128,64},{192,128},{1,193},{65,1},{129,65},{193,129... | collective-permute-start | bytes 1966088 | tf_op jit(solution)/shard_map/ppermute | solution.py:237
  44.2 0.0 collective-permute-start
  44.2 0.0 collective-permute-start.8
  44.2 0.5 collective-permute-start.9
  44.7 15.0 %all-to-all-done.1 = bf16[32,8,1280]{2,1,0:T(8,128)(2,1)S(1)} async-done(((bf16[32,8,1280]{2,1,0:T(8,128)(2,1)}), bf16[32,8,1280]{2,1,0:T(8,128)(2,1)S(1)}, u32[]{:S(2)}, u32[]{:S(2)}) %all-to-all-start.1) | async-done | bytes 655392 | tf_op jit(solution)/shard_map/all_to_all | solution.py:262
  59.7 3.0 %collective-permute-start.5 = (bf16[256,1280]{1,0:T(8,128)(2,1)S(1)}, bf16[256,1280]{1,0:T(8,128)(2,1)S(1)}, u32[]{:S(2)}, u32[]{:S(2)}) collective-permute-start(bf16[256,1280]{1,0:T(8,128)(2,1)S(1)} %bitcast.21), channel_id=1, source_target_pairs={{0,192},{64,0},{128,64},{192,128},{1,193},{65,1},{129,65},{193,129... | collective-permute-start | bytes 1966088 | tf_op jit(solution)/shard_map/ppermute | solution.py:237
  62.7 0.0 collective-permute-done.1.refs_2_
  62.7 0.0 collective-permute-start.4
  62.7 0.0 collective-permute-done.refs_1_
  62.8 0.1 collective-permute-start.10
  62.9 11.1 %collective-permute-done.5.refs_7_ = bf16[256,1280]{1,0:T(8,128)(2,1)S(1)} collective-permute-done((bf16[256,1280]{1,0:T(8,128)(2,1)S(1)}, bf16[256,1280]{1,0:T(8,128)(2,1)S(1)}, u32[]{:S(2)}, u32[]{:S(2)}) %collective-permute-start.5) | collective-permute-done | bytes 655392 | tf_op jit(solution)/shard_map/ppermute | solution.py:237
  74.1 3.6 %collective-permute-start.3 = (bf16[128,1280]{1,0:T(8,128)(2,1)S(1)}, bf16[128,1280]{1,0:T(8,128)(2,1)S(1)}, u32[]{:S(2)}, u32[]{:S(2)}) collective-permute-start(bf16[128,1280]{1,0:T(8,128)(2,1)S(1)} %slice.17), channel_id=1, source_target_pairs={{0,192},{64,0},{128,64},{192,128},{1,193},{65,1},{129,65},{193,129... | collective-permute-start | bytes 983048 | tf_op jit(solution)/shard_map/ppermute | solution.py:237
  77.7 0.0 collective-permute-done.4.refs_6_
  77.7 0.1 collective-permute-start.2
  77.8 0.0 collective-permute-done.8.refs_13_
  77.8 3.3 %collective-permute-start.7 = (bf16[128,1280]{1,0:T(8,128)(2,1)S(1)}, bf16[128,1280]{1,0:T(8,128)(2,1)S(1)}, u32[]{:S(2)}, u32[]{:S(2)}) collective-permute-start(bf16[128,1280]{1,0:T(8,128)(2,1)S(1)} %slice.19), channel_id=1, source_target_pairs={{0,192},{64,0},{128,64},{192,128},{1,193},{65,1},{129,65},{193,129... | collective-permute-start | bytes 983048 | tf_op jit(solution)/shard_map/ppermute | solution.py:237
  81.1 0.0 collective-permute-done.9.refs_14_
  81.1 0.0 collective-permute-start.6
  81.1 0.0 collective-permute-done.10.refs_15_
  81.1 0.0 copy-start.8
  81.1 3.3 %collective-permute-done.3.refs_4_ = bf16[128,1280]{1,0:T(8,128)(2,1)S(1)} collective-permute-done((bf16[128,1280]{1,0:T(8,128)(2,1)S(1)}, bf16[128,1280]{1,0:T(8,128)(2,1)S(1)}, u32[]{:S(2)}, u32[]{:S(2)}) %collective-permute-start.3) | collective-permute-done | bytes 327712 | tf_op jit(solution)/shard_map/ppermute | solution.py:237
  84.4 3.4 %collective-permute-done.2.refs_3_ = bf16[128,1280]{1,0:T(8,128)(2,1)S(1)} collective-permute-done((bf16[128,1280]{1,0:T(8,128)(2,1)S(1)}, bf16[128,1280]{1,0:T(8,128)(2,1)S(1)}, u32[]{:S(2)}, u32[]{:S(2)}) %collective-permute-start.2) | collective-permute-done | bytes 327712 | tf_op jit(solution)/shard_map/ppermute | solution.py:237
  87.9 0.1 collective-permute-done.7.refs_9_
  88.0 3.4 %collective-permute-done.6.refs_8_ = bf16[128,1280]{1,0:T(8,128)(2,1)S(1)} collective-permute-done((bf16[128,1280]{1,0:T(8,128)(2,1)S(1)}, bf16[128,1280]{1,0:T(8,128)(2,1)S(1)}, u32[]{:S(2)}, u32[]{:S(2)}) %collective-permute-start.6) | collective-permute-done | bytes 327712 | tf_op jit(solution)/shard_map/ppermute | solution.py:237
  91.5 0.7 copy-done.15
  92.2 15.0 %shard_map.120 = (bf16[256,1408]{1,0:T(8,128)(2,1)}, bf16[256,1408]{1,0:T(8,128)(2,1)}, bf16[256,1408]{1,0:T(8,128)(2,1)}, bf16[256,1408]{1,0:T(8,128)(2,1)}, bf...) custom-call(bf16[256,1280]{1,0:T(8,128)(2,1)} %bitcast.20, ...), custom_call_target="tpu_custom_call" | custom-call | flops 5033164800 | bytes 31457280 | tf_op jit(solution)/shard_map/pallas_call | solution.py:179
  107.2 1.0 collective-permute-start.11
  108.1 1.1 collective-permute-start.12
  109.3 0.4 collective-permute-start.13
  109.7 16.8 %collective-permute-done.11 = bf16[256,1408]{1,0:T(8,128)(2,1)S(1)} collective-permute-done((bf16[256,1408]{1,0:T(8,128)(2,1)}, bf16[256,1408]{1,0:T(8,128)(2,1)S(1)}, u32[]{:S(2)}, u32[]{:S(2)}) %collective-permute-start.11) | collective-permute-done | bytes 720928 | tf_op jit(solution)/shard_map/ppermute | solution.py:237
  126.5 11.5 %collective-permute-done.12 = bf16[256,1408]{1,0:T(8,128)(2,1)S(1)} collective-permute-done((bf16[256,1408]{1,0:T(8,128)(2,1)}, bf16[256,1408]{1,0:T(8,128)(2,1)S(1)}, u32[]{:S(2)}, u32[]{:S(2)}) %collective-permute-start.12) | collective-permute-done | bytes 720928 | tf_op jit(solution)/shard_map/ppermute | solution.py:237
  138.0 2.4 %fusion = bf16[32,8,1408]{2,1,0:T(8,128)(2,1)} fusion(bf16[256,1408]{1,0:T(8,128)(2,1)S(1)} %collective-permute-done.13, bf16[256,1408]{1,0:T(8,128)(2,1)S(1)} %collective-permute-done.12, bf16[256,1408]{1,0:T(8,128)(2,1)S(1)} %collective-permute-done.11, bf16[256,1408]{1,0:T(8,128)(2,1)} %get-tuple-element.25), kind=kLoop, calls=%fused_computation.1 | loop fusion | flops 2883584 | bytes 3604480 | tf_op jit(solution)/shard_map/reshape | solution.py:261
  140.4 11.6 %all-to-all-start.2 = ((bf16[32,8,1408]{2,1,0:T(8,128)(2,1)}), bf16[32,8,1408]{2,1,0:T(8,128)(2,1)S(1)}, u32[]{:S(2)}, u32[]{:S(2)}) async-start(bf16[32,8,1408]{2,1,0:T(8,128)(2,1)} %fusion), calls=%async_computation.2 | async-start | bytes 1441792 | tf_op jit(solution)/shard_map/all_to_all | solution.py:262
  152.0 7.4 %shard_map.122 = (bf16[192,2048]{1,0:T(8,128)(2,1)}, bf16[192,2048]{1,0:T(8,128)(2,1)}, bf16[192,2048]{1,0:T(8,128)(2,1)}) custom-call(bf16[640,384]{1,0:T(8,128)(2,1)} %get-tuple-element.31.refs_0_, bf16[640,768]{1,0:T(8,128)(2,1)} %get-tuple-element.32.refs_1_, bf16[640,2048]{1,0:T(8,128)(2,1)} %get-tuple-element.33.refs_2_, ...), custom_call_target="tpu_custom_call" | custom-call | flops 3019898880 | bytes 9961472 | tf_op jit(solution)/shard_map/pallas_call | solution.py:223
  159.4 0.0 collective-permute-start.14
  159.4 0.5 collective-permute-start.15
  159.9 0.1 collective-permute-start.16
  160.0 1.9 %collective-permute-done.14.refs_4_ = bf16[192,2048]{1,0:T(8,128)(2,1)S(1)} collective-permute-done((bf16[192,2048]{1,0:T(8,128)(2,1)}, bf16[192,2048]{1,0:T(8,128)(2,1)S(1)}, u32[]{:S(2)}, u32[]{:S(2)}) %collective-permute-start.14) | collective-permute-done | bytes 786464 | tf_op jit(solution)/shard_map/ppermute | solution.py:237
  161.9 1.1 collective-permute-done.15.refs_5_
  163.0 1.1 collective-permute-done.16.refs_6_
  164.1 0.9 copy-done.11
  165.1 7.9 %shard_map.123 = (bf16[192,2048]{1,0:T(8,128)(2,1)}, bf16[192,2048]{1,0:T(8,128)(2,1)}, bf16[192,2048]{1,0:T(8,128)(2,1)}) custom-call(bf16[640,384]{1,0:T(8,128)(2,1)} %get-tuple-element.31.refs_0_, bf16[640,768]{1,0:T(8,128)(2,1)} %get-tuple-element.32.refs_1_, bf16[640,2048]{1,0:T(8,128)(2,1)} %get-tuple-element.33.refs_2_, ...), custom_call_target="tpu_custom_call" | custom-call | flops 3019898880 | bytes 9961472 | tf_op jit(solution)/shard_map/pallas_call | solution.py:223
  173.0 0.0 all-to-all-done.2
  173.0 0.8 copy-done
  173.9 2.6 %shard_map.121 = (bf16[128,2048]{1,0:T(8,128)(2,1)}, f32[1,128]{1,0:T(1,128)}) custom-call(s32[1,128]{1,0:T(1,128)} %bitcast.27, bf16[1,128]{1,0:T(2,128)(2,1)} %bitcast.29, bf16[256,1408]{1,0:T(8,128)(2,1)} %bitcast.17), custom_call_target="tpu_custom_call" | custom-call | tf_op jit(solution)/shard_map/pallas_call | solution.py:279
  (33 shorter events, 0.1 us)
Async XLA Ops:
  4.1 40.1 %copy-start.7 = (bf16[1,192,2048]{2,1,0:T(8,128)(2,1)S(1)}, bf16[1,192,2048]{2,1,0:T(8,128)(2,1)}, u32[]{:S(2)}) copy-start(bf16[1,192,2048]{2,1,0:T(8,128)(2,1)} %param.13) | copy-start | bytes 2359300
  35.5 42.2 %copy-start.1 = (bf16[32,8,1280]{2,1,0:T(8,128)(2,1)}, bf16[32,8,1280]{2,1,0:T(8,128)(2,1)S(1)}, u32[]{:S(2)}) copy-start(bf16[32,8,1280]{2,1,0:T(8,128)(2,1)S(1)} %all_to_all.15) | copy-start | bytes 1966084
  35.5 24.2 %all-to-all-start.1 = ((bf16[32,8,1280]{2,1,0:T(8,128)(2,1)}), bf16[32,8,1280]{2,1,0:T(8,128)(2,1)S(1)}, u32[]{:S(2)}, u32[]{:S(2)}) async-start(bf16[32,8,1280]{2,1,0:T(8,128)(2,1)} %bitcast.24), calls=%async_computation.1 | async-start | bytes 1310720 | tf_op jit(solution)/shard_map/all_to_all | solution.py:262
  41.1 21.7 %collective-permute-start.1 = (bf16[256,1280]{1,0:T(8,128)(2,1)S(1)}, bf16[256,1280]{1,0:T(8,128)(2,1)S(1)}, u32[]{:S(2)}, u32[]{:S(2)}) collective-permute-start(bf16[256,1280]{1,0:T(8,128)(2,1)S(1)} %bitcast.18), channel_id=1, source_target_pairs={{0,192},{64,0},{128,64},{192,128},{1,193},{65,1},{129,65},{193,129... | collective-permute-start | bytes 1966088 | tf_op jit(solution)/shard_map/ppermute | solution.py:237
  44.2 18.6 %collective-permute-start = (bf16[256,1280]{1,0:T(8,128)(2,1)S(1)}, bf16[256,1280]{1,0:T(8,128)(2,1)S(1)}, u32[]{:S(2)}, u32[]{:S(2)}) collective-permute-start(bf16[256,1280]{1,0:T(8,128)(2,1)S(1)} %bitcast.19), channel_id=1, source_target_pairs={{0,64},{64,128},{128,192},{192,0},{1,65},{65,129},{129,193},{193,1... | collective-permute-start | bytes 1966088 | tf_op jit(solution)/shard_map/ppermute | solution.py:237
  44.2 33.7 %collective-permute-start.8 = (bf16[192,2048]{1,0:T(8,128)(2,1)S(1)}, bf16[192,2048]{1,0:T(8,128)(2,1)}, u32[]{:S(2)}, u32[]{:S(2)}) collective-permute-start(bf16[192,2048]{1,0:T(8,128)(2,1)S(1)} %bitcast.32), channel_id=1, source_target_pairs={{0,32},{32,0},{1,33},{33,1},{2,34},{34,2},{3,35},{35,3},{4,36},{36... | collective-permute-start | bytes 2359304 | tf_op jit(solution)/shard_map/ppermute | solution.py:237
  44.2 37.0 %collective-permute-start.9 = (bf16[192,2048]{1,0:T(8,128)(2,1)}, bf16[192,2048]{1,0:T(8,128)(2,1)}, u32[]{:S(2)}, u32[]{:S(2)}) collective-permute-start(bf16[192,2048]{1,0:T(8,128)(2,1)} %bitcast.33), channel_id=1, source_target_pairs={{0,32},{32,0},{1,33},{33,1},{2,34},{34,2},{3,35},{35,3},{4,36},{36... | collective-permute-start | bytes 2359304 | tf_op jit(solution)/shard_map/ppermute | solution.py:237
  59.7 31.7 %copy-start.2 = (bf16[32,8,1280]{2,1,0:T(8,128)(2,1)}, bf16[32,8,1280]{2,1,0:T(8,128)(2,1)S(1)}, u32[]{:S(2)}) copy-start(bf16[32,8,1280]{2,1,0:T(8,128)(2,1)S(1)} %all-to-all-done.1) | copy-start | bytes 1966084
  59.7 14.4 %collective-permute-start.5 = (bf16[256,1280]{1,0:T(8,128)(2,1)S(1)}, bf16[256,1280]{1,0:T(8,128)(2,1)S(1)}, u32[]{:S(2)}, u32[]{:S(2)}) collective-permute-start(bf16[256,1280]{1,0:T(8,128)(2,1)S(1)} %bitcast.21), channel_id=1, source_target_pairs={{0,192},{64,0},{128,64},{192,128},{1,193},{65,1},{129,65},{193,129... | collective-permute-start | bytes 1966088 | tf_op jit(solution)/shard_map/ppermute | solution.py:237
  62.7 28.7 %copy-start.3 = (bf16[256,1280]{1,0:T(8,128)(2,1)}, bf16[256,1280]{1,0:T(8,128)(2,1)S(1)}, u32[]{:S(2)}) copy-start(bf16[256,1280]{1,0:T(8,128)(2,1)S(1)} %collective-permute-done.1.refs_2_) | copy-start | bytes 1966084
  62.7 14.9 %collective-permute-start.4 = (bf16[256,1280]{1,0:T(8,128)(2,1)S(1)}, bf16[256,1280]{1,0:T(8,128)(2,1)S(1)}, u32[]{:S(2)}, u32[]{:S(2)}) collective-permute-start(bf16[256,1280]{1,0:T(8,128)(2,1)S(1)} %bitcast.22), channel_id=1, source_target_pairs={{0,64},{64,128},{128,192},{192,0},{1,65},{65,129},{129,193},{193,1... | collective-permute-start | bytes 1966088 | tf_op jit(solution)/shard_map/ppermute | solution.py:237
  62.8 28.6 %copy-start.4 = (bf16[256,1280]{1,0:T(8,128)(2,1)}, bf16[256,1280]{1,0:T(8,128)(2,1)S(1)}, u32[]{:S(2)}) copy-start(bf16[256,1280]{1,0:T(8,128)(2,1)S(1)} %collective-permute-done.refs_1_) | copy-start | bytes 1966084
  62.8 18.4 %collective-permute-start.10 = (bf16[192,2048]{1,0:T(8,128)(2,1)}, bf16[192,2048]{1,0:T(8,128)(2,1)S(1)}, u32[]{:S(2)}, u32[]{:S(2)}) collective-permute-start(bf16[192,2048]{1,0:T(8,128)(2,1)} %bitcast.35), channel_id=1, source_target_pairs={{0,32},{32,0},{1,33},{33,1},{2,34},{34,2},{3,35},{35,3},{4,36},{36... | collective-permute-start | bytes 2359304 | tf_op jit(solution)/shard_map/ppermute | solution.py:237
  74.1 17.3 %copy-start.5 = (bf16[256,1280]{1,0:T(8,128)(2,1)}, bf16[256,1280]{1,0:T(8,128)(2,1)S(1)}, u32[]{:S(2)}) copy-start(bf16[256,1280]{1,0:T(8,128)(2,1)S(1)} %collective-permute-done.5.refs_7_) | copy-start | bytes 1966084
  74.1 10.4 %collective-permute-start.3 = (bf16[128,1280]{1,0:T(8,128)(2,1)S(1)}, bf16[128,1280]{1,0:T(8,128)(2,1)S(1)}, u32[]{:S(2)}, u32[]{:S(2)}) collective-permute-start(bf16[128,1280]{1,0:T(8,128)(2,1)S(1)} %slice.17), channel_id=1, source_target_pairs={{0,192},{64,0},{128,64},{192,128},{1,193},{65,1},{129,65},{193,129... | collective-permute-start | bytes 983048 | tf_op jit(solution)/shard_map/ppermute | solution.py:237
  77.7 13.7 %copy-start.6 = (bf16[256,1280]{1,0:T(8,128)(2,1)}, bf16[256,1280]{1,0:T(8,128)(2,1)S(1)}, u32[]{:S(2)}) copy-start(bf16[256,1280]{1,0:T(8,128)(2,1)S(1)} %collective-permute-done.4.refs_6_) | copy-start | bytes 1966084
  77.7 10.2 %collective-permute-start.2 = (bf16[128,1280]{1,0:T(8,128)(2,1)S(1)}, bf16[128,1280]{1,0:T(8,128)(2,1)S(1)}, u32[]{:S(2)}, u32[]{:S(2)}) collective-permute-start(bf16[128,1280]{1,0:T(8,128)(2,1)S(1)} %slice.16), channel_id=1, source_target_pairs={{0,64},{64,128},{128,192},{192,0},{1,65},{65,129},{129,193},{193,1... | collective-permute-start | bytes 983048 | tf_op jit(solution)/shard_map/ppermute | solution.py:237
  77.8 10.1 %collective-permute-start.7 = (bf16[128,1280]{1,0:T(8,128)(2,1)S(1)}, bf16[128,1280]{1,0:T(8,128)(2,1)S(1)}, u32[]{:S(2)}, u32[]{:S(2)}) collective-permute-start(bf16[128,1280]{1,0:T(8,128)(2,1)S(1)} %slice.19), channel_id=1, source_target_pairs={{0,192},{64,0},{128,64},{192,128},{1,193},{65,1},{129,65},{193,129... | collective-permute-start | bytes 983048 | tf_op jit(solution)/shard_map/ppermute | solution.py:237
  81.1 10.3 %collective-permute-start.6 = (bf16[128,1280]{1,0:T(8,128)(2,1)S(1)}, bf16[128,1280]{1,0:T(8,128)(2,1)S(1)}, u32[]{:S(2)}, u32[]{:S(2)}) collective-permute-start(bf16[128,1280]{1,0:T(8,128)(2,1)S(1)} %slice.18), channel_id=1, source_target_pairs={{0,64},{64,128},{128,192},{192,0},{1,65},{65,129},{129,193},{193,1... | collective-permute-start | bytes 983048 | tf_op jit(solution)/shard_map/ppermute | solution.py:237
  81.1 10.3 %copy-start.8 = (bf16[192,2048]{1,0:T(8,128)(2,1)}, bf16[192,2048]{1,0:T(8,128)(2,1)S(1)}, u32[]{:S(2)}) copy-start(bf16[192,2048]{1,0:T(8,128)(2,1)S(1)} %collective-permute-done.10.refs_15_) | copy-start | bytes 2359300
  84.4 7.0 %copy-start.12 = (bf16[128,1280]{1,0:T(8,128)(2,1)}, bf16[128,1280]{1,0:T(8,128)(2,1)S(1)}, u32[]{:S(2)}) copy-start(bf16[128,1280]{1,0:T(8,128)(2,1)S(1)} %collective-permute-done.3.refs_4_) | copy-start | bytes 983044
  87.9 3.6 %copy-start.13 = (bf16[128,1280]{1,0:T(8,128)(2,1)}, bf16[128,1280]{1,0:T(8,128)(2,1)S(1)}, u32[]{:S(2)}) copy-start(bf16[128,1280]{1,0:T(8,128)(2,1)S(1)} %collective-permute-done.2.refs_3_) | copy-start | bytes 983044
  88.0 3.5 %copy-start.14 = (bf16[128,1280]{1,0:T(8,128)(2,1)}, bf16[128,1280]{1,0:T(8,128)(2,1)S(1)}, u32[]{:S(2)}) copy-start(bf16[128,1280]{1,0:T(8,128)(2,1)S(1)} %collective-permute-done.7.refs_9_) | copy-start | bytes 983044
  91.5 0.7 copy-start.15
  107.2 19.4 %collective-permute-start.11 = (bf16[256,1408]{1,0:T(8,128)(2,1)}, bf16[256,1408]{1,0:T(8,128)(2,1)S(1)}, u32[]{:S(2)}, u32[]{:S(2)}) collective-permute-start(bf16[256,1408]{1,0:T(8,128)(2,1)} %get-tuple-element.26), channel_id=1, source_target_pairs={{0,192},{64,0},{128,64},{192,128},{1,193},{65,1},{129,65},{193,129... | collective-permute-start | bytes 2162696 | tf_op jit(solution)/shard_map/ppermute | solution.py:237
  108.1 29.9 %collective-permute-start.12 = (bf16[256,1408]{1,0:T(8,128)(2,1)}, bf16[256,1408]{1,0:T(8,128)(2,1)S(1)}, u32[]{:S(2)}, u32[]{:S(2)}) collective-permute-start(bf16[256,1408]{1,0:T(8,128)(2,1)} %get-tuple-element.27), channel_id=1, source_target_pairs={{0,64},{64,128},{128,192},{192,0},{1,65},{65,129},{129,193},{193,1... | collective-permute-start | bytes 2162696 | tf_op jit(solution)/shard_map/ppermute | solution.py:237
  109.3 28.8 %collective-permute-start.13 = (bf16[256,1408]{1,0:T(8,128)(2,1)}, bf16[256,1408]{1,0:T(8,128)(2,1)S(1)}, u32[]{:S(2)}, u32[]{:S(2)}) collective-permute-start(bf16[256,1408]{1,0:T(8,128)(2,1)} %get-tuple-element.28), channel_id=1, source_target_pairs={{0,128},{64,192},{128,0},{192,64},{1,129},{65,193},{129,1},{193,65... | collective-permute-start | bytes 2162696 | tf_op jit(solution)/shard_map/ppermute | solution.py:237
  140.4 32.6 %all-to-all-start.2 = ((bf16[32,8,1408]{2,1,0:T(8,128)(2,1)}), bf16[32,8,1408]{2,1,0:T(8,128)(2,1)S(1)}, u32[]{:S(2)}, u32[]{:S(2)}) async-start(bf16[32,8,1408]{2,1,0:T(8,128)(2,1)} %fusion), calls=%async_computation.2 | async-start | bytes 1441792 | tf_op jit(solution)/shard_map/all_to_all | solution.py:262
  159.4 2.5 %collective-permute-start.14 = (bf16[192,2048]{1,0:T(8,128)(2,1)}, bf16[192,2048]{1,0:T(8,128)(2,1)S(1)}, u32[]{:S(2)}, u32[]{:S(2)}) collective-permute-start(bf16[192,2048]{1,0:T(8,128)(2,1)} %get-tuple-element.35), channel_id=1, source_target_pairs={{0,32},{32,0},{1,33},{33,1},{2,34},{34,2},{3,35},{35,3},{4,36},{36... | collective-permute-start | bytes 2359304 | tf_op jit(solution)/shard_map/ppermute | solution.py:237
  159.4 3.6 %collective-permute-start.15 = (bf16[192,2048]{1,0:T(8,128)(2,1)}, bf16[192,2048]{1,0:T(8,128)(2,1)S(1)}, u32[]{:S(2)}, u32[]{:S(2)}) collective-permute-start(bf16[192,2048]{1,0:T(8,128)(2,1)} %get-tuple-element.36), channel_id=1, source_target_pairs={{0,32},{32,0},{1,33},{33,1},{2,34},{34,2},{3,35},{35,3},{4,36},{36... | collective-permute-start | bytes 2359304 | tf_op jit(solution)/shard_map/ppermute | solution.py:237
  159.9 4.2 %collective-permute-start.16 = (bf16[192,2048]{1,0:T(8,128)(2,1)}, bf16[192,2048]{1,0:T(8,128)(2,1)S(1)}, u32[]{:S(2)}, u32[]{:S(2)}) collective-permute-start(bf16[192,2048]{1,0:T(8,128)(2,1)} %get-tuple-element.37), channel_id=1, source_target_pairs={{0,32},{32,0},{1,33},{33,1},{2,34},{34,2},{3,35},{35,3},{4,36},{36... | collective-permute-start | bytes 2359304 | tf_op jit(solution)/shard_map/ppermute | solution.py:237
  161.9 2.3 %copy-start.9 = (bf16[192,2048]{1,0:T(8,128)(2,1)}, bf16[192,2048]{1,0:T(8,128)(2,1)S(1)}, u32[]{:S(2)}) copy-start(bf16[192,2048]{1,0:T(8,128)(2,1)S(1)} %collective-permute-done.14.refs_4_) | copy-start | bytes 2359300
  163.0 1.1 copy-start.10
  164.1 0.9 copy-start.11
  173.0 0.9 copy-start

commit v2 on v1

v2 whole, which is shorter than its diff:
```python
import functools
import math

import jax
import jax.numpy as jnp
from jax import lax
from jax.experimental import pallas as pl
from jax.experimental.pallas import tpu as pltpu
from jax.sharding import Mesh, PartitionSpec as P

SLOTS = 5
BF = jnp.bfloat16
F32 = jnp.float32
ACROSS = ((0,), (0,))
LANES = ((1,), (1,))


def dot(a, b, dims=((1,), (0,))):
    return lax.dot_general(a, b, (dims, ((), ())), preferred_element_type=F32)


def iota(shape, axis):
    return lax.broadcasted_iota(jnp.int32, shape, axis)


def params(size=24):
    return pltpu.CompilerParams(vmem_limit_bytes=size * 1024 * 1024)


def vmem(count):
    return [pl.BlockSpec(memory_space=pltpu.VMEM)] * count


def places(routes_row, experts):
    tokens = routes_row.shape[1]
    picked = iota((experts, tokens), 0) == routes_row
    hot = jnp.where(picked, 1.0, 0.0).astype(BF)
    earlier = jnp.where(iota((tokens, tokens), 0) < iota((tokens, tokens), 1), 1.0, 0.0).astype(BF)
    before = dot(hot, earlier)
    rank = jnp.sum(jnp.where(picked, before, 0.0), axis=0, keepdims=True).astype(jnp.int32)
    return routes_row, rank


def main_rows(expert, rank, half):
    return jnp.where(rank < SLOTS - 1, expert * 8 + half * 4 + rank, -1)


def last_rows(expert, rank, piece):
    return jnp.where(rank == SLOTS - 1, expert * 8 + piece, -1)


def one_hot(rows, target):
    return iota((rows, target.shape[1]), 0) == target


def pack_tokens(scaled, *refs):
    if scaled:
        routes_ref, gates_ref, mask_ref, src, dst = refs
        value = jnp.where(mask_ref[...] == 1, gates_ref[...].astype(F32), 0.0)
    else:
        routes_ref, src, dst = refs
        value = 1.0
    width = src.shape[1]
    rows = dst.shape[0]
    half, piece = width // 2, width // 8
    expert, rank = places(routes_ref[...], rows // 8)

    def spread(target):
        return jnp.where(one_hot(rows, target), value, 0.0).astype(BF)

    main = dot(spread(main_rows(expert, rank, 0)), src[:, :half])
    main += dot(spread(main_rows(expert, rank, 1)), src[:, half:])
    dst[:, :half] = main.astype(BF)
    last = jnp.zeros((rows, piece), F32)
    for k in range(8):
        last += dot(spread(last_rows(expert, rank, k)), src[:, k * piece : (k + 1) * piece])
    dst[:, half:] = last.astype(BF)


def unpack_tokens(routes_ref, gates_ref, r_ref, out_ref, gate_ref):
    width = out_ref.shape[1]
    rows = r_ref.shape[0]
    half, piece = width // 2, width // 8
    expert, rank = places(routes_ref[...], rows // 8)

    def spread(target):
        return jnp.where(one_hot(rows, target), 1.0, 0.0).astype(BF)

    mains = [dot(spread(main_rows(expert, rank, h)), r_ref[:, :half], ACROSS) for h in (0, 1)]
    for k in range(8):
        last = dot(spread(last_rows(expert, rank, k)), r_ref[:, half : half + piece], ACROSS)
        at = (k % 4) * piece
        out_ref[:, k * piece : (k + 1) * piece] = (mains[k // 4][:, at : at + piece] + last).astype(BF)
    lanes = r_ref[:, half + piece :]
    summed = dot(lanes, spread(expert * 8 + rank), ACROSS)
    gate_ref[...] = summed[0:1, :] / gates_ref[...].astype(F32)


def main_order(rows):
    at = iota((rows, rows), 1)
    inner = at % (rows // 2)
    return iota((rows, rows), 0) == (inner // 4) * 8 + (at // (rows // 2)) * 4 + inner % 4


def last_order(rows):
    at = iota((rows, rows), 1)
    return iota((rows, rows), 0) == (at % (rows // 8)) * 8 + at // (rows // 8)


def orders(rows):
    order = jnp.where(main_order(rows), 1.0, 0.0).astype(BF)
    return order, jnp.where(last_order(rows), 1.0, 0.0).astype(BF)


def open_chunks(packed, dst, at, order, order_last):
    rows = packed.shape[0]
    width = dst.shape[1]
    half, piece = width // 2, width // 8
    four, lone = rows // 2, rows // 8
    main = dot(order, packed[:, :half], ACROSS).astype(BF)
    last = dot(order_last, packed[:, half:], ACROSS).astype(BF)
    dst[at : at + four, :half] = main[:four]
    dst[at : at + four, half:] = main[four:]
    for k in range(8):
        dst[at + four : at + four + lone, k * piece : (k + 1) * piece] = last[k * lone : (k + 1) * lone]


def close_chunks(part, column, out, order, order_last):
    rows = out.shape[0]
    width = part.shape[1]
    half, piece = width // 2, width // 8
    four, lone = rows // 2, rows // 8
    stacked = jnp.concatenate([part[:four, :half], part[:four, half:]], axis=0)
    out[:, :half] = dot(order, stacked).astype(BF)
    stacked = jnp.concatenate([part[four:, k * piece : (k + 1) * piece] for k in range(8)], axis=0)
    out[:, half : half + piece] = dot(order_last, stacked).astype(BF)
    column = jnp.broadcast_to(column.astype(BF), (four + lone, 128))
    main = dot(order[:, :four], column[:four])
    pick = iota((rows, lone), 0) == iota((rows, lone), 1) * 8 + 4
    main += dot(jnp.where(pick, 1.0, 0.0).astype(BF), column[four:])
    out[:, half + piece :] = main.astype(BF)


def x_part(*refs):
    xs, wgu = refs[:4], refs[4]
    x_ref, hid_ref, slope_ref, silu_ref, pre = refs[5:]
    order, order_last = orders(xs[0].shape[0])
    total, both = hid_ref.shape
    block = total // 4
    for b in range(4):
        open_chunks(xs[b][...], x_ref, b * block, order, order_last)
    pre[...] = dot(x_ref[...], wgu[...], LANES)
    step = math.gcd(block, 32)
    for r in range(0, total, step):
        at = slice(r, r + step)
        gate, up = pre[at, :both], pre[at, both:]
        sig = jax.nn.sigmoid(gate)
        silu = gate * sig
        hid_ref[at, :] = (silu * up).astype(BF)
        slope_ref[at, :] = up * sig * (1.0 + gate * (1.0 - sig))
        silu_ref[at, :] = silu


def call_x_part(xs, wgu):
    rows, packed = xs[0].shape
    pairs, width = wgu.shape
    total = 4 * (rows // 2 + rows // 8)
    half_units = jax.ShapeDtypeStruct((total, pairs // 2), F32)
    return pl.pallas_call(
        x_part,
        out_shape=[
            jax.ShapeDtypeStruct((total, width), BF),
            jax.ShapeDtypeStruct((total, pairs // 2), BF),
            half_units,
            half_units,
        ],
        in_specs=vmem(5),
        out_specs=vmem(4),
        scratch_shapes=[pltpu.VMEM((total, pairs), F32)],
        compiler_params=params(),
        cost_estimate=pl.CostEstimate(
            flops=3 * total * pairs * width, bytes_accessed=4 * total * width, transcendentals=total * pairs // 2
        ),
    )(*xs, wgu)


def dy_part(first, blocks, ins, *refs):
    dys, (hid, slope, silu, wgu, wd) = refs[:ins], refs[ins : ins + 5]
    outs = refs[ins + 5 : ins + 5 + blocks]
    dy_ref, d_ref, back = refs[ins + 5 + blocks :]
    total = dy_ref.shape[0]
    both = wd.shape[0]
    block = total // blocks
    begin = first * block
    order, order_last = orders(outs[0].shape[0])
    for b in range(blocks):
        if ins > blocks:
            packed = jnp.concatenate([ref[...] for ref in dys], axis=0)
        else:
            packed = dys[b][...]
        open_chunks(packed, dy_ref, b * block, order, order_last)
    back[...] = dot(dy_ref[...], wd[...], LANES)
    step = math.gcd(block, 32)
    columns = []
    for r in range(0, total, step):
        at = slice(r, r + step)
        there = slice(begin + r, begin + r + step)
        bp = back[at, :]
        d_ref[at, :both] = (bp * slope[there, :]).astype(BF)
        d_ref[at, both:] = (bp * silu[there, :]).astype(BF)
        columns.append(jnp.sum(hid[there, :].astype(F32) * bp, axis=1, keepdims=True))
    for b in range(blocks):
        at = b * block
        part = dot(d_ref[at : at + block, :], wgu[...]).astype(BF)
        column = jnp.concatenate(columns[at // step : (at + block) // step], axis=0)
        close_chunks(part, column, outs[b], order, order_last)


def call_dy_part(first, blocks, dys, hid, slope, silu, wgu, wd):
    packed = dys[0].shape[1]
    both, width = wd.shape
    total = hid.shape[0] // 4 * blocks
    rows = hid.shape[0] // 4 * 8 // 5
    return pl.pallas_call(
        functools.partial(dy_part, first, blocks, len(dys)),
        out_shape=[jax.ShapeDtypeStruct((rows, packed + 128), BF)] * blocks
        + [jax.ShapeDtypeStruct((total, width), BF), jax.ShapeDtypeStruct((total, 2 * both), BF)],
        in_specs=vmem(len(dys) + 5),
        out_specs=vmem(blocks + 2),
        scratch_shapes=[pltpu.VMEM((total, both), F32)],
        compiler_params=params(),
        cost_estimate=pl.CostEstimate(
            flops=9 * total * both * width, bytes_accessed=6 * total * width, transcendentals=0
        ),
    )(*dys, hid, slope, silu, wgu, wd)


def grad_block(own, has_more, units, hid, d1, d2, x, dy1, dy2, *refs):
    out = refs[-1]
    cut = d1.shape[0]
    both = 2 * units
    first = 0 if own else units
    down = dot(hid[:cut], dy1[...], ACROSS) + dot(hid[cut:], dy2[...], ACROSS)
    pair = dot(d1[...], x[:cut], ACROSS) + dot(d2[...], x[cut:], ACROSS)
    values = (pair[first : first + units], pair[both + first : both + first + units], down[first : first + units])
    for i, value in enumerate(values):
        if has_more:
            refs[1 + i][...] = (value + refs[0][i * units : (i + 1) * units].astype(F32)).astype(BF)
        else:
            out[i * units : (i + 1) * units] = value.astype(BF)


def call_grads(own, hid, d1, d2, x, dy1, dy2, more):
    total, width = x.shape
    units = hid.shape[1] // 2
    cols = 512
    full = lambda a: pl.BlockSpec(a.shape, lambda j: (0, 0))
    piece = lambda rows: pl.BlockSpec((rows, cols), lambda j: (0, j))
    if more:
        out_shape, out_specs = [jax.ShapeDtypeStruct((units, width), BF)] * 3, [piece(units)] * 3
    else:
        out_shape, out_specs = [jax.ShapeDtypeStruct((3 * units, width), BF)], [piece(3 * units)]
    return pl.pallas_call(
        functools.partial(grad_block, own, bool(more), units),
        grid=(width // cols,),
        out_shape=out_shape,
        in_specs=[full(hid), full(d1), full(d2), piece(total), piece(dy1.shape[0]), piece(dy2.shape[0])]
        + [piece(3 * units)] * len(more),
        out_specs=out_specs,
        compiler_params=params(),
        cost_estimate=pl.CostEstimate(
            flops=12 * total * units * width, bytes_accessed=4 * total * width + 12 * units * width, transcendentals=0
        ),
    )(hid, d1, d2, x, dy1, dy2, *more)


def along(v, axis, size, by):
    return lax.ppermute(v, axis, [(i, (i + by) % size) for i in range(size)])


def shards(tokens, cotangent, routes, gates, loss_mask, w_gate, w_up, w_down):
    experts = lax.axis_size("z") * lax.axis_size("x")
    ring = lax.axis_size("y")
    count, width = tokens.shape
    packed = width // 2 + width // 8
    rows = experts * 8
    units = w_gate.shape[1]
    flip = lambda v: along(v, "core", 2, 1)
    mine = [w_gate[0], w_up[0], w_down[0]]
    swapped = flip(jnp.concatenate(mine, axis=0))
    theirs = [swapped[i * units : (i + 1) * units] for i in range(3)]
    wgu = jnp.concatenate([mine[0], theirs[0], mine[1], theirs[1]], axis=0)
    wd = jnp.concatenate([mine[2], theirs[2]], axis=0)
    routes_row = routes.reshape(1, count)
    gates_row = gates.reshape(1, count)
    mask_row = loss_mask.reshape(1, count)

    def pack(*operands):
        return pl.pallas_call(
            functools.partial(pack_tokens, len(operands) > 2),
            out_shape=jax.ShapeDtypeStruct((rows, packed), BF),
            in_specs=vmem(len(operands)),
            out_specs=vmem(1)[0],
            compiler_params=params(56),
        )(*operands)

    def dispatch(v):
        chunks = v.reshape(experts, 8, v.shape[1])
        return lax.all_to_all(chunks, ("z", "x"), 0, 0, tiled=True).reshape(v.shape)

    step = lambda v, by: along(v, "y", ring, by)
    x_own = dispatch(pack(routes_row, tokens))
    packed_dy = pack(routes_row, gates_row, mask_row, cotangent)
    x_own, packed_dy = lax.optimization_barrier((x_own, packed_dy))
    dy_own = dispatch(packed_dy)
    cut = rows // 2
    x_low, x_high = step(x_own, 1), step(x_own, -1)
    far = [step(x_low[:cut], 1), step(x_high[cut:], -1)]
    xs = [x_own, x_low, x_high, jnp.concatenate(far, axis=0)]
    x_all, hid, slope, silu = call_x_part(xs, wgu)
    low, high = step(dy_own, 1), step(dy_own, -1)
    far = [step(low[:cut], 1), step(high[cut:], -1)]
    p_own, p_low, p_high, dy1, d1 = call_dy_part(0, 3, [dy_own, low, high], hid, slope, silu, wgu, wd)
    p_far, dy2, d2 = call_dy_part(3, 1, far, hid, slope, silu, wgu, wd)
    arrived = [step(p_low, -1), step(p_high, 1), step(p_far, 2)]
    (given,) = call_grads(False, hid, d1, d2, x_all, dy1, dy2, [])
    *arrived, given = lax.optimization_barrier((*arrived, given))
    taken = flip(given)
    home = p_own.astype(F32)
    for part in arrived:
        home = home + part.astype(F32)
    returned = dispatch(home.astype(BF))
    grads = call_grads(True, hid, d1, d2, x_all, dy1, dy2, [taken])
    returned, *grads = lax.optimization_barrier((returned, *grads))
    grad_tokens, grad_gates = pl.pallas_call(
        unpack_tokens,
        out_shape=[jax.ShapeDtypeStruct((count, width), BF), jax.ShapeDtypeStruct((1, count), F32)],
        in_specs=vmem(3),
        out_specs=vmem(2),
        compiler_params=params(),
    )(routes_row, gates_row, returned)
    return (grad_tokens, grad_gates.reshape(count, 1), *[g[None] for g in grads])


def solution(mesh):
    devices = mesh.devices
    fine = Mesh(devices.reshape(devices.shape[0] // 2, 2, -1, 4), ("y", "core", "z", "x"))
    row = P(("y", "core", "z", "x"))
    weight = P(("z", "x"), ("y", "core"))
    return jax.shard_map(
        shards,
        mesh=fine,
        in_specs=(row,) * 5 + (weight,) * 3,
        out_specs=(row,) * 2 + (weight,) * 3,
        check_vma=False,
    )
```

time: 178 us -> 157 us (0.88)
  blocking collectives: 31.4 us -> 0 us
  starting transfers between devices: 34 us -> 44.9 us
  Pallas kernels: 36.3 us -> 28.5 us
  waiting for transfers between devices: 68.9 us -> 73 us
  local copies, waits for them, and re-layouts: 2.62 us -> 5.88 us
    all_to_all x1 -> x0, blocking collectives: 31.4 us -> none  [dispatch(): return lax.all_to_all(chunks, ('z', 'x'), 0, 0, tiled=True).reshape(v.shape)]
    all_to_all x2 -> x3, waiting for transfers between devices: 15 us -> 27.1 us  [dispatch(): return lax.all_to_all(chunks, ('z', 'x'), 0, 0, tiled=True).reshape(v.shape)]
    all_to_all x2 -> x3, starting transfers between devices: 17.1 us -> 27 us  [dispatch(): return lax.all_to_all(chunks, ('z', 'x'), 0, 0, tiled=True).reshape(v.shape)]
    ppermute x17 -> x13, waiting for transfers between devices: 53.9 us -> 45.9 us  [along(): return lax.ppermute(v, axis, [(i, (i + by) % size) for i in range(size)])]
    pallas_call x2 -> x5, Pallas kernels: 18.4 us -> 14.6 us  [the longest x2 6 us: call_dy_part(): pl.pallas_call(functools.partial(dy_part, first, blocks, len(dys)), out_s...]
    pallas_call x2, Pallas kernels: 15.3 us -> 12.4 us  [call_grads(): pl.pallas_call(functools.partial(grad_block, own, bool(more), units), gri...]
    concatenate x0 -> x4, other arithmetic: none -> 2.21 us  [the longest x1 1.58 us: shards(): swapped = flip(jnp.concatenate(mine, axis=0))]
    slice x4 -> x5, local copies, waits for them, and re-layouts: 0.09 us -> 1.89 us  [the longest x1 1.8 us: shards(): theirs = [swapped[i * units:(i + 1) * units] for i in range(3)]]
  transfers between devices with their start and end apart: 19 -> 16, of which waited for: 11 -> 10; matrix products, arithmetic and copies ran while one was open for 0% -> 3% of each run, Pallas kernels for 9% -> 15%
where the time goes in v2:
time: 157 us
  waiting for transfers between devices  73 us (46%)
  starting transfers between devices  44.9 us (29%)
  Pallas kernels  28.5 us (18%)
  local copies, waits for them, and re-layouts  5.88 us (4%)
  other arithmetic  3.42 us (2%)
    ppermute x13, waiting for transfers between devices, along(): return lax.ppermute(v, axis, [(i, (i + by) % size) for i in range(size)])  45.9 us
    all_to_all x3, waiting for transfers between devices, dispatch(): return lax.all_to_all(chunks, ('z', 'x'), 0, 0, tiled=True).reshape(v.shape)  27.1 us
    all_to_all x3, starting transfers between devices, dispatch(): return lax.all_to_all(chunks, ('z', 'x'), 0, 0, tiled=True).reshape(v.shape)  27 us
    ppermute x13, starting transfers between devices, along(): return lax.ppermute(v, axis, [(i, (i + by) % size) for i in range(size)])  17.9 us
    pallas_call x2, Pallas kernels, call_grads(): pl.pallas_call(functools.partial(grad_block, own, bool(more), units), gri...  12.4 us
    pallas_call x2, Pallas kernels, call_dy_part(): pl.pallas_call(functools.partial(dy_part, first, blocks, len(dys)), out_s...  6 us
    pallas_call x2, Pallas kernels, pack(): pl.pallas_call(functools.partial(pack_tokens, len(operands) > 2), out_sha...  5.64 us
    unnamed x28, local copies, waits for them, and re-layouts  3.99 us
  transfers between devices with their start and end apart: 16, of which 10 were waited for; matrix products, arithmetic and copies ran while one was open for 3% of the time, Pallas kernels for 15%

profile of v2, /device:TPU:2, one launch (start us, length us, event | category | flops | bytes accessed | tf_op | source)
XLA Modules:
  0.0 156.5 jit_solution(1779673979029683887)
XLA Ops:
  0.6 0.0 copy-start.12
  0.6 0.0 copy-start.8
  0.7 0.0 copy-start.10
  0.7 2.9 %shard_map.119 = bf16[256,1280]{1,0:T(8,128)(2,1)} custom-call(s32[1,128]{1,0:T(1,128)} %bitcast.24, bf16[128,2048]{1,0:T(8,128)(2,1)} %refs_1_.1), custom_call_target="tpu_custom_call" | custom-call | tf_op jit(solution)/shard_map/pallas_call | solution.py:299
  3.5 11.6 %all-to-all-start = ((bf16[32,8,1280]{2,1,0:T(8,128)(2,1)}), bf16[32,8,1280]{2,1,0:T(8,128)(2,1)S(1)}, u32[]{:S(2)}, u32[]{:S(2)}) async-start(bf16[32,8,1280]{2,1,0:T(8,128)(2,1)} %bitcast.36), calls=%async_computation | async-start | bytes 1310720 | tf_op jit(solution)/shard_map/all_to_all | solution.py:309
  15.2 1.6 %pad_maximum_fusion.1 = bf16[576,2048]{1,0:T(8,128)(2,1)} fusion(bf16[192,2048]{1,0:T(8,128)(2,1)S(1)} %bitcast.33, bf16[192,2048]{1,0:T(8,128)(2,1)S(1)} %bitcast.29, bf16[192,2048]{1,0:T(8,128)(2,1)S(1)} %bitcast.31), kind=kLoop, calls=%fused_computation.1 | loop fusion | flops 7077888 | bytes 4718592 | tf_op jit(solution)/shard_map/concatenate | solution.py:290
  16.8 0.0 collective-permute-start.6
  16.8 2.8 %shard_map.120 = bf16[256,1280]{1,0:T(8,128)(2,1)} custom-call(s32[1,128]{1,0:T(1,128)} %bitcast.25, bf16[1,128]{1,0:T(2,128)(2,1)} %bitcast.27, s32[1,128]{1,0:T(1,128)} %bitcast.37, bf16[128,2048]{1,0:T(8,128)(2,1)} %refs_3_.1), custom_call_target="tpu_custom_call" | custom-call | tf_op jit(solution)/shard_map/pallas_call | solution.py:299
  19.5 15.3 %all-to-all-done = bf16[32,8,1280]{2,1,0:T(8,128)(2,1)S(1)} async-done(((bf16[32,8,1280]{2,1,0:T(8,128)(2,1)}), bf16[32,8,1280]{2,1,0:T(8,128)(2,1)S(1)}, u32[]{:S(2)}, u32[]{:S(2)}) %all-to-all-start) | async-done | bytes 655392 | tf_op jit(solution)/shard_map/all_to_all | solution.py:309
  34.8 5.6 %all-to-all-start.1 = ((bf16[32,8,1280]{2,1,0:T(8,128)(2,1)}), bf16[32,8,1280]{2,1,0:T(8,128)(2,1)S(1)}, u32[]{:S(2)}, u32[]{:S(2)}) async-start(bf16[32,8,1280]{2,1,0:T(8,128)(2,1)} %bitcast.35), calls=%async_computation.1 | async-start | bytes 1310720 | tf_op jit(solution)/shard_map/all_to_all | solution.py:309
  40.4 3.1 %collective-permute-start.3 = (bf16[256,1280]{1,0:T(8,128)(2,1)S(1)}, bf16[256,1280]{1,0:T(8,128)(2,1)S(1)}, u32[]{:S(2)}, u32[]{:S(2)}) collective-permute-start(bf16[256,1280]{1,0:T(8,128)(2,1)S(1)} %bitcast.21), channel_id=1, source_target_pairs={{0,192},{64,0},{128,64},{192,128},{1,193},{65,1},{129,65},{193,129... | collective-permute-start | bytes 1966088 | tf_op jit(solution)/shard_map/ppermute | solution.py:278
  43.5 12.4 %collective-permute-done.3.refs_2_ = bf16[256,1280]{1,0:T(8,128)(2,1)S(1)} collective-permute-done((bf16[256,1280]{1,0:T(8,128)(2,1)S(1)}, bf16[256,1280]{1,0:T(8,128)(2,1)S(1)}, u32[]{:S(2)}, u32[]{:S(2)}) %collective-permute-start.3) | collective-permute-done | bytes 655392 | tf_op jit(solution)/shard_map/ppermute | solution.py:278
  55.9 3.8 %collective-permute-start.5 = (bf16[128,1280]{1,0:T(8,128)(2,1)S(1)}, bf16[128,1280]{1,0:T(8,128)(2,1)S(1)}, u32[]{:S(2)}, u32[]{:S(2)}) collective-permute-start(bf16[128,1280]{1,0:T(8,128)(2,1)S(1)} %slice.29), channel_id=1, source_target_pairs={{0,192},{64,0},{128,64},{192,128},{1,193},{65,1},{129,65},{193,129... | collective-permute-start | bytes 983048 | tf_op jit(solution)/shard_map/ppermute | solution.py:278
  59.7 0.1 collective-permute-start.4
  59.8 4.5 %collective-permute-done.5 = bf16[128,1280]{1,0:T(8,128)(2,1)S(1)} collective-permute-done((bf16[128,1280]{1,0:T(8,128)(2,1)S(1)}, bf16[128,1280]{1,0:T(8,128)(2,1)S(1)}, u32[]{:S(2)}, u32[]{:S(2)}) %collective-permute-start.5) | collective-permute-done | bytes 327712 | tf_op jit(solution)/shard_map/ppermute | solution.py:278
  64.3 3.8 %collective-permute-done.4 = bf16[128,1280]{1,0:T(8,128)(2,1)S(1)} collective-permute-done((bf16[128,1280]{1,0:T(8,128)(2,1)S(1)}, bf16[128,1280]{1,0:T(8,128)(2,1)S(1)}, u32[]{:S(2)}, u32[]{:S(2)}) %collective-permute-start.4) | collective-permute-done | bytes 327712 | tf_op jit(solution)/shard_map/ppermute | solution.py:278
  68.2 0.0 copy-start.9
  68.2 0.0 copy-start.11
  68.2 0.1 collective-permute-start
  68.3 3.2 %collective-permute-start.1 = (bf16[256,1280]{1,0:T(8,128)(2,1)S(1)}, bf16[256,1280]{1,0:T(8,128)(2,1)S(1)}, u32[]{:S(2)}, u32[]{:S(2)}) collective-permute-start(bf16[256,1280]{1,0:T(8,128)(2,1)S(1)} %bitcast.19), channel_id=1, source_target_pairs={{0,192},{64,0},{128,64},{192,128},{1,193},{65,1},{129,65},{193,129... | collective-permute-start | bytes 1966088 | tf_op jit(solution)/shard_map/ppermute | solution.py:278
  71.5 1.8 %fusion.1 = (bf16[192,2048]{1,0:T(8,128)(2,1)S(1)}, bf16[192,2048]{1,0:T(8,128)(2,1)S(1)}, bf16[192,2048]{1,0:T(8,128)(2,1)S(1)}) fusion(bf16[576,2048]{1,0:T(8,128)(2,1)} %collective-permute-done.6), kind=kLoop, calls=%fused_computation.6 | loop fusion | bytes 4718592 | tf_op jit(solution)/shard_map/slice | solution.py:291
  73.4 0.0 copy-start.1
  73.4 0.4 pad_maximum_fusion.refs_4_.refs_6_.refs_5_
  73.8 0.7 copy-done.1
  74.5 3.0 %shard_map.121 = (bf16[640,2048]{1,0:T(8,128)(2,1)S(1)}, bf16[640,384]{1,0:T(8,128)(2,1)S(1)}, f32[640,384]{1,0:T(8,128)S(1)}, f32[640,384]{1,0:T(8,128)S(1)}) custom-call(bf16[256,1280]{1,0:T(8,128)(2,1)S(1)} %bitcast.23, bf16[256,1280]{1,0:T(8,128)(2,1)S(1)} %copy-done.1, bf16[256,1280]{1,0:T(8,128)(2,1)S(1)} %collective-permute-done.3.refs_2_, ...), custom_call_target="tpu_custom_call" | custom-call | flops 3019898880 | bytes 5242880 | tf_op jit(solution)/shard_map/pallas_call | solution.py:169
  77.5 5.6 %collective-permute-done.refs_1_ = bf16[256,1280]{1,0:T(8,128)(2,1)S(1)} collective-permute-done((bf16[256,1280]{1,0:T(8,128)(2,1)S(1)}, bf16[256,1280]{1,0:T(8,128)(2,1)S(1)}, u32[]{:S(2)}, u32[]{:S(2)}) %collective-permute-start) | collective-permute-done | bytes 655392 | tf_op jit(solution)/shard_map/ppermute | solution.py:278
  83.1 0.1 collective-permute-start.9
  83.3 3.5 %collective-permute-start.10 = (bf16[128,1280]{1,0:T(8,128)(2,1)S(1)}, bf16[128,1280]{1,0:T(8,128)(2,1)S(1)}, u32[]{:S(2)}, u32[]{:S(2)}) collective-permute-start(bf16[128,1280]{1,0:T(8,128)(2,1)S(1)} %slice.34), channel_id=1, source_target_pairs={{0,192},{64,0},{128,64},{192,128},{1,193},{65,1},{129,65},{193,129... | collective-permute-start | bytes 983048 | tf_op jit(solution)/shard_map/ppermute | solution.py:278
  86.7 0.2 pad_maximum_fusion.2.refs_7_.refs_6_
  86.9 4.1 %shard_map.122 = (bf16[256,1408]{1,0:T(8,128)(2,1)S(1)}, bf16[256,1408]{1,0:T(8,128)(2,1)S(1)}, bf16[256,1408]{1,0:T(8,128)(2,1)S(1)}, bf16[480,2048]{1,0:T(8,128)(2,1)S(1)}, bf16[480,768]{1,0:T(8,128)(2,1)S(1)}) custom-call(bf16[256,1280]{1,0:T(8,128)(2,1)S(1)} %bitcast.20, bf16[256,1280]{1,0:T(8,128)(2,1)S(1)} %collective-permute-done.refs_1_, ...), custom_call_target="tpu_custom_call" | custom-call | flops 3397386240 | bytes 5898240 | tf_op jit(solution)/shard_map/pallas_call | solution.py:224
  91.0 0.1 collective-permute-start.7
  91.2 2.0 %collective-permute-start.8 = (bf16[256,1408]{1,0:T(8,128)(2,1)S(1)}, bf16[256,1408]{1,0:T(8,128)(2,1)S(1)}, u32[]{:S(2)}, u32[]{:S(2)}) collective-permute-start(bf16[256,1408]{1,0:T(8,128)(2,1)S(1)} %get-tuple-element.39), channel_id=1, source_target_pairs={{0,64},{64,128},{128,192},{192,0},{1,65},{65,129},{129,193},{193,1... | collective-permute-start | bytes 2162696 | tf_op jit(solution)/shard_map/ppermute | solution.py:278
  93.2 1.3 collective-permute-done.9.refs_0_
  94.4 0.5 collective-permute-done.10.refs_1_
  94.9 1.9 %shard_map.123 = (bf16[256,1408]{1,0:T(8,128)(2,1)S(1)}, bf16[160,2048]{1,0:T(8,128)(2,1)S(1)}, bf16[160,768]{1,0:T(8,128)(2,1)S(1)}) custom-call(bf16[128,1280]{1,0:T(8,128)(2,1)S(1)} %collective-permute-done.9.refs_0_, bf16[128,1280]{1,0:T(8,128)(2,1)S(1)} %collective-permute-done.10.refs_1_, bf16[640,384]{1,0:T(8,128)(2,1)S(1)} %get-tuple-element.34.refs_3_.refs_2_.hid, ...), custom_call_target="tpu_custom_call" | custom-call | flops 1132462080 | bytes 1966080 | tf_op jit(solution)/shard_map/pallas_call | solution.py:224
  96.8 2.0 %collective-permute-start.11 = (bf16[256,1408]{1,0:T(8,128)(2,1)S(1)}, bf16[256,1408]{1,0:T(8,128)(2,1)S(1)}, u32[]{:S(2)}, u32[]{:S(2)}) collective-permute-start(bf16[256,1408]{1,0:T(8,128)(2,1)S(1)} %get-tuple-element.40), channel_id=1, source_target_pairs={{0,128},{64,192},{128,0},{192,64},{1,129},{65,193},{129,1},{193,65... | collective-permute-start | bytes 2162696 | tf_op jit(solution)/shard_map/ppermute | solution.py:278
  98.8 5.8 %shard_map.124 = bf16[576,2048]{1,0:T(8,128)(2,1)} custom-call(bf16[640,384]{1,0:T(8,128)(2,1)S(1)} %get-tuple-element.34.refs_3_.refs_2_.hid, bf16[480,768]{1,0:T(8,128)(2,1)S(1)} %get-tuple-element.41.d1, bf16[160,768]{1,0:T(8,128)(2,1)S(1)} %get-tuple-element.42.d2, bf16[640,2048]{1,0:T(8,128)(2,1)S(1)} %get-tuple-element.43.x, ...), custom_call_target="tpu_custom_call" | custom-call | flops 3019898880 | bytes 9961472 | tf_op jit(solution)/shard_map/pallas_call | solution.py:263
  104.6 5.6 %collective-permute-done.7 = bf16[256,1408]{1,0:T(8,128)(2,1)S(1)} collective-permute-done((bf16[256,1408]{1,0:T(8,128)(2,1)S(1)}, bf16[256,1408]{1,0:T(8,128)(2,1)S(1)}, u32[]{:S(2)}, u32[]{:S(2)}) %collective-permute-start.7) | collective-permute-done | bytes 720928 | tf_op jit(solution)/shard_map/ppermute | solution.py:278
  110.2 12.2 %collective-permute-done.8 = bf16[256,1408]{1,0:T(8,128)(2,1)S(1)} collective-permute-done((bf16[256,1408]{1,0:T(8,128)(2,1)S(1)}, bf16[256,1408]{1,0:T(8,128)(2,1)S(1)}, u32[]{:S(2)}, u32[]{:S(2)}) %collective-permute-start.8) | collective-permute-done | bytes 720928 | tf_op jit(solution)/shard_map/ppermute | solution.py:278
  122.4 1.2 fusion
  123.6 9.8 %all-to-all-start.2 = ((bf16[32,8,1408]{2,1,0:T(8,128)(2,1)}), bf16[32,8,1408]{2,1,0:T(8,128)(2,1)S(1)}, u32[]{:S(2)}, u32[]{:S(2)}) async-start(bf16[32,8,1408]{2,1,0:T(8,128)(2,1)} %fusion), calls=%async_computation.2 | async-start | bytes 1441792 | tf_op jit(solution)/shard_map/all_to_all | solution.py:309
  133.4 0.0 copy-start.2
  133.4 0.0 copy-start.3
  133.4 1.7 %copy-done.5 = bf16[640,2048]{1,0:T(8,128)(2,1)S(1)} copy-done((bf16[640,2048]{1,0:T(8,128)(2,1)S(1)}, bf16[640,2048]{1,0:T(8,128)(2,1)}, u32[]{:S(2)}) %copy-start.5) | copy-done | bytes 2621464
  135.2 1.5 copy-done.7
  136.7 6.6 %shard_map.125 = (bf16[192,2048]{1,0:T(8,128)(2,1)}, bf16[192,2048]{1,0:T(8,128)(2,1)}, bf16[192,2048]{1,0:T(8,128)(2,1)}) custom-call(bf16[640,384]{1,0:T(8,128)(2,1)S(1)} %get-tuple-element.34.refs_3_.refs_2_.hid, bf16[480,768]{1,0:T(8,128)(2,1)S(1)} %get-tuple-element.41.d1, bf16[160,768]{1,0:T(8,128)(2,1)S(1)} %get-tuple-element.42.d2, ...), custom_call_target="tpu_custom_call" | custom-call | flops 3019898880 | bytes 9961472 | tf_op jit(solution)/shard_map/pallas_call | solution.py:263
  143.3 11.8 %all-to-all-done.2 = bf16[32,8,1408]{2,1,0:T(8,128)(2,1)S(1)} async-done(((bf16[32,8,1408]{2,1,0:T(8,128)(2,1)}), bf16[32,8,1408]{2,1,0:T(8,128)(2,1)S(1)}, u32[]{:S(2)}, u32[]{:S(2)}) %all-to-all-start.2) | async-done | bytes 720928 | tf_op jit(solution)/shard_map/all_to_all | solution.py:309
  155.1 1.4 shard_map.126
  (30 shorter events, 0.2 us)
Async XLA Ops:
  0.6 14.5 %copy-start.12 = (bf16[1,192,2048]{2,1,0:T(8,128)(2,1)S(1)}, bf16[1,192,2048]{2,1,0:T(8,128)(2,1)}, u32[]{:S(2)}) copy-start(bf16[1,192,2048]{2,1,0:T(8,128)(2,1)} %param.15) | copy-start | bytes 2359300
  0.6 14.5 %copy-start.8 = (bf16[1,192,2048]{2,1,0:T(8,128)(2,1)S(1)}, bf16[1,192,2048]{2,1,0:T(8,128)(2,1)}, u32[]{:S(2)}) copy-start(bf16[1,192,2048]{2,1,0:T(8,128)(2,1)} %param.14) | copy-start | bytes 2359300
  0.7 14.5 %copy-start.10 = (bf16[1,192,2048]{2,1,0:T(8,128)(2,1)S(1)}, bf16[1,192,2048]{2,1,0:T(8,128)(2,1)}, u32[]{:S(2)}) copy-start(bf16[1,192,2048]{2,1,0:T(8,128)(2,1)} %param.13) | copy-start | bytes 2359300
  3.5 31.3 %all-to-all-start = ((bf16[32,8,1280]{2,1,0:T(8,128)(2,1)}), bf16[32,8,1280]{2,1,0:T(8,128)(2,1)S(1)}, u32[]{:S(2)}, u32[]{:S(2)}) async-start(bf16[32,8,1280]{2,1,0:T(8,128)(2,1)} %bitcast.36), calls=%async_computation | async-start | bytes 1310720 | tf_op jit(solution)/shard_map/all_to_all | solution.py:309
  16.8 54.8 %collective-permute-start.6 = (bf16[576,2048]{1,0:T(8,128)(2,1)}, bf16[576,2048]{1,0:T(8,128)(2,1)}, u32[]{:S(2)}, u32[]{:S(2)}) collective-permute-start(bf16[576,2048]{1,0:T(8,128)(2,1)} %pad_maximum_fusion.1), channel_id=1, source_target_pairs={{0,32},{32,0},{1,33},{33,1},{2,34},{34,2},{3,35},{35,3},{4,36},{36... | collective-permute-start | bytes 7077896 | tf_op jit(solution)/shard_map/ppermute | solution.py:278
  34.8 33.4 %all-to-all-start.1 = ((bf16[32,8,1280]{2,1,0:T(8,128)(2,1)}), bf16[32,8,1280]{2,1,0:T(8,128)(2,1)S(1)}, u32[]{:S(2)}, u32[]{:S(2)}) async-start(bf16[32,8,1280]{2,1,0:T(8,128)(2,1)} %bitcast.35), calls=%async_computation.1 | async-start | bytes 1310720 | tf_op jit(solution)/shard_map/all_to_all | solution.py:309
  40.4 15.5 %collective-permute-start.3 = (bf16[256,1280]{1,0:T(8,128)(2,1)S(1)}, bf16[256,1280]{1,0:T(8,128)(2,1)S(1)}, u32[]{:S(2)}, u32[]{:S(2)}) collective-permute-start(bf16[256,1280]{1,0:T(8,128)(2,1)S(1)} %bitcast.21), channel_id=1, source_target_pairs={{0,192},{64,0},{128,64},{192,128},{1,193},{65,1},{129,65},{193,129... | collective-permute-start | bytes 1966088 | tf_op jit(solution)/shard_map/ppermute | solution.py:278
  43.5 16.2 %collective-permute-start.2 = (bf16[256,1280]{1,0:T(8,128)(2,1)S(1)}, bf16[256,1280]{1,0:T(8,128)(2,1)S(1)}, u32[]{:S(2)}, u32[]{:S(2)}) collective-permute-start(bf16[256,1280]{1,0:T(8,128)(2,1)S(1)} %bitcast.22), channel_id=1, source_target_pairs={{0,64},{64,128},{128,192},{192,0},{1,65},{65,129},{129,193},{193,1... | collective-permute-start | bytes 1966088 | tf_op jit(solution)/shard_map/ppermute | solution.py:278
  55.9 8.4 %collective-permute-start.5 = (bf16[128,1280]{1,0:T(8,128)(2,1)S(1)}, bf16[128,1280]{1,0:T(8,128)(2,1)S(1)}, u32[]{:S(2)}, u32[]{:S(2)}) collective-permute-start(bf16[128,1280]{1,0:T(8,128)(2,1)S(1)} %slice.29), channel_id=1, source_target_pairs={{0,192},{64,0},{128,64},{192,128},{1,193},{65,1},{129,65},{193,129... | collective-permute-start | bytes 983048 | tf_op jit(solution)/shard_map/ppermute | solution.py:278
  59.7 4.6 %copy-start = (bf16[256,1280]{1,0:T(8,128)(2,1)}, bf16[256,1280]{1,0:T(8,128)(2,1)S(1)}, u32[]{:S(2)}) copy-start(bf16[256,1280]{1,0:T(8,128)(2,1)S(1)} %collective-permute-done.2.refs_1_) | copy-start | bytes 1966084
  59.7 8.4 %collective-permute-start.4 = (bf16[128,1280]{1,0:T(8,128)(2,1)S(1)}, bf16[128,1280]{1,0:T(8,128)(2,1)S(1)}, u32[]{:S(2)}, u32[]{:S(2)}) collective-permute-start(bf16[128,1280]{1,0:T(8,128)(2,1)S(1)} %slice.28), channel_id=1, source_target_pairs={{0,64},{64,128},{128,192},{192,0},{1,65},{65,129},{129,193},{193,1... | collective-permute-start | bytes 983048 | tf_op jit(solution)/shard_map/ppermute | solution.py:278
  68.2 5.2 %copy-start.9 = (bf16[1,192,2048]{2,1,0:T(8,128)(2,1)S(1)}, bf16[1,192,2048]{2,1,0:T(8,128)(2,1)}, u32[]{:S(2)}) copy-start(bf16[1,192,2048]{2,1,0:T(8,128)(2,1)} %param.14) | copy-start | bytes 2359300
  68.2 5.2 %copy-start.11 = (bf16[1,192,2048]{2,1,0:T(8,128)(2,1)S(1)}, bf16[1,192,2048]{2,1,0:T(8,128)(2,1)}, u32[]{:S(2)}) copy-start(bf16[1,192,2048]{2,1,0:T(8,128)(2,1)} %param.13) | copy-start | bytes 2359300
  68.2 14.9 %collective-permute-start = (bf16[256,1280]{1,0:T(8,128)(2,1)S(1)}, bf16[256,1280]{1,0:T(8,128)(2,1)S(1)}, u32[]{:S(2)}, u32[]{:S(2)}) collective-permute-start(bf16[256,1280]{1,0:T(8,128)(2,1)S(1)} %bitcast.18), channel_id=1, source_target_pairs={{0,64},{64,128},{128,192},{192,0},{1,65},{65,129},{129,193},{193,1... | collective-permute-start | bytes 1966088 | tf_op jit(solution)/shard_map/ppermute | solution.py:278
  68.3 14.9 %collective-permute-start.1 = (bf16[256,1280]{1,0:T(8,128)(2,1)S(1)}, bf16[256,1280]{1,0:T(8,128)(2,1)S(1)}, u32[]{:S(2)}, u32[]{:S(2)}) collective-permute-start(bf16[256,1280]{1,0:T(8,128)(2,1)S(1)} %bitcast.19), channel_id=1, source_target_pairs={{0,192},{64,0},{128,64},{192,128},{1,193},{65,1},{129,65},{193,129... | collective-permute-start | bytes 1966088 | tf_op jit(solution)/shard_map/ppermute | solution.py:278
  73.4 1.1 copy-start.1
  74.5 12.3 %copy-start.13 = (bf16[1,192,2048]{2,1,0:T(8,128)(2,1)S(1)}, bf16[1,192,2048]{2,1,0:T(8,128)(2,1)}, u32[]{:S(2)}) copy-start(bf16[1,192,2048]{2,1,0:T(8,128)(2,1)} %param.15) | copy-start | bytes 2359300
  77.5 21.3 %copy-start.4 = (bf16[640,2048]{1,0:T(8,128)(2,1)}, bf16[640,2048]{1,0:T(8,128)(2,1)S(1)}, u32[]{:S(2)}) copy-start(bf16[640,2048]{1,0:T(8,128)(2,1)S(1)} %get-tuple-element.43.x) | copy-start | bytes 7864324
  83.1 11.3 %collective-permute-start.9 = (bf16[128,1280]{1,0:T(8,128)(2,1)S(1)}, bf16[128,1280]{1,0:T(8,128)(2,1)S(1)}, u32[]{:S(2)}, u32[]{:S(2)}) collective-permute-start(bf16[128,1280]{1,0:T(8,128)(2,1)S(1)} %slice.33), channel_id=1, source_target_pairs={{0,64},{64,128},{128,192},{192,0},{1,65},{65,129},{129,193},{193,1... | collective-permute-start | bytes 983048 | tf_op jit(solution)/shard_map/ppermute | solution.py:278
  83.3 11.6 %collective-permute-start.10 = (bf16[128,1280]{1,0:T(8,128)(2,1)S(1)}, bf16[128,1280]{1,0:T(8,128)(2,1)S(1)}, u32[]{:S(2)}, u32[]{:S(2)}) collective-permute-start(bf16[128,1280]{1,0:T(8,128)(2,1)S(1)} %slice.34), channel_id=1, source_target_pairs={{0,192},{64,0},{128,64},{192,128},{1,193},{65,1},{129,65},{193,129... | collective-permute-start | bytes 983048 | tf_op jit(solution)/shard_map/ppermute | solution.py:278
  91.0 7.8 %copy-start.6 = (bf16[480,2048]{1,0:T(8,128)(2,1)}, bf16[480,2048]{1,0:T(8,128)(2,1)S(1)}, u32[]{:S(2)}) copy-start(bf16[480,2048]{1,0:T(8,128)(2,1)S(1)} %get-tuple-element.44.dy1) | copy-start | bytes 5898244
  91.0 19.2 %collective-permute-start.7 = (bf16[256,1408]{1,0:T(8,128)(2,1)S(1)}, bf16[256,1408]{1,0:T(8,128)(2,1)S(1)}, u32[]{:S(2)}, u32[]{:S(2)}) collective-permute-start(bf16[256,1408]{1,0:T(8,128)(2,1)S(1)} %get-tuple-element.38), channel_id=1, source_target_pairs={{0,192},{64,0},{128,64},{192,128},{1,193},{65,1},{129,65},{193,129... | collective-permute-start | bytes 2162696 | tf_op jit(solution)/shard_map/ppermute | solution.py:278
  91.2 31.2 %collective-permute-start.8 = (bf16[256,1408]{1,0:T(8,128)(2,1)S(1)}, bf16[256,1408]{1,0:T(8,128)(2,1)S(1)}, u32[]{:S(2)}, u32[]{:S(2)}) collective-permute-start(bf16[256,1408]{1,0:T(8,128)(2,1)S(1)} %get-tuple-element.39), channel_id=1, source_target_pairs={{0,64},{64,128},{128,192},{192,0},{1,65},{65,129},{129,193},{193,1... | collective-permute-start | bytes 2162696 | tf_op jit(solution)/shard_map/ppermute | solution.py:278
  96.8 25.6 %collective-permute-start.11 = (bf16[256,1408]{1,0:T(8,128)(2,1)S(1)}, bf16[256,1408]{1,0:T(8,128)(2,1)S(1)}, u32[]{:S(2)}, u32[]{:S(2)}) collective-permute-start(bf16[256,1408]{1,0:T(8,128)(2,1)S(1)} %get-tuple-element.40), channel_id=1, source_target_pairs={{0,128},{64,192},{128,0},{192,64},{1,129},{65,193},{129,1},{193,65... | collective-permute-start | bytes 2162696 | tf_op jit(solution)/shard_map/ppermute | solution.py:278
  122.4 11.0 %collective-permute-start.12 = (bf16[576,2048]{1,0:T(8,128)(2,1)}, bf16[576,2048]{1,0:T(8,128)(2,1)}, u32[]{:S(2)}, u32[]{:S(2)}) collective-permute-start(bf16[576,2048]{1,0:T(8,128)(2,1)} %shard_map.124), channel_id=1, source_target_pairs={{0,32},{32,0},{1,33},{33,1},{2,34},{34,2},{3,35},{35,3},{4,36},{36... | collective-permute-start | bytes 7077896 | tf_op jit(solution)/shard_map/ppermute | solution.py:278
  123.6 31.5 %all-to-all-start.2 = ((bf16[32,8,1408]{2,1,0:T(8,128)(2,1)}), bf16[32,8,1408]{2,1,0:T(8,128)(2,1)S(1)}, u32[]{:S(2)}, u32[]{:S(2)}) async-start(bf16[32,8,1408]{2,1,0:T(8,128)(2,1)} %fusion), calls=%async_computation.2 | async-start | bytes 1441792 | tf_op jit(solution)/shard_map/all_to_all | solution.py:309
  133.4 21.7 %copy-start.2 = (s32[128,1]{0,1:T(1,128)S(1)}, s32[128,1]{0,1:T(1,128)}, u32[]{:S(2)}) copy-start(s32[128,1]{0,1:T(1,128)} %param.10) | copy-start | bytes 1540
  133.4 21.7 %copy-start.3 = (bf16[128,1]{0,1:T(2,128)(2,1)S(1)}, bf16[128,1]{0,1:T(2,128)(2,1)}, u32[]{:S(2)}) copy-start(bf16[128,1]{0,1:T(2,128)(2,1)} %param.11) | copy-start | bytes 772
  133.4 1.7 %copy-start.5 = (bf16[640,2048]{1,0:T(8,128)(2,1)S(1)}, bf16[640,2048]{1,0:T(8,128)(2,1)}, u32[]{:S(2)}) copy-start(bf16[640,2048]{1,0:T(8,128)(2,1)} %copy-done.4) | copy-start | bytes 7864324
  135.2 1.5 copy-start.7

commit v3 on v2

--- a/solution.py
+++ b/solution.py
@@ -141,14 +141,19 @@
     out[:, half + piece :] = main.astype(BF)
 
 
-def x_part(*refs):
-    xs, wgu = refs[:4], refs[4]
-    x_ref, hid_ref, slope_ref, silu_ref, pre = refs[5:]
-    order, order_last = orders(xs[0].shape[0])
+def held_rows(refs):
+    return refs[0][...] if len(refs) == 1 else jnp.concatenate([ref[...] for ref in refs], axis=0)
+
+
+def x_part(counts, *refs):
+    refs = list(refs)
+    xs = [[refs.pop(0) for _ in range(count)] for count in counts]
+    wgu, x_ref, hid_ref, slope_ref, silu_ref, pre = refs
+    order, order_last = orders(xs[0][0].shape[0])
     total, both = hid_ref.shape
     block = total // 4
     for b in range(4):
-        open_chunks(xs[b][...], x_ref, b * block, order, order_last)
+        open_chunks(held_rows(xs[b]), x_ref, b * block, order, order_last)
     pre[...] = dot(x_ref[...], wgu[...], LANES)
     step = math.gcd(block, 32)
     for r in range(0, total, step):
@@ -162,43 +167,41 @@
 
 
 def call_x_part(xs, wgu):
-    rows, packed = xs[0].shape
+    rows = xs[0][0].shape[0]
     pairs, width = wgu.shape
+    flat = [v for held in xs for v in held]
     total = 4 * (rows // 2 + rows // 8)
     half_units = jax.ShapeDtypeStruct((total, pairs // 2), F32)
     return pl.pallas_call(
-        x_part,
+        functools.partial(x_part, [len(held) for held in xs]),
         out_shape=[
             jax.ShapeDtypeStruct((total, width), BF),
             jax.ShapeDtypeStruct((total, pairs // 2), BF),
             half_units,
             half_units,
         ],
-        in_specs=vmem(5),
+        in_specs=vmem(len(flat) + 1),
         out_specs=vmem(4),
         scratch_shapes=[pltpu.VMEM((total, pairs), F32)],
         compiler_params=params(),
-        cost_estimate=pl.CostEstimate(
-            flops=3 * total * pairs * width, bytes_accessed=4 * total * width, transcendentals=total * pairs // 2
-        ),
-    )(*xs, wgu)
-
-
-def dy_part(first, blocks, ins, *refs):
-    dys, (hid, slope, silu, wgu, wd) = refs[:ins], refs[ins : ins + 5]
-    outs = refs[ins + 5 : ins + 5 + blocks]
-    dy_ref, d_ref, back = refs[ins + 5 + blocks :]
+        cost_estimate=pl.CostEstimate(flops=1000, bytes_accessed=1000, transcendentals=0),
+    )(*flat, wgu)
+
+
+def dy_part(first, counts, *refs):
+    refs = list(refs)
+    blocks = len(counts)
+    dys = [[refs.pop(0) for _ in range(count)] for count in counts]
+    hid, slope, silu, wgu, wd = refs[:5]
+    outs = refs[5 : 5 + blocks]
+    dy_ref, d_ref, back = refs[5 + blocks :]
     total = dy_ref.shape[0]
     both = wd.shape[0]
     block = total // blocks
     begin = first * block
     order, order_last = orders(outs[0].shape[0])
     for b in range(blocks):
-        if ins > blocks:
-            packed = jnp.concatenate([ref[...] for ref in dys], axis=0)
-        else:
-            packed = dys[b][...]
-        open_chunks(packed, dy_ref, b * block, order, order_last)
+        open_chunks(held_rows(dys[b]), dy_ref, b * block, order, order_last)
     back[...] = dot(dy_ref[...], wd[...], LANES)
     step = math.gcd(block, 32)
     columns = []
@@ -216,23 +219,23 @@
         close_chunks(part, column, outs[b], order, order_last)
 
 
-def call_dy_part(first, blocks, dys, hid, slope, silu, wgu, wd):
-    packed = dys[0].shape[1]
+def call_dy_part(first, dys, hid, slope, silu, wgu, wd):
+    blocks = len(dys)
+    packed = dys[0][0].shape[1]
+    flat = [v for held in dys for v in held]
     both, width = wd.shape
     total = hid.shape[0] // 4 * blocks
     rows = hid.shape[0] // 4 * 8 // 5
     return pl.pallas_call(
-        functools.partial(dy_part, first, blocks, len(dys)),
+        functools.partial(dy_part, first, [len(held) for held in dys]),
         out_shape=[jax.ShapeDtypeStruct((rows, packed + 128), BF)] * blocks
         + [jax.ShapeDtypeStruct((total, width), BF), jax.ShapeDtypeStruct((total, 2 * both), BF)],
-        in_specs=vmem(len(dys) + 5),
+        in_specs=vmem(len(flat) + 5),
         out_specs=vmem(blocks + 2),
         scratch_shapes=[pltpu.VMEM((total, both), F32)],
         compiler_params=params(),
-        cost_estimate=pl.CostEstimate(
-            flops=9 * total * both * width, bytes_accessed=6 * total * width, transcendentals=0
-        ),
-    )(*dys, hid, slope, silu, wgu, wd)
+        cost_estimate=pl.CostEstimate(flops=1000, bytes_accessed=1000, transcendentals=0),
+    )(*flat, hid, slope, silu, wgu, wd)
 
 
 def grad_block(own, has_more, units, hid, d1, d2, x, dy1, dy2, *refs):
@@ -268,9 +271,7 @@
         + [piece(3 * units)] * len(more),
         out_specs=out_specs,
         compiler_params=params(),
-        cost_estimate=pl.CostEstimate(
-            flops=12 * total * units * width, bytes_accessed=4 * total * width + 12 * units * width, transcendentals=0
-        ),
+        cost_estimate=pl.CostEstimate(flops=1000, bytes_accessed=1000, transcendentals=0),
     )(hid, d1, d2, x, dy1, dy2, *more)
 
 
@@ -284,13 +285,6 @@
     count, width = tokens.shape
     packed = width // 2 + width // 8
     rows = experts * 8
-    units = w_gate.shape[1]
-    flip = lambda v: along(v, "core", 2, 1)
-    mine = [w_gate[0], w_up[0], w_down[0]]
-    swapped = flip(jnp.concatenate(mine, axis=0))
-    theirs = [swapped[i * units : (i + 1) * units] for i in range(3)]
-    wgu = jnp.concatenate([mine[0], theirs[0], mine[1], theirs[1]], axis=0)
-    wd = jnp.concatenate([mine[2], theirs[2]], axis=0)
     routes_row = routes.reshape(1, count)
     gates_row = gates.reshape(1, count)
     mask_row = loss_mask.reshape(1, count)
@@ -309,19 +303,34 @@
         return lax.all_to_all(chunks, ("z", "x"), 0, 0, tiled=True).reshape(v.shape)
 
     step = lambda v, by: along(v, "y", ring, by)
+    units = w_gate.shape[1]
+    flip = lambda v: along(v, "core", 2, 1)
+    packed_dy = pack(routes_row, gates_row, mask_row, cotangent)
+    packed_dy, *mine = lax.optimization_barrier((packed_dy, w_gate[0], w_up[0], w_down[0]))
+    swapped = flip(jnp.concatenate(mine, axis=0))
+    theirs = [swapped[i * units : (i + 1) * units] for i in range(3)]
+    wgu = jnp.concatenate([mine[0], theirs[0], mine[1], theirs[1]], axis=0)
+    wd = jnp.concatenate([mine[2], theirs[2]], axis=0)
     x_own = dispatch(pack(routes_row, tokens))
-    packed_dy = pack(routes_row, gates_row, mask_row, cotangent)
     x_own, packed_dy = lax.optimization_barrier((x_own, packed_dy))
     dy_own = dispatch(packed_dy)
     cut = rows // 2
-    x_low, x_high = step(x_own, 1), step(x_own, -1)
-    far = [step(x_low[:cut], 1), step(x_high[cut:], -1)]
-    xs = [x_own, x_low, x_high, jnp.concatenate(far, axis=0)]
+
+    def near(own):
+        first, second = own[:cut], own[cut:]
+        return step(first, 1), step(second, -1), step(second, 1), step(first, -1)
+
+    def gathered(own, low_first, high_second, low_second, high_first):
+        far = [step(low_first, 1), step(high_second, -1)]
+        return [[own], [low_first, low_second], [high_first, high_second], far]
+
+    xs = gathered(x_own, *near(x_own))
     x_all, hid, slope, silu = call_x_part(xs, wgu)
-    low, high = step(dy_own, 1), step(dy_own, -1)
-    far = [step(low[:cut], 1), step(high[cut:], -1)]
-    p_own, p_low, p_high, dy1, d1 = call_dy_part(0, 3, [dy_own, low, high], hid, slope, silu, wgu, wd)
-    p_far, dy2, d2 = call_dy_part(3, 1, far, hid, slope, silu, wgu, wd)
+    low_first, high_second, low_second, high_first = near(dy_own)
+    low_first, high_second, hid = lax.optimization_barrier((low_first, high_second, hid))
+    dys = gathered(dy_own, low_first, high_second, low_second, high_first)
+    p_own, p_low, p_high, dy1, d1 = call_dy_part(0, dys[:3], hid, slope, silu, wgu, wd)
+    p_far, dy2, d2 = call_dy_part(3, dys[3:], hid, slope, silu, wgu, wd)
     arrived = [step(p_low, -1), step(p_high, 1), step(p_far, 2)]
     (given,) = call_grads(False, hid, d1, d2, x_all, dy1, dy2, [])
     *arrived, given = lax.optimization_barrier((*arrived, given))

time: 157 us -> 154 us (0.981)
  waiting for transfers between devices: 73 us -> 56 us
  local copies, waits for them, and re-layouts: 5.88 us -> 12.7 us
  starting transfers between devices: 44.9 us -> 50.6 us
    ppermute x13 -> x17, waiting for transfers between devices: 45.9 us -> 26.8 us  [along(): return lax.ppermute(v, axis, [(i, (i + by) % size) for i in range(size)])]
    unnamed x28 -> x56, local copies, waits for them, and re-layouts: 3.99 us -> 9.92 us
    ppermute x13 -> x17, starting transfers between devices: 17.9 us -> 23.6 us  [along(): return lax.ppermute(v, axis, [(i, (i + by) % size) for i in range(size)])]
    all_to_all x3, waiting for transfers between devices: 27.1 us -> 29.2 us  [dispatch(): return lax.all_to_all(chunks, ('z', 'x'), 0, 0, tiled=True).reshape(v.shape)]
  transfers between devices with their start and end apart: 16 -> 20, of which waited for: 10 -> 9; matrix products, arithmetic and copies ran while one was open for 3% -> 4% of each run, Pallas kernels for 15% -> 16%
where the time goes in v3:
time: 154 us; the launch traced here: 153 us
  waiting for transfers between devices  56 us (36%)
  starting transfers between devices  50.6 us (33%)
  Pallas kernels  29.6 us (19%)
  local copies, waits for them, and re-layouts  12.7 us (8%)
  other arithmetic  3.39 us (2%)
    all_to_all x3, waiting for transfers between devices, dispatch(): return lax.all_to_all(chunks, ('z', 'x'), 0, 0, tiled=True).reshape(v.shape)  29.2 us
    all_to_all x3, starting transfers between devices, dispatch(): return lax.all_to_all(chunks, ('z', 'x'), 0, 0, tiled=True).reshape(v.shape)  27 us
    ppermute x17, waiting for transfers between devices, along(): return lax.ppermute(v, axis, [(i, (i + by) % size) for i in range(size)])  26.8 us
    ppermute x17, starting transfers between devices, along(): return lax.ppermute(v, axis, [(i, (i + by) % size) for i in range(size)])  23.6 us
    pallas_call x2, Pallas kernels, call_grads(): pl.pallas_call(functools.partial(grad_block, own, bool(more), units), gri...  12.5 us
    unnamed x56, local copies, waits for them, and re-layouts  9.92 us
    pallas_call x2, Pallas kernels, call_dy_part(): pl.pallas_call(functools.partial(dy_part, first, [len(held) for held in d...  6.01 us
    pallas_call x2, Pallas kernels, pack(): pl.pallas_call(functools.partial(pack_tokens, len(operands) > 2), out_sha...  5.65 us
  transfers between devices with their start and end apart: 20, of which 9 were waited for; matrix products, arithmetic and copies ran while one was open for 4% of the time, Pallas kernels for 16%

profile of v3, /device:TPU:2, one launch (start us, length us, event | category | flops | bytes accessed | tf_op | source)
XLA Modules:
  0.0 153.3 jit_solution(2983641981982088394)
XLA Ops:
  0.7 2.9 %shard_map.119 = bf16[256,1280]{1,0:T(8,128)(2,1)} custom-call(s32[1,128]{1,0:T(1,128)} %bitcast.24, bf16[128,2048]{1,0:T(8,128)(2,1)} %refs_1_.1), custom_call_target="tpu_custom_call" | custom-call | tf_op jit(solution)/shard_map/pallas_call | solution.py:293
  3.5 11.6 %all-to-all-start = ((bf16[32,8,1280]{2,1,0:T(8,128)(2,1)}), bf16[32,8,1280]{2,1,0:T(8,128)(2,1)S(1)}, u32[]{:S(2)}, u32[]{:S(2)}) async-start(bf16[32,8,1280]{2,1,0:T(8,128)(2,1)} %bitcast.36), calls=%async_computation | async-start | bytes 1310720 | tf_op jit(solution)/shard_map/all_to_all | solution.py:303
  15.2 2.8 %shard_map.120 = bf16[256,1280]{1,0:T(8,128)(2,1)} custom-call(s32[1,128]{1,0:T(1,128)} %bitcast.25, bf16[1,128]{1,0:T(2,128)(2,1)} %bitcast.27, s32[1,128]{1,0:T(1,128)} %bitcast.37, bf16[128,2048]{1,0:T(8,128)(2,1)} %refs_3_.1), custom_call_target="tpu_custom_call" | custom-call | tf_op jit(solution)/shard_map/pallas_call | solution.py:293
  17.9 1.6 %pad_maximum_fusion.1 = bf16[576,2048]{1,0:T(8,128)(2,1)} fusion(bf16[192,2048]{1,0:T(8,128)(2,1)S(1)} %bitcast.33, bf16[192,2048]{1,0:T(8,128)(2,1)S(1)} %bitcast.29, bf16[192,2048]{1,0:T(8,128)(2,1)S(1)} %bitcast.31), kind=kLoop, calls=%fused_computation.1 | loop fusion | flops 7077888 | bytes 4718592 | tf_op jit(solution)/shard_map/concatenate | solution.py:310
  19.5 15.3 %all-to-all-done = bf16[32,8,1280]{2,1,0:T(8,128)(2,1)S(1)} async-done(((bf16[32,8,1280]{2,1,0:T(8,128)(2,1)}), bf16[32,8,1280]{2,1,0:T(8,128)(2,1)S(1)}, u32[]{:S(2)}, u32[]{:S(2)}) %all-to-all-start) | async-done | bytes 655392 | tf_op jit(solution)/shard_map/all_to_all | solution.py:303
  34.8 5.6 %all-to-all-start.1 = ((bf16[32,8,1280]{2,1,0:T(8,128)(2,1)}), bf16[32,8,1280]{2,1,0:T(8,128)(2,1)S(1)}, u32[]{:S(2)}, u32[]{:S(2)}) async-start(bf16[32,8,1280]{2,1,0:T(8,128)(2,1)} %bitcast.35), calls=%async_computation.1 | async-start | bytes 1310720 | tf_op jit(solution)/shard_map/all_to_all | solution.py:303
  40.4 0.9 fusion.2
  41.3 1.6 %collective-permute-start.2 = (bf16[128,1280]{1,0:T(8,128)(2,1)}, bf16[128,1280]{1,0:T(8,128)(2,1)S(1)}, u32[]{:S(2)}, u32[]{:S(2)}) collective-permute-start(bf16[128,1280]{1,0:T(8,128)(2,1)} %get-tuple-element.77), channel_id=1, source_target_pairs={{0,64},{64,128},{128,192},{192,0},{1,65},{65,129},{129,193},{193,1... | collective-permute-start | bytes 983048 | tf_op jit(solution)/shard_map/ppermute | solution.py:279
  42.8 1.7 %collective-permute-start.5 = (bf16[128,1280]{1,0:T(8,128)(2,1)}, bf16[128,1280]{1,0:T(8,128)(2,1)S(1)}, u32[]{:S(2)}, u32[]{:S(2)}) collective-permute-start(bf16[128,1280]{1,0:T(8,128)(2,1)} %get-tuple-element.76), channel_id=1, source_target_pairs={{0,192},{64,0},{128,64},{192,128},{1,193},{65,1},{129,65},{193,129... | collective-permute-start | bytes 983048 | tf_op jit(solution)/shard_map/ppermute | solution.py:279
  44.5 0.4 collective-permute-start.3
  44.9 2.9 %collective-permute-start.4 = (bf16[128,1280]{1,0:T(8,128)(2,1)}, bf16[128,1280]{1,0:T(8,128)(2,1)S(1)}, u32[]{:S(2)}, u32[]{:S(2)}) collective-permute-start(bf16[128,1280]{1,0:T(8,128)(2,1)} %get-tuple-element.77), channel_id=1, source_target_pairs={{0,192},{64,0},{128,64},{192,128},{1,193},{65,1},{129,65},{193,129... | collective-permute-start | bytes 983048 | tf_op jit(solution)/shard_map/ppermute | solution.py:279
  47.7 5.6 %collective-permute-done.2.refs_1_ = bf16[128,1280]{1,0:T(8,128)(2,1)S(1)} collective-permute-done((bf16[128,1280]{1,0:T(8,128)(2,1)}, bf16[128,1280]{1,0:T(8,128)(2,1)S(1)}, u32[]{:S(2)}, u32[]{:S(2)}) %collective-permute-start.2) | collective-permute-done | bytes 327712 | tf_op jit(solution)/shard_map/ppermute | solution.py:279
  53.3 0.4 collective-permute-start.6
  53.7 2.9 %collective-permute-start.7 = (bf16[128,1280]{1,0:T(8,128)(2,1)S(1)}, bf16[128,1280]{1,0:T(8,128)(2,1)S(1)}, u32[]{:S(2)}, u32[]{:S(2)}) collective-permute-start(bf16[128,1280]{1,0:T(8,128)(2,1)S(1)} %collective-permute-done.5.refs_4_), channel_id=1, source_target_pairs={{0,192},{64,0},{128,64},{192,128},{1,193},{65,1},{129,65},{193,129... | collective-permute-start | bytes 983048 | tf_op jit(solution)/shard_map/ppermute | solution.py:279
  56.6 2.5 %all-to-all-done.1 = bf16[32,8,1280]{2,1,0:T(8,128)(2,1)S(1)} async-done(((bf16[32,8,1280]{2,1,0:T(8,128)(2,1)}), bf16[32,8,1280]{2,1,0:T(8,128)(2,1)S(1)}, u32[]{:S(2)}, u32[]{:S(2)}) %all-to-all-start.1) | async-done | bytes 655392 | tf_op jit(solution)/shard_map/all_to_all | solution.py:303
  59.1 1.2 collective-permute-done.3.refs_2_
  60.4 0.4 collective-permute-start
  60.8 2.8 %collective-permute-start.1 = (bf16[128,1280]{1,0:T(8,128)(2,1)S(1)}, bf16[128,1280]{1,0:T(8,128)(2,1)S(1)}, u32[]{:S(2)}, u32[]{:S(2)}) collective-permute-start(bf16[128,1280]{1,0:T(8,128)(2,1)S(1)} %get-tuple-element.78), channel_id=1, source_target_pairs={{0,192},{64,0},{128,64},{192,128},{1,193},{65,1},{129,65},{193,129... | collective-permute-start | bytes 983048 | tf_op jit(solution)/shard_map/ppermute | solution.py:279
  63.6 1.9 %fusion.1 = (bf16[192,2048]{1,0:T(8,128)(2,1)S(1)}, bf16[192,2048]{1,0:T(8,128)(2,1)S(1)}, bf16[192,2048]{1,0:T(8,128)(2,1)S(1)}) fusion(bf16[576,2048]{1,0:T(8,128)(2,1)} %collective-permute-done.8), kind=kLoop, calls=%fused_computation.7 | loop fusion | bytes 4718592 | tf_op jit(solution)/shard_map/slice | solution.py:311
  65.6 0.5 pad_maximum_fusion.refs_7_.refs_8_.refs_5_
  66.1 0.7 copy-done.14
  66.8 0.6 collective-permute-done.6.refs_5_
  67.4 0.7 copy-done.16
  68.1 2.6 %collective-permute-start.10 = (bf16[128,1280]{1,0:T(8,128)(2,1)S(1)}, bf16[128,1280]{1,0:T(8,128)(2,1)S(1)}, u32[]{:S(2)}, u32[]{:S(2)}) collective-permute-start(bf16[128,1280]{1,0:T(8,128)(2,1)S(1)} %get-tuple-element.79), channel_id=1, source_target_pairs={{0,192},{64,0},{128,64},{192,128},{1,193},{65,1},{129,65},{193,129... | collective-permute-start | bytes 983048 | tf_op jit(solution)/shard_map/ppermute | solution.py:279
  70.8 0.7 copy-done.18
  71.5 1.0 copy-done.13
  72.5 1.0 copy-done.15
  73.5 1.0 copy-done.17
  74.4 1.0 copy-done.19
  75.4 3.0 %shard_map.121 = (bf16[640,2048]{1,0:T(8,128)(2,1)S(1)}, bf16[640,384]{1,0:T(8,128)(2,1)S(1)}, f32[640,384]{1,0:T(8,128)S(1)}, f32[640,384]{1,0:T(8,128)S(1)}) custom-call(bf16[256,1280]{1,0:T(8,128)(2,1)S(1)} %bitcast.23, bf16[128,1280]{1,0:T(8,128)(2,1)S(1)} %collective-permute-done.2.refs_1_, bf16[128,1280]{1,0:T(8,128)(2,1)S(1)} %copy-done.13, ...), custom_call_target="tpu_custom_call" | custom-call | flops 1000 | bytes 1000 | tf_op jit(solution)/shard_map/pallas_call | solution.py:175
  78.5 3.2 %collective-permute-start.14 = (bf16[128,1280]{1,0:T(8,128)(2,1)S(1)}, bf16[128,1280]{1,0:T(8,128)(2,1)S(1)}, u32[]{:S(2)}, u32[]{:S(2)}) collective-permute-start(bf16[128,1280]{1,0:T(8,128)(2,1)S(1)} %collective-permute-done.1.refs_4_), channel_id=1, source_target_pairs={{0,192},{64,0},{128,64},{192,128},{1,193},{65,1},{129,65},{193,129... | collective-permute-start | bytes 983048 | tf_op jit(solution)/shard_map/ppermute | solution.py:279
  81.9 4.1 %shard_map.122 = (bf16[256,1408]{1,0:T(8,128)(2,1)S(1)}, bf16[256,1408]{1,0:T(8,128)(2,1)S(1)}, bf16[256,1408]{1,0:T(8,128)(2,1)S(1)}, bf16[480,2048]{1,0:T(8,128)(2,1)S(1)}, bf16[480,768]{1,0:T(8,128)(2,1)S(1)}) custom-call(bf16[256,1280]{1,0:T(8,128)(2,1)S(1)} %bitcast.21, bf16[128,1280]{1,0:T(8,128)(2,1)S(1)} %collective-permute-done.refs_1_, ...), custom_call_target="tpu_custom_call" | custom-call | flops 1000 | bytes 1000 | tf_op jit(solution)/shard_map/pallas_call | solution.py:229
  86.0 1.4 collective-permute-start.11
  87.5 0.7 collective-permute-start.12
  88.1 1.4 collective-permute-done.14.refs_1_
  89.6 1.9 %shard_map.123 = (bf16[256,1408]{1,0:T(8,128)(2,1)S(1)}, bf16[160,2048]{1,0:T(8,128)(2,1)S(1)}, bf16[160,768]{1,0:T(8,128)(2,1)S(1)}) custom-call(bf16[128,1280]{1,0:T(8,128)(2,1)S(1)} %collective-permute-done.13.refs_0_, bf16[128,1280]{1,0:T(8,128)(2,1)S(1)} %collective-permute-done.14.refs_1_, bf16[640,384]{1,0:T(8,128)(2,1)S(1)} %get-tuple-element.48.refs_5_.refs_2_.hid, ...), custom_call_target="tpu_custom_call" | custom-call | flops 1000 | bytes 1000 | tf_op jit(solution)/shard_map/pallas_call | solution.py:229
  91.5 2.5 %collective-permute-start.15 = (bf16[256,1408]{1,0:T(8,128)(2,1)S(1)}, bf16[256,1408]{1,0:T(8,128)(2,1)S(1)}, u32[]{:S(2)}, u32[]{:S(2)}) collective-permute-start(bf16[256,1408]{1,0:T(8,128)(2,1)S(1)} %get-tuple-element.54), channel_id=1, source_target_pairs={{0,128},{64,192},{128,0},{192,64},{1,129},{65,193},{129,1},{193,65... | collective-permute-start | bytes 2162696 | tf_op jit(solution)/shard_map/ppermute | solution.py:279
  94.0 5.8 %shard_map.124 = bf16[576,2048]{1,0:T(8,128)(2,1)} custom-call(bf16[640,384]{1,0:T(8,128)(2,1)S(1)} %get-tuple-element.48.refs_5_.refs_2_.hid, bf16[480,768]{1,0:T(8,128)(2,1)S(1)} %get-tuple-element.55.d1, bf16[160,768]{1,0:T(8,128)(2,1)S(1)} %get-tuple-element.56.d2, bf16[640,2048]{1,0:T(8,128)(2,1)S(1)} %get-tuple-element.57.x, ...), custom_call_target="tpu_custom_call" | custom-call | flops 1000 | bytes 1000 | tf_op jit(solution)/shard_map/pallas_call | solution.py:266
  99.9 17.4 %collective-permute-done.11 = bf16[256,1408]{1,0:T(8,128)(2,1)S(1)} collective-permute-done((bf16[256,1408]{1,0:T(8,128)(2,1)S(1)}, bf16[256,1408]{1,0:T(8,128)(2,1)S(1)}, u32[]{:S(2)}, u32[]{:S(2)}) %collective-permute-start.11) | collective-permute-done | bytes 720928 | tf_op jit(solution)/shard_map/ppermute | solution.py:279
  117.2 0.6 collective-permute-done.15
  117.8 1.3 fusion
  119.1 9.8 %all-to-all-start.2 = ((bf16[32,8,1408]{2,1,0:T(8,128)(2,1)}), bf16[32,8,1408]{2,1,0:T(8,128)(2,1)}, u32[]{:S(2)}, u32[]{:S(2)}) async-start(bf16[32,8,1408]{2,1,0:T(8,128)(2,1)} %fusion), calls=%async_computation.2 | async-start | bytes 1441792 | tf_op jit(solution)/shard_map/all_to_all | solution.py:303
  129.0 1.5 %copy-done.1 = bf16[480,2048]{1,0:T(8,128)(2,1)S(1)} copy-done((bf16[480,2048]{1,0:T(8,128)(2,1)S(1)}, bf16[480,2048]{1,0:T(8,128)(2,1)}, u32[]{:S(2)}) %copy-start.1) | copy-done | bytes 1966104
  130.5 1.1 copy-done.7
  131.6 1.1 copy-done.9
  132.7 6.6 %shard_map.125 = (bf16[192,2048]{1,0:T(8,128)(2,1)}, bf16[192,2048]{1,0:T(8,128)(2,1)}, bf16[192,2048]{1,0:T(8,128)(2,1)}) custom-call(bf16[640,384]{1,0:T(8,128)(2,1)S(1)} %get-tuple-element.48.refs_5_.refs_2_.hid, bf16[480,768]{1,0:T(8,128)(2,1)S(1)} %copy-done.7, bf16[160,768]{1,0:T(8,128)(2,1)S(1)} %get-tuple-element.56.d2, ...), custom_call_target="tpu_custom_call" | custom-call | flops 1000 | bytes 1000 | tf_op jit(solution)/shard_map/pallas_call | solution.py:266
  139.3 11.4 %all-to-all-done.2 = bf16[32,8,1408]{2,1,0:T(8,128)(2,1)} async-done(((bf16[32,8,1408]{2,1,0:T(8,128)(2,1)}), bf16[32,8,1408]{2,1,0:T(8,128)(2,1)}, u32[]{:S(2)}, u32[]{:S(2)}) %all-to-all-start.2) | async-done | bytes 720928 | tf_op jit(solution)/shard_map/all_to_all | solution.py:303
  150.7 2.5 %shard_map.126 = (bf16[128,2048]{1,0:T(8,128)(2,1)}, f32[1,128]{1,0:T(1,128)}) custom-call(s32[1,128]{1,0:T(1,128)S(1)} %bitcast.26, bf16[1,128]{1,0:T(2,128)(2,1)S(1)} %bitcast.28, bf16[256,1408]{1,0:T(8,128)(2,1)} %bitcast.13.r_ref), custom_call_target="tpu_custom_call" | custom-call | tf_op jit(solution)/shard_map/pallas_call | solution.py:344
  (63 shorter events, 0.4 us)
Async XLA Ops:
  0.6 17.3 %copy-start.24 = (bf16[1,192,2048]{2,1,0:T(8,128)(2,1)S(1)}, bf16[1,192,2048]{2,1,0:T(8,128)(2,1)}, u32[]{:S(2)}) copy-start(bf16[1,192,2048]{2,1,0:T(8,128)(2,1)} %param.13) | copy-start | bytes 2359300
  0.6 17.3 %copy-start.22 = (bf16[1,192,2048]{2,1,0:T(8,128)(2,1)S(1)}, bf16[1,192,2048]{2,1,0:T(8,128)(2,1)}, u32[]{:S(2)}) copy-start(bf16[1,192,2048]{2,1,0:T(8,128)(2,1)} %param.14) | copy-start | bytes 2359300
  0.7 17.3 %copy-start.26 = (bf16[1,192,2048]{2,1,0:T(8,128)(2,1)S(1)}, bf16[1,192,2048]{2,1,0:T(8,128)(2,1)}, u32[]{:S(2)}) copy-start(bf16[1,192,2048]{2,1,0:T(8,128)(2,1)} %param.15) | copy-start | bytes 2359300
  3.5 31.3 %all-to-all-start = ((bf16[32,8,1280]{2,1,0:T(8,128)(2,1)}), bf16[32,8,1280]{2,1,0:T(8,128)(2,1)S(1)}, u32[]{:S(2)}, u32[]{:S(2)}) async-start(bf16[32,8,1280]{2,1,0:T(8,128)(2,1)} %bitcast.36), calls=%async_computation | async-start | bytes 1310720 | tf_op jit(solution)/shard_map/all_to_all | solution.py:303
  19.5 41.3 %collective-permute-start.8 = (bf16[576,2048]{1,0:T(8,128)(2,1)}, bf16[576,2048]{1,0:T(8,128)(2,1)}, u32[]{:S(2)}, u32[]{:S(2)}) collective-permute-start(bf16[576,2048]{1,0:T(8,128)(2,1)} %pad_maximum_fusion.1), channel_id=1, source_target_pairs={{0,32},{32,0},{1,33},{33,1},{2,34},{34,2},{3,35},{35,3},{4,36},{36... | collective-permute-start | bytes 7077896 | tf_op jit(solution)/shard_map/ppermute | solution.py:279
  34.8 30.7 %copy-start.4 = (bf16[32,8,1280]{2,1,0:T(8,128)(2,1)}, bf16[32,8,1280]{2,1,0:T(8,128)(2,1)S(1)}, u32[]{:S(2)}) copy-start(bf16[32,8,1280]{2,1,0:T(8,128)(2,1)S(1)} %all-to-all-done) | copy-start | bytes 1966084
  34.8 24.2 %all-to-all-start.1 = ((bf16[32,8,1280]{2,1,0:T(8,128)(2,1)}), bf16[32,8,1280]{2,1,0:T(8,128)(2,1)S(1)}, u32[]{:S(2)}, u32[]{:S(2)}) async-start(bf16[32,8,1280]{2,1,0:T(8,128)(2,1)} %bitcast.35), calls=%async_computation.1 | async-start | bytes 1310720 | tf_op jit(solution)/shard_map/all_to_all | solution.py:303
  41.3 12.1 %collective-permute-start.2 = (bf16[128,1280]{1,0:T(8,128)(2,1)}, bf16[128,1280]{1,0:T(8,128)(2,1)S(1)}, u32[]{:S(2)}, u32[]{:S(2)}) collective-permute-start(bf16[128,1280]{1,0:T(8,128)(2,1)} %get-tuple-element.77), channel_id=1, source_target_pairs={{0,64},{64,128},{128,192},{192,0},{1,65},{65,129},{129,193},{193,1... | collective-permute-start | bytes 983048 | tf_op jit(solution)/shard_map/ppermute | solution.py:279
  42.8 10.9 %collective-permute-start.5 = (bf16[128,1280]{1,0:T(8,128)(2,1)}, bf16[128,1280]{1,0:T(8,128)(2,1)S(1)}, u32[]{:S(2)}, u32[]{:S(2)}) collective-permute-start(bf16[128,1280]{1,0:T(8,128)(2,1)} %get-tuple-element.76), channel_id=1, source_target_pairs={{0,192},{64,0},{128,64},{192,128},{1,193},{65,1},{129,65},{193,129... | collective-permute-start | bytes 983048 | tf_op jit(solution)/shard_map/ppermute | solution.py:279
  44.5 15.9 %collective-permute-start.3 = (bf16[128,1280]{1,0:T(8,128)(2,1)}, bf16[128,1280]{1,0:T(8,128)(2,1)S(1)}, u32[]{:S(2)}, u32[]{:S(2)}) collective-permute-start(bf16[128,1280]{1,0:T(8,128)(2,1)} %get-tuple-element.76), channel_id=1, source_target_pairs={{0,64},{64,128},{128,192},{192,0},{1,65},{65,129},{129,193},{193,1... | collective-permute-start | bytes 983048 | tf_op jit(solution)/shard_map/ppermute | solution.py:279
  44.9 21.2 %collective-permute-start.4 = (bf16[128,1280]{1,0:T(8,128)(2,1)}, bf16[128,1280]{1,0:T(8,128)(2,1)S(1)}, u32[]{:S(2)}, u32[]{:S(2)}) collective-permute-start(bf16[128,1280]{1,0:T(8,128)(2,1)} %get-tuple-element.77), channel_id=1, source_target_pairs={{0,192},{64,0},{128,64},{192,128},{1,193},{65,1},{129,65},{193,129... | collective-permute-start | bytes 983048 | tf_op jit(solution)/shard_map/ppermute | solution.py:279
  53.3 14.0 %collective-permute-start.6 = (bf16[128,1280]{1,0:T(8,128)(2,1)S(1)}, bf16[128,1280]{1,0:T(8,128)(2,1)S(1)}, u32[]{:S(2)}, u32[]{:S(2)}) collective-permute-start(bf16[128,1280]{1,0:T(8,128)(2,1)S(1)} %collective-permute-done.2.refs_1_), channel_id=1, source_target_pairs={{0,64},{64,128},{128,192},{192,0},{1,65},{65,129},{129,193},{193,1... | collective-permute-start | bytes 983048 | tf_op jit(solution)/shard_map/ppermute | solution.py:279
  53.7 11.8 %copy-start.10 = (bf16[128,1280]{1,0:T(8,128)(2,1)}, bf16[128,1280]{1,0:T(8,128)(2,1)S(1)}, u32[]{:S(2)}) copy-start(bf16[128,1280]{1,0:T(8,128)(2,1)S(1)} %collective-permute-done.5.refs_4_) | copy-start | bytes 983044
  53.7 17.1 %collective-permute-start.7 = (bf16[128,1280]{1,0:T(8,128)(2,1)S(1)}, bf16[128,1280]{1,0:T(8,128)(2,1)S(1)}, u32[]{:S(2)}, u32[]{:S(2)}) collective-permute-start(bf16[128,1280]{1,0:T(8,128)(2,1)S(1)} %collective-permute-done.5.refs_4_), channel_id=1, source_target_pairs={{0,192},{64,0},{128,64},{192,128},{1,193},{65,1},{129,65},{193,129... | collective-permute-start | bytes 983048 | tf_op jit(solution)/shard_map/ppermute | solution.py:279
  59.0 6.5 %copy-start.2 = (bf16[32,8,1280]{2,1,0:T(8,128)(2,1)}, bf16[32,8,1280]{2,1,0:T(8,128)(2,1)S(1)}, u32[]{:S(2)}) copy-start(bf16[32,8,1280]{2,1,0:T(8,128)(2,1)S(1)} %all-to-all-done.1) | copy-start | bytes 1966084
  59.1 6.4 %copy-start.23 = (bf16[1,192,2048]{2,1,0:T(8,128)(2,1)S(1)}, bf16[1,192,2048]{2,1,0:T(8,128)(2,1)}, u32[]{:S(2)}) copy-start(bf16[1,192,2048]{2,1,0:T(8,128)(2,1)} %param.14) | copy-start | bytes 2359300
  59.1 6.4 %copy-start.25 = (bf16[1,192,2048]{2,1,0:T(8,128)(2,1)S(1)}, bf16[1,192,2048]{2,1,0:T(8,128)(2,1)}, u32[]{:S(2)}) copy-start(bf16[1,192,2048]{2,1,0:T(8,128)(2,1)} %param.13) | copy-start | bytes 2359300
  60.4 5.7 %copy-start.12 = (bf16[128,1280]{1,0:T(8,128)(2,1)}, bf16[128,1280]{1,0:T(8,128)(2,1)S(1)}, u32[]{:S(2)}) copy-start(bf16[128,1280]{1,0:T(8,128)(2,1)S(1)} %collective-permute-done.3.refs_2_) | copy-start | bytes 983044
  60.4 18.1 %collective-permute-start = (bf16[128,1280]{1,0:T(8,128)(2,1)S(1)}, bf16[128,1280]{1,0:T(8,128)(2,1)S(1)}, u32[]{:S(2)}, u32[]{:S(2)}) collective-permute-start(bf16[128,1280]{1,0:T(8,128)(2,1)S(1)} %get-tuple-element.79), channel_id=1, source_target_pairs={{0,64},{64,128},{128,192},{192,0},{1,65},{65,129},{129,193},{193,1... | collective-permute-start | bytes 983048 | tf_op jit(solution)/shard_map/ppermute | solution.py:279
  60.8 17.6 %collective-permute-start.1 = (bf16[128,1280]{1,0:T(8,128)(2,1)S(1)}, bf16[128,1280]{1,0:T(8,128)(2,1)S(1)}, u32[]{:S(2)}, u32[]{:S(2)}) collective-permute-start(bf16[128,1280]{1,0:T(8,128)(2,1)S(1)} %get-tuple-element.78), channel_id=1, source_target_pairs={{0,192},{64,0},{128,64},{192,128},{1,193},{65,1},{129,65},{193,129... | collective-permute-start | bytes 983048 | tf_op jit(solution)/shard_map/ppermute | solution.py:279
  65.5 6.0 %copy-start.5 = (bf16[32,8,1280]{2,1,0:T(8,128)(2,1)S(1)}, bf16[32,8,1280]{2,1,0:T(8,128)(2,1)}, u32[]{:S(2)}) copy-start(bf16[32,8,1280]{2,1,0:T(8,128)(2,1)} %copy-done.4) | copy-start | bytes 1966084
  65.5 6.0 %copy-start.11 = (bf16[128,1280]{1,0:T(8,128)(2,1)S(1)}, bf16[128,1280]{1,0:T(8,128)(2,1)}, u32[]{:S(2)}) copy-start(bf16[128,1280]{1,0:T(8,128)(2,1)} %copy-done.10) | copy-start | bytes 983044
  65.6 16.2 %copy-start.27 = (bf16[1,192,2048]{2,1,0:T(8,128)(2,1)S(1)}, bf16[1,192,2048]{2,1,0:T(8,128)(2,1)}, u32[]{:S(2)}) copy-start(bf16[1,192,2048]{2,1,0:T(8,128)(2,1)} %param.15) | copy-start | bytes 2359300
  66.0 0.7 copy-start.14
  66.8 15.1 %collective-permute-start.9 = (bf16[128,1280]{1,0:T(8,128)(2,1)S(1)}, bf16[128,1280]{1,0:T(8,128)(2,1)S(1)}, u32[]{:S(2)}, u32[]{:S(2)}) collective-permute-start(bf16[128,1280]{1,0:T(8,128)(2,1)S(1)} %get-tuple-element.78), channel_id=1, source_target_pairs={{0,64},{64,128},{128,192},{192,0},{1,65},{65,129},{129,193},{193,1... | collective-permute-start | bytes 983048 | tf_op jit(solution)/shard_map/ppermute | solution.py:279
  67.4 0.7 copy-start.16
  68.1 13.7 %collective-permute-start.10 = (bf16[128,1280]{1,0:T(8,128)(2,1)S(1)}, bf16[128,1280]{1,0:T(8,128)(2,1)S(1)}, u32[]{:S(2)}, u32[]{:S(2)}) collective-permute-start(bf16[128,1280]{1,0:T(8,128)(2,1)S(1)} %get-tuple-element.79), channel_id=1, source_target_pairs={{0,192},{64,0},{128,64},{192,128},{1,193},{65,1},{129,65},{193,129... | collective-permute-start | bytes 983048 | tf_op jit(solution)/shard_map/ppermute | solution.py:279
  70.8 0.7 copy-start.18
  71.5 1.0 copy-start.13
  72.5 1.0 copy-start.15
  73.5 1.0 copy-start.17
  74.4 1.0 copy-start.19
  78.4 3.5 %copy-start.3 = (bf16[32,8,1280]{2,1,0:T(8,128)(2,1)S(1)}, bf16[32,8,1280]{2,1,0:T(8,128)(2,1)}, u32[]{:S(2)}) copy-start(bf16[32,8,1280]{2,1,0:T(8,128)(2,1)} %copy-done.2) | copy-start | bytes 1966084
  78.4 9.7 %collective-permute-start.13 = (bf16[128,1280]{1,0:T(8,128)(2,1)S(1)}, bf16[128,1280]{1,0:T(8,128)(2,1)S(1)}, u32[]{:S(2)}, u32[]{:S(2)}) collective-permute-start(bf16[128,1280]{1,0:T(8,128)(2,1)S(1)} %collective-permute-done.refs_1_), channel_id=1, source_target_pairs={{0,64},{64,128},{128,192},{192,0},{1,65},{65,129},{129,193},{193,1... | collective-permute-start | bytes 983048 | tf_op jit(solution)/shard_map/ppermute | solution.py:279
  78.5 11.1 %collective-permute-start.14 = (bf16[128,1280]{1,0:T(8,128)(2,1)S(1)}, bf16[128,1280]{1,0:T(8,128)(2,1)S(1)}, u32[]{:S(2)}, u32[]{:S(2)}) collective-permute-start(bf16[128,1280]{1,0:T(8,128)(2,1)S(1)} %collective-permute-done.1.refs_4_), channel_id=1, source_target_pairs={{0,192},{64,0},{128,64},{192,128},{1,193},{65,1},{129,65},{193,129... | collective-permute-start | bytes 983048 | tf_op jit(solution)/shard_map/ppermute | solution.py:279
  86.0 8.0 %copy-start = (bf16[480,2048]{1,0:T(8,128)(2,1)}, bf16[480,2048]{1,0:T(8,128)(2,1)S(1)}, u32[]{:S(2)}) copy-start(bf16[480,2048]{1,0:T(8,128)(2,1)S(1)} %get-tuple-element.58.dy1) | copy-start | bytes 5898244
  86.0 8.0 %copy-start.6 = (bf16[480,768]{1,0:T(8,128)(2,1)}, bf16[480,768]{1,0:T(8,128)(2,1)S(1)}, u32[]{:S(2)}) copy-start(bf16[480,768]{1,0:T(8,128)(2,1)S(1)} %get-tuple-element.55.d1) | copy-start | bytes 2211844
  86.0 31.2 %collective-permute-start.11 = (bf16[256,1408]{1,0:T(8,128)(2,1)S(1)}, bf16[256,1408]{1,0:T(8,128)(2,1)S(1)}, u32[]{:S(2)}, u32[]{:S(2)}) collective-permute-start(bf16[256,1408]{1,0:T(8,128)(2,1)S(1)} %get-tuple-element.52), channel_id=1, source_target_pairs={{0,192},{64,0},{128,64},{192,128},{1,193},{65,1},{129,65},{193,129... | collective-permute-start | bytes 2162696 | tf_op jit(solution)/shard_map/ppermute | solution.py:279
  87.5 29.8 %collective-permute-start.12 = (bf16[256,1408]{1,0:T(8,128)(2,1)S(1)}, bf16[256,1408]{1,0:T(8,128)(2,1)S(1)}, u32[]{:S(2)}, u32[]{:S(2)}) collective-permute-start(bf16[256,1408]{1,0:T(8,128)(2,1)S(1)} %get-tuple-element.53), channel_id=1, source_target_pairs={{0,64},{64,128},{128,192},{192,0},{1,65},{65,129},{129,193},{193,1... | collective-permute-start | bytes 2162696 | tf_op jit(solution)/shard_map/ppermute | solution.py:279
  91.5 8.4 %copy-start.8 = (bf16[160,2048]{1,0:T(8,128)(2,1)}, bf16[160,2048]{1,0:T(8,128)(2,1)S(1)}, u32[]{:S(2)}) copy-start(bf16[160,2048]{1,0:T(8,128)(2,1)S(1)} %get-tuple-element.59.dy2) | copy-start | bytes 1966084
  91.5 26.4 %collective-permute-start.15 = (bf16[256,1408]{1,0:T(8,128)(2,1)S(1)}, bf16[256,1408]{1,0:T(8,128)(2,1)S(1)}, u32[]{:S(2)}, u32[]{:S(2)}) collective-permute-start(bf16[256,1408]{1,0:T(8,128)(2,1)S(1)} %get-tuple-element.54), channel_id=1, source_target_pairs={{0,128},{64,192},{128,0},{192,64},{1,129},{65,193},{129,1},{193,65... | collective-permute-start | bytes 2162696 | tf_op jit(solution)/shard_map/ppermute | solution.py:279
  117.8 11.1 %collective-permute-start.16 = (bf16[576,2048]{1,0:T(8,128)(2,1)}, bf16[576,2048]{1,0:T(8,128)(2,1)}, u32[]{:S(2)}, u32[]{:S(2)}) collective-permute-start(bf16[576,2048]{1,0:T(8,128)(2,1)} %shard_map.124), channel_id=1, source_target_pairs={{0,32},{32,0},{1,33},{33,1},{2,34},{34,2},{3,35},{35,3},{4,36},{36... | collective-permute-start | bytes 7077896 | tf_op jit(solution)/shard_map/ppermute | solution.py:279
  119.1 31.6 %all-to-all-start.2 = ((bf16[32,8,1408]{2,1,0:T(8,128)(2,1)}), bf16[32,8,1408]{2,1,0:T(8,128)(2,1)}, u32[]{:S(2)}, u32[]{:S(2)}) async-start(bf16[32,8,1408]{2,1,0:T(8,128)(2,1)} %fusion), calls=%async_computation.2 | async-start | bytes 1441792 | tf_op jit(solution)/shard_map/all_to_all | solution.py:303
  129.0 1.5 %copy-start.1 = (bf16[480,2048]{1,0:T(8,128)(2,1)S(1)}, bf16[480,2048]{1,0:T(8,128)(2,1)}, u32[]{:S(2)}) copy-start(bf16[480,2048]{1,0:T(8,128)(2,1)} %copy-done) | copy-start | bytes 5898244
  130.5 1.1 copy-start.7
  131.6 1.1 copy-start.9
  132.7 18.0 %copy-start.20 = (s32[128,1]{0,1:T(1,128)S(1)}, s32[128,1]{0,1:T(1,128)}, u32[]{:S(2)}) copy-start(s32[128,1]{0,1:T(1,128)} %param.10) | copy-start | bytes 1540
  132.7 18.0 %copy-start.21 = (bf16[128,1]{0,1:T(2,128)(2,1)S(1)}, bf16[128,1]{0,1:T(2,128)(2,1)}, u32[]{:S(2)}) copy-start(bf16[128,1]{0,1:T(2,128)(2,1)} %param.11) | copy-start | bytes 772

commit v4 on v3

--- a/solution.py
+++ b/solution.py
@@ -125,20 +125,23 @@
         dst[at + four : at + four + lone, k * piece : (k + 1) * piece] = last[k * lone : (k + 1) * lone]
 
 
-def close_chunks(part, column, out, order, order_last):
-    rows = out.shape[0]
+def close_chunks(part, column, outs, order, order_last):
+    rows = order.shape[0]
     width = part.shape[1]
     half, piece = width // 2, width // 8
     four, lone = rows // 2, rows // 8
     stacked = jnp.concatenate([part[:four, :half], part[:four, half:]], axis=0)
-    out[:, :half] = dot(order, stacked).astype(BF)
+    packed = [dot(order, stacked).astype(BF)]
     stacked = jnp.concatenate([part[four:, k * piece : (k + 1) * piece] for k in range(8)], axis=0)
-    out[:, half : half + piece] = dot(order_last, stacked).astype(BF)
+    packed.append(dot(order_last, stacked).astype(BF))
     column = jnp.broadcast_to(column.astype(BF), (four + lone, 128))
     main = dot(order[:, :four], column[:four])
     pick = iota((rows, lone), 0) == iota((rows, lone), 1) * 8 + 4
     main += dot(jnp.where(pick, 1.0, 0.0).astype(BF), column[four:])
-    out[:, half + piece :] = main.astype(BF)
+    packed = jnp.concatenate([*packed, main.astype(BF)], axis=1)
+    height = rows // len(outs)
+    for i, out in enumerate(outs):
+        out[...] = packed[i * height : (i + 1) * height]
 
 
 def held_rows(refs):
@@ -149,10 +152,10 @@
     refs = list(refs)
     xs = [[refs.pop(0) for _ in range(count)] for count in counts]
     wgu, x_ref, hid_ref, slope_ref, silu_ref, pre = refs
-    order, order_last = orders(xs[0][0].shape[0])
+    order, order_last = orders(sum(ref.shape[0] for ref in xs[0]))
     total, both = hid_ref.shape
-    block = total // 4
-    for b in range(4):
+    block = total // len(counts)
+    for b in range(len(counts)):
         open_chunks(held_rows(xs[b]), x_ref, b * block, order, order_last)
     pre[...] = dot(x_ref[...], wgu[...], LANES)
     step = math.gcd(block, 32)
@@ -167,10 +170,10 @@
 
 
 def call_x_part(xs, wgu):
-    rows = xs[0][0].shape[0]
+    rows = sum(v.shape[0] for v in xs[0])
     pairs, width = wgu.shape
     flat = [v for held in xs for v in held]
-    total = 4 * (rows // 2 + rows // 8)
+    total = len(xs) * (rows // 2 + rows // 8)
     half_units = jax.ShapeDtypeStruct((total, pairs // 2), F32)
     return pl.pallas_call(
         functools.partial(x_part, [len(held) for held in xs]),
@@ -188,18 +191,17 @@
     )(*flat, wgu)
 
 
-def dy_part(first, counts, *refs):
+def dy_part(counts, *refs):
     refs = list(refs)
     blocks = len(counts)
     dys = [[refs.pop(0) for _ in range(count)] for count in counts]
     hid, slope, silu, wgu, wd = refs[:5]
-    outs = refs[5 : 5 + blocks]
-    dy_ref, d_ref, back = refs[5 + blocks :]
+    dy_ref, d_ref, back = refs[-3:]
+    outs = [refs[5 + 2 * b : 7 + 2 * b] for b in range(blocks)]
     total = dy_ref.shape[0]
     both = wd.shape[0]
     block = total // blocks
-    begin = first * block
-    order, order_last = orders(outs[0].shape[0])
+    order, order_last = orders(2 * outs[0][0].shape[0])
     for b in range(blocks):
         open_chunks(held_rows(dys[b]), dy_ref, b * block, order, order_last)
     back[...] = dot(dy_ref[...], wd[...], LANES)
@@ -207,11 +209,10 @@
     columns = []
     for r in range(0, total, step):
         at = slice(r, r + step)
-        there = slice(begin + r, begin + r + step)
         bp = back[at, :]
-        d_ref[at, :both] = (bp * slope[there, :]).astype(BF)
-        d_ref[at, both:] = (bp * silu[there, :]).astype(BF)
-        columns.append(jnp.sum(hid[there, :].astype(F32) * bp, axis=1, keepdims=True))
+        d_ref[at, :both] = (bp * slope[at, :]).astype(BF)
+        d_ref[at, both:] = (bp * silu[at, :]).astype(BF)
+        columns.append(jnp.sum(hid[at, :].astype(F32) * bp, axis=1, keepdims=True))
     for b in range(blocks):
         at = b * block
         part = dot(d_ref[at : at + block, :], wgu[...]).astype(BF)
@@ -219,32 +220,31 @@
         close_chunks(part, column, outs[b], order, order_last)
 
 
-def call_dy_part(first, dys, hid, slope, silu, wgu, wd):
+def call_dy_part(dys, hid, slope, silu, wgu, wd):
     blocks = len(dys)
     packed = dys[0][0].shape[1]
     flat = [v for held in dys for v in held]
     both, width = wd.shape
-    total = hid.shape[0] // 4 * blocks
-    rows = hid.shape[0] // 4 * 8 // 5
+    total = hid.shape[0]
+    rows = total // blocks * 8 // 5
     return pl.pallas_call(
-        functools.partial(dy_part, first, [len(held) for held in dys]),
-        out_shape=[jax.ShapeDtypeStruct((rows, packed + 128), BF)] * blocks
+        functools.partial(dy_part, [len(held) for held in dys]),
+        out_shape=[jax.ShapeDtypeStruct((rows // 2, packed + 128), BF)] * (2 * blocks)
         + [jax.ShapeDtypeStruct((total, width), BF), jax.ShapeDtypeStruct((total, 2 * both), BF)],
         in_specs=vmem(len(flat) + 5),
-        out_specs=vmem(blocks + 2),
+        out_specs=vmem(2 * blocks + 2),
         scratch_shapes=[pltpu.VMEM((total, both), F32)],
         compiler_params=params(),
         cost_estimate=pl.CostEstimate(flops=1000, bytes_accessed=1000, transcendentals=0),
     )(*flat, hid, slope, silu, wgu, wd)
 
 
-def grad_block(own, has_more, units, hid, d1, d2, x, dy1, dy2, *refs):
+def grad_block(own, has_more, units, hid1, hid2, d1, d2, x1, x2, dy1, dy2, *refs):
     out = refs[-1]
-    cut = d1.shape[0]
     both = 2 * units
     first = 0 if own else units
-    down = dot(hid[:cut], dy1[...], ACROSS) + dot(hid[cut:], dy2[...], ACROSS)
-    pair = dot(d1[...], x[:cut], ACROSS) + dot(d2[...], x[cut:], ACROSS)
+    down = dot(hid1[...], dy1[...], ACROSS) + dot(hid2[...], dy2[...], ACROSS)
+    pair = dot(d1[...], x1[...], ACROSS) + dot(d2[...], x2[...], ACROSS)
     values = (pair[first : first + units], pair[both + first : both + first + units], down[first : first + units])
     for i, value in enumerate(values):
         if has_more:
@@ -253,9 +253,9 @@
             out[i * units : (i + 1) * units] = value.astype(BF)
 
 
-def call_grads(own, hid, d1, d2, x, dy1, dy2, more):
-    total, width = x.shape
-    units = hid.shape[1] // 2
+def call_grads(own, acts, rows, more):
+    width = rows[0].shape[1]
+    units = acts[0].shape[1] // 2
     cols = 512
     full = lambda a: pl.BlockSpec(a.shape, lambda j: (0, 0))
     piece = lambda rows: pl.BlockSpec((rows, cols), lambda j: (0, j))
@@ -267,12 +267,17 @@
         functools.partial(grad_block, own, bool(more), units),
         grid=(width // cols,),
         out_shape=out_shape,
-        in_specs=[full(hid), full(d1), full(d2), piece(total), piece(dy1.shape[0]), piece(dy2.shape[0])]
+        in_specs=[full(a) for a in acts]
+        + [piece(r.shape[0]) for r in rows]
         + [piece(3 * units)] * len(more),
         out_specs=out_specs,
-        compiler_params=params(),
+        compiler_params=params(52 if more else 14),
         cost_estimate=pl.CostEstimate(flops=1000, bytes_accessed=1000, transcendentals=0),
-    )(hid, d1, d2, x, dy1, dy2, *more)
+    )(*acts, *rows, *more)
+
+
+def add(*parts):
+    return sum(part.astype(F32) for part in parts).astype(BF)
 
 
 def along(v, axis, size, by):
@@ -316,30 +321,37 @@
     dy_own = dispatch(packed_dy)
     cut = rows // 2
 
-    def near(own):
-        first, second = own[:cut], own[cut:]
-        return step(first, 1), step(second, -1), step(second, 1), step(first, -1)
-
-    def gathered(own, low_first, high_second, low_second, high_first):
-        far = [step(low_first, 1), step(high_second, -1)]
-        return [[own], [low_first, low_second], [high_first, high_second], far]
-
-    xs = gathered(x_own, *near(x_own))
-    x_all, hid, slope, silu = call_x_part(xs, wgu)
-    low_first, high_second, low_second, high_first = near(dy_own)
-    low_first, high_second, hid = lax.optimization_barrier((low_first, high_second, hid))
-    dys = gathered(dy_own, low_first, high_second, low_second, high_first)
-    p_own, p_low, p_high, dy1, d1 = call_dy_part(0, dys[:3], hid, slope, silu, wgu, wd)
-    p_far, dy2, d2 = call_dy_part(3, dys[3:], hid, slope, silu, wgu, wd)
-    arrived = [step(p_low, -1), step(p_high, 1), step(p_far, 2)]
-    (given,) = call_grads(False, hid, d1, d2, x_all, dy1, dy2, [])
-    *arrived, given = lax.optimization_barrier((*arrived, given))
+    def halves(own):
+        return own[:cut], own[cut:]
+
+    def lead(first, second):
+        return step(first, 1), step(second, -1)
+
+    def follow(first, second):
+        return step(second, 1), step(first, -1)
+
+    first, second = halves(x_own)
+    x_lead, x_follow = lead(first, second), follow(first, second)
+    x_near = [[x_own], [x_lead[0], x_follow[0]], [x_follow[1], x_lead[1]]]
+    x1, hid1, slope1, silu1 = call_x_part(x_near, wgu)
+    first, second = halves(dy_own)
+    dy_lead = lead(first, second)
+    first, second, hid1, *x_far = lax.optimization_barrier((first, second, hid1, *lead(*x_lead)))
+    dy_follow = follow(first, second)
+    dy_near = [[dy_own], [dy_lead[0], dy_follow[0]], [dy_follow[1], dy_lead[1]]]
+    own1, own2, low1, low2, high1, high2, dy1, d1 = call_dy_part(dy_near, hid1, slope1, silu1, wgu, wd)
+    x2, hid2, slope2, silu2 = call_x_part([x_far], wgu)
+    *dy_far, low1 = lax.optimization_barrier((*lead(*dy_lead), low1))
+    far1, far2, dy2, d2 = call_dy_part([dy_far], hid2, slope2, silu2, wgu, wd)
+    acts, kept_rows = [hid1, hid2, d1, d2], [x1, x2, dy1, dy2]
+    low1, high2 = step(low1, -1), step(high2, 1)
+    low2 = step(add(low2, step(far2, -1)), -1)
+    high1 = step(add(high1, step(far1, 1)), 1)
+    (given,) = call_grads(False, acts, kept_rows, [])
+    low1, low2, high1, high2, given = lax.optimization_barrier((low1, low2, high1, high2, given))
     taken = flip(given)
-    home = p_own.astype(F32)
-    for part in arrived:
-        home = home + part.astype(F32)
-    returned = dispatch(home.astype(BF))
-    grads = call_grads(True, hid, d1, d2, x_all, dy1, dy2, [taken])
+    returned = dispatch(jnp.concatenate([add(own1, low1, high1), add(own2, low2, high2)], axis=0))
+    grads = call_grads(True, acts, kept_rows, [taken])
     returned, *grads = lax.optimization_barrier((returned, *grads))
     grad_tokens, grad_gates = pl.pallas_call(
         unpack_tokens,

time: 154 us -> 148 us (0.961)
  waiting for transfers between devices: 56 us -> 47.5 us
  local copies, waits for them, and re-layouts: 12.7 us -> 5.42 us
  starting transfers between devices: 50.6 us -> 55.4 us
  Pallas kernels: 29.6 us -> 32.5 us
    ppermute x17 -> x20, waiting for transfers between devices: 26.8 us -> 16.8 us  [along(): return lax.ppermute(v, axis, [(i, (i + by) % size) for i in range(size)])]
    unnamed x56 -> x38, local copies, waits for them, and re-layouts: 9.92 us -> 2.74 us
    ppermute x17 -> x20, starting transfers between devices: 23.6 us -> 28.4 us  [along(): return lax.ppermute(v, axis, [(i, (i + by) % size) for i in range(size)])]
    pallas_call x1 -> x2, Pallas kernels: 2.98 us -> 6.13 us  [call_x_part(): pl.pallas_call(functools.partial(x_part, [len(held) for held in xs]), out...]
  transfers between devices with their start and end apart: 20 -> 23, of which waited for: 9 -> 9; matrix products, arithmetic and copies ran while one was open for 4% -> 5% of each run, Pallas kernels for 16% -> 18%
where the time goes in v4:
time: 148 us; the launch traced here: 146 us
  starting transfers between devices  55.4 us (37%)
  waiting for transfers between devices  47.5 us (32%)
  Pallas kernels  32.5 us (22%)
  local copies, waits for them, and re-layouts  5.42 us (4%)
  other arithmetic  4.54 us (3%)
    all_to_all x3, waiting for transfers between devices, dispatch(): return lax.all_to_all(chunks, ('z', 'x'), 0, 0, tiled=True).reshape(v.shape)  30.7 us
    ppermute x20, starting transfers between devices, along(): return lax.ppermute(v, axis, [(i, (i + by) % size) for i in range(size)])  28.4 us
    all_to_all x3, starting transfers between devices, dispatch(): return lax.all_to_all(chunks, ('z', 'x'), 0, 0, tiled=True).reshape(v.shape)  27 us
    ppermute x20, waiting for transfers between devices, along(): return lax.ppermute(v, axis, [(i, (i + by) % size) for i in range(size)])  16.8 us
    pallas_call x2, Pallas kernels, call_grads(): pl.pallas_call(functools.partial(grad_block, own, bool(more), units), gri...  13.3 us
    pallas_call x2, Pallas kernels, call_x_part(): pl.pallas_call(functools.partial(x_part, [len(held) for held in xs]), out...  6.13 us
    pallas_call x2, Pallas kernels, call_dy_part(): pl.pallas_call(functools.partial(dy_part, [len(held) for held in dys]), o...  6.06 us
    pallas_call x2, Pallas kernels, pack(): pl.pallas_call(functools.partial(pack_tokens, len(operands) > 2), out_sha...  5.61 us
  transfers between devices with their start and end apart: 23, of which 9 were waited for; matrix products, arithmetic and copies ran while one was open for 5% of the time, Pallas kernels for 18%

profile of v4, /device:TPU:2, one launch (start us, length us, event | category | flops | bytes accessed | tf_op | source)
XLA Modules:
  0.0 146.3 jit_solution(14397732579726747618)
XLA Ops:
  0.7 2.8 %shard_map.119 = bf16[256,1280]{1,0:T(8,128)(2,1)} custom-call(s32[1,128]{1,0:T(1,128)} %bitcast.25, bf16[128,2048]{1,0:T(8,128)(2,1)} %refs_1_.1), custom_call_target="tpu_custom_call" | custom-call | tf_op jit(solution)/shard_map/pallas_call | solution.py:298
  3.5 11.6 %all-to-all-start = ((bf16[32,8,1280]{2,1,0:T(8,128)(2,1)}), bf16[32,8,1280]{2,1,0:T(8,128)(2,1)S(1)}, u32[]{:S(2)}, u32[]{:S(2)}) async-start(bf16[32,8,1280]{2,1,0:T(8,128)(2,1)} %bitcast.36), calls=%async_computation | async-start | bytes 1310720 | tf_op jit(solution)/shard_map/all_to_all | solution.py:308
  15.1 2.8 %shard_map.120 = bf16[256,1280]{1,0:T(8,128)(2,1)} custom-call(s32[1,128]{1,0:T(1,128)} %bitcast.26, bf16[1,128]{1,0:T(2,128)(2,1)} %bitcast.28, s32[1,128]{1,0:T(1,128)} %bitcast.37, bf16[128,2048]{1,0:T(8,128)(2,1)} %refs_3_.1), custom_call_target="tpu_custom_call" | custom-call | tf_op jit(solution)/shard_map/pallas_call | solution.py:298
  17.9 2.8 %pad_maximum_fusion.1 = bf16[576,2048]{1,0:T(8,128)(2,1)} fusion(bf16[192,2048]{1,0:T(8,128)(2,1)} %bitcast.34, bf16[192,2048]{1,0:T(8,128)(2,1)S(1)} %bitcast.30, bf16[192,2048]{1,0:T(8,128)(2,1)S(1)} %bitcast.32), kind=kLoop, calls=%fused_computation.1 | loop fusion | flops 7077888 | bytes 4718592 | tf_op jit(solution)/shard_map/concatenate | solution.py:315
  20.7 14.1 %all-to-all-done = bf16[32,8,1280]{2,1,0:T(8,128)(2,1)S(1)} async-done(((bf16[32,8,1280]{2,1,0:T(8,128)(2,1)}), bf16[32,8,1280]{2,1,0:T(8,128)(2,1)S(1)}, u32[]{:S(2)}, u32[]{:S(2)}) %all-to-all-start) | async-done | bytes 655392 | tf_op jit(solution)/shard_map/all_to_all | solution.py:308
  34.8 5.6 %all-to-all-start.1 = ((bf16[32,8,1280]{2,1,0:T(8,128)(2,1)}), bf16[32,8,1280]{2,1,0:T(8,128)(2,1)S(1)}, u32[]{:S(2)}, u32[]{:S(2)}) async-start(bf16[32,8,1280]{2,1,0:T(8,128)(2,1)} %bitcast.8), calls=%async_computation.1 | async-start | bytes 1310720 | tf_op jit(solution)/shard_map/all_to_all | solution.py:308
  40.3 0.9 fusion.1
  41.2 1.6 %collective-permute-start.1 = (bf16[128,1280]{1,0:T(8,128)(2,1)}, bf16[128,1280]{1,0:T(8,128)(2,1)}, u32[]{:S(2)}, u32[]{:S(2)}) collective-permute-start(bf16[128,1280]{1,0:T(8,128)(2,1)} %get-tuple-element.105), channel_id=1, source_target_pairs={{0,64},{64,128},{128,192},{192,0},{1,65},{65,129},{129,193},{193,1... | collective-permute-start | bytes 983048 | tf_op jit(solution)/shard_map/ppermute | solution.py:284
  42.8 1.7 %collective-permute-start.4 = (bf16[128,1280]{1,0:T(8,128)(2,1)}, bf16[128,1280]{1,0:T(8,128)(2,1)}, u32[]{:S(2)}, u32[]{:S(2)}) collective-permute-start(bf16[128,1280]{1,0:T(8,128)(2,1)} %get-tuple-element.104), channel_id=1, source_target_pairs={{0,192},{64,0},{128,64},{192,128},{1,193},{65,1},{129,65},{193,129... | collective-permute-start | bytes 983048 | tf_op jit(solution)/shard_map/ppermute | solution.py:284
  44.4 0.4 collective-permute-start.2
  44.8 2.9 %collective-permute-start.3 = (bf16[128,1280]{1,0:T(8,128)(2,1)}, bf16[128,1280]{1,0:T(8,128)(2,1)S(1)}, u32[]{:S(2)}, u32[]{:S(2)}) collective-permute-start(bf16[128,1280]{1,0:T(8,128)(2,1)} %get-tuple-element.105), channel_id=1, source_target_pairs={{0,192},{64,0},{128,64},{192,128},{1,193},{65,1},{129,65},{193,129... | collective-permute-start | bytes 983048 | tf_op jit(solution)/shard_map/ppermute | solution.py:284
  47.7 5.7 %collective-permute-done.1.refs_1_ = bf16[128,1280]{1,0:T(8,128)(2,1)} collective-permute-done((bf16[128,1280]{1,0:T(8,128)(2,1)}, bf16[128,1280]{1,0:T(8,128)(2,1)}, u32[]{:S(2)}, u32[]{:S(2)}) %collective-permute-start.1) | collective-permute-done | bytes 327712 | tf_op jit(solution)/shard_map/ppermute | solution.py:284
  53.4 0.4 collective-permute-start.6
  53.8 2.9 %collective-permute-start.7 = (bf16[128,1280]{1,0:T(8,128)(2,1)}, bf16[128,1280]{1,0:T(8,128)(2,1)}, u32[]{:S(2)}, u32[]{:S(2)}) collective-permute-start(bf16[128,1280]{1,0:T(8,128)(2,1)} %collective-permute-done.4.refs_4_), channel_id=1, source_target_pairs={{0,192},{64,0},{128,64},{192,128},{1,193},{65,1},{129,65},{193,129... | collective-permute-start | bytes 983048 | tf_op jit(solution)/shard_map/ppermute | solution.py:284
  56.6 2.4 %all-to-all-done.1 = bf16[32,8,1280]{2,1,0:T(8,128)(2,1)S(1)} async-done(((bf16[32,8,1280]{2,1,0:T(8,128)(2,1)}), bf16[32,8,1280]{2,1,0:T(8,128)(2,1)S(1)}, u32[]{:S(2)}, u32[]{:S(2)}) %all-to-all-start.1) | async-done | bytes 655392 | tf_op jit(solution)/shard_map/all_to_all | solution.py:308
  59.0 1.3 collective-permute-done.2.refs_2_
  60.3 0.4 collective-permute-start
  60.7 2.8 %collective-permute-start.10 = (bf16[128,1280]{1,0:T(8,128)(2,1)S(1)}, bf16[128,1280]{1,0:T(8,128)(2,1)S(1)}, u32[]{:S(2)}, u32[]{:S(2)}) collective-permute-start(bf16[128,1280]{1,0:T(8,128)(2,1)S(1)} %get-tuple-element.60), channel_id=1, source_target_pairs={{0,192},{64,0},{128,64},{192,128},{1,193},{65,1},{129,65},{193,129... | collective-permute-start | bytes 983048 | tf_op jit(solution)/shard_map/ppermute | solution.py:284
  63.5 1.8 %fusion = (bf16[192,2048]{1,0:T(8,128)(2,1)S(1)}, bf16[192,2048]{1,0:T(8,128)(2,1)S(1)}, bf16[192,2048]{1,0:T(8,128)(2,1)S(1)}) fusion(bf16[576,2048]{1,0:T(8,128)(2,1)} %collective-permute-done.5), kind=kLoop, calls=%fused_computation.10 | loop fusion | bytes 4718592 | tf_op jit(solution)/shard_map/slice | solution.py:316
  65.3 0.3 pad_maximum_fusion.refs_5_.refs_8_.refs_2_
  65.6 0.7 copy-done.12
  66.4 1.0 copy-done.11
  67.3 1.0 copy-done.13
  68.3 3.5 %shard_map.121 = (bf16[480,2048]{1,0:T(8,128)(2,1)S(1)}, bf16[480,384]{1,0:T(8,128)(2,1)S(1)}, f32[480,384]{1,0:T(8,128)S(1)}, f32[480,384]{1,0:T(8,128)S(1)}) custom-call(bf16[256,1280]{1,0:T(8,128)(2,1)S(1)} %bitcast.23, bf16[128,1280]{1,0:T(8,128)(2,1)} %collective-permute-done.1.refs_1_, bf16[128,1280]{1,0:T(8,128)(2,1)S(1)} %copy-done.11, ...), custom_call_target="tpu_custom_call" | custom-call | flops 1000 | bytes 1000 | tf_op jit(solution)/shard_map/pallas_call | solution.py:178
  71.8 0.3 collective-permute-start.8
  72.1 3.2 %collective-permute-start.9 = (bf16[128,1280]{1,0:T(8,128)(2,1)S(1)}, bf16[128,1280]{1,0:T(8,128)(2,1)S(1)}, u32[]{:S(2)}, u32[]{:S(2)}) collective-permute-start(bf16[128,1280]{1,0:T(8,128)(2,1)S(1)} %get-tuple-element.61), channel_id=1, source_target_pairs={{0,192},{64,0},{128,64},{192,128},{1,193},{65,1},{129,65},{193,129... | collective-permute-start | bytes 983048 | tf_op jit(solution)/shard_map/ppermute | solution.py:284
  75.4 3.2 %collective-permute-start.12 = (bf16[128,1280]{1,0:T(8,128)(2,1)S(1)}, bf16[128,1280]{1,0:T(8,128)(2,1)S(1)}, u32[]{:S(2)}, u32[]{:S(2)}) collective-permute-start(bf16[128,1280]{1,0:T(8,128)(2,1)S(1)} %collective-permute-done.10.refs_4_), channel_id=1, source_target_pairs={{0,192},{64,0},{128,64},{192,128},{1,193},{65,1},{129,65},{193,129... | collective-permute-start | bytes 983048 | tf_op jit(solution)/shard_map/ppermute | solution.py:284
  78.6 0.1 pad_maximum_fusion.2.refs_9_.refs_6_
  78.7 2.6 %shard_map.123 = (bf16[160,2048]{1,0:T(8,128)(2,1)S(1)}, bf16[160,384]{1,0:T(8,128)(2,1)S(1)}, f32[160,384]{1,0:T(8,128)S(1)}, f32[160,384]{1,0:T(8,128)S(1)}) custom-call(bf16[128,1280]{1,0:T(8,128)(2,1)} %collective-permute-done.6.refs_0_, bf16[128,1280]{1,0:T(8,128)(2,1)} %collective-permute-done.7.refs_1_, ...), custom_call_target="tpu_custom_call" | custom-call | flops 1000 | bytes 1000 | tf_op jit(solution)/shard_map/pallas_call | solution.py:178
  81.4 0.8 collective-permute-done.8.refs_2_
  82.2 4.2 %shard_map.122 = (bf16[128,1408]{1,0:T(8,128)(2,1)S(1)}, bf16[128,1408]{1,0:T(8,128)(2,1)S(1)}, bf16[128,1408]{1,0:T(8,128)(2,1)S(1)}, bf16[128,1408]{1,0:T(8,12...) custom-call(bf16[256,1280]{1,0:T(8,128)(2,1)S(1)} %bitcast.21, ...), custom_call_target="tpu_custom_call" | custom-call | flops 1000 | bytes 1000 | tf_op jit(solution)/shard_map/pallas_call | solution.py:230
  86.4 1.9 %shard_map.124 = (bf16[128,1408]{1,0:T(8,128)(2,1)S(1)}, bf16[128,1408]{1,0:T(8,128)(2,1)S(1)}, bf16[160,2048]{1,0:T(8,128)(2,1)S(1)}, bf16[160,768]{1,0:T(8,128)(2,1)S(1)}) custom-call(bf16[128,1280]{1,0:T(8,128)(2,1)S(1)} %collective-permute-done.11.refs_0_, bf16[128,1280]{1,0:T(8,128)(2,1)S(1)} %collective-permute-done.12.refs_1_, ...), custom_call_target="tpu_custom_call" | custom-call | flops 1000 | bytes 1000 | tf_op jit(solution)/shard_map/pallas_call | solution.py:230
  88.4 1.4 collective-permute-start.16
  89.8 1.6 %collective-permute-start.18 = (bf16[128,1408]{1,0:T(8,128)(2,1)S(1)}, bf16[128,1408]{1,0:T(8,128)(2,1)S(1)}, u32[]{:S(2)}, u32[]{:S(2)}) collective-permute-start(bf16[128,1408]{1,0:T(8,128)(2,1)S(1)} %get-tuple-element.79), channel_id=1, source_target_pairs={{0,64},{64,128},{128,192},{192,0},{1,65},{65,129},{129,193},{193,1... | collective-permute-start | bytes 1081352 | tf_op jit(solution)/shard_map/ppermute | solution.py:284
  91.3 1.7 %collective-permute-start.14 = (bf16[128,1408]{1,0:T(8,128)(2,1)S(1)}, bf16[128,1408]{1,0:T(8,128)(2,1)S(1)}, u32[]{:S(2)}, u32[]{:S(2)}) collective-permute-start(bf16[128,1408]{1,0:T(8,128)(2,1)S(1)} %get-tuple-element.76), channel_id=1, source_target_pairs={{0,192},{64,0},{128,64},{192,128},{1,193},{65,1},{129,65},{193,129... | collective-permute-start | bytes 1081352 | tf_op jit(solution)/shard_map/ppermute | solution.py:284
  93.0 0.7 collective-permute-start.13
  93.7 7.3 %collective-permute-done.16 = bf16[128,1408]{1,0:T(8,128)(2,1)S(1)} collective-permute-done((bf16[128,1408]{1,0:T(8,128)(2,1)S(1)}, bf16[128,1408]{1,0:T(8,128)(2,1)S(1)}, u32[]{:S(2)}, u32[]{:S(2)}) %collective-permute-start.16) | collective-permute-done | bytes 360480 | tf_op jit(solution)/shard_map/ppermute | solution.py:284
  101.1 0.4 collective-permute-start.17
  101.5 1.2 collective-permute-done.14
  102.8 3.0 %collective-permute-start.15 = (bf16[128,1408]{1,0:T(8,128)(2,1)S(1)}, bf16[128,1408]{1,0:T(8,128)(2,1)S(1)}, u32[]{:S(2)}, u32[]{:S(2)}) collective-permute-start(bf16[128,1408]{1,0:T(8,128)(2,1)S(1)} %add_convert_fusion.3), channel_id=1, source_target_pairs={{0,192},{64,0},{128,64},{192,128},{1,193},{65,1},{129,65},{193,129... | collective-permute-start | bytes 1081352 | tf_op jit(solution)/shard_map/ppermute | solution.py:284
  105.7 5.8 %shard_map.125 = bf16[576,2048]{1,0:T(8,128)(2,1)} custom-call(bf16[480,384]{1,0:T(8,128)(2,1)S(1)} %get-tuple-element.62.refs_5_.hid1, bf16[160,384]{1,0:T(8,128)(2,1)S(1)} %get-tuple-element.73.refs_2_.hid2, bf16[480,768]{1,0:T(8,128)(2,1)S(1)} %get-tuple-element.80.d1, bf16[160,768]{1,0:T(8,128)(2,1)S(1)} %get-tuple-element.81.d2, ...), custom_call_target="tpu_custom_call" | custom-call | flops 1000 | bytes 1000 | tf_op jit(solution)/shard_map/pallas_call | solution.py:266
  111.6 0.5 collective-permute-done.15
  112.1 0.3 add_convert_fusion
  112.4 1.0 maximum_bitcast_fusion
  113.3 9.8 %all-to-all-start.2 = ((bf16[32,8,1408]{2,1,0:T(8,128)(2,1)}), bf16[32,8,1408]{2,1,0:T(8,128)(2,1)S(1)}, u32[]{:S(2)}, u32[]{:S(2)}) async-start(bf16[32,8,1408]{2,1,0:T(8,128)(2,1)} %maximum_bitcast_fusion), calls=%async_computation.2 | async-start | bytes 1441792 | tf_op jit(solution)/shard_map/all_to_all | solution.py:308
  123.2 7.4 %shard_map.126 = (bf16[192,2048]{1,0:T(8,128)(2,1)}, bf16[192,2048]{1,0:T(8,128)(2,1)}, bf16[192,2048]{1,0:T(8,128)(2,1)}) custom-call(bf16[480,384]{1,0:T(8,128)(2,1)S(1)} %copy-done.3, bf16[160,384]{1,0:T(8,128)(2,1)S(1)} %get-tuple-element.73.refs_2_.hid2, bf16[480,768]{1,0:T(8,128)(2,1)} %copy-done.4, bf16[160,768]{1,0:T(8,128)(2,1)S(1)} %copy-done.9, ...), custom_call_target="tpu_custom_call" | custom-call | flops 1000 | bytes 1000 | tf_op jit(solution)/shard_map/pallas_call | solution.py:266
  130.7 14.2 %all-to-all-done.2 = bf16[32,8,1408]{2,1,0:T(8,128)(2,1)S(1)} async-done(((bf16[32,8,1408]{2,1,0:T(8,128)(2,1)}), bf16[32,8,1408]{2,1,0:T(8,128)(2,1)S(1)}, u32[]{:S(2)}, u32[]{:S(2)}) %all-to-all-start.2) | async-done | bytes 720928 | tf_op jit(solution)/shard_map/all_to_all | solution.py:308
  144.9 1.4 shard_map.127
  (55 shorter events, 0.4 us)
Async XLA Ops:
  0.6 17.3 %copy-start.17 = (bf16[1,192,2048]{2,1,0:T(8,128)(2,1)S(1)}, bf16[1,192,2048]{2,1,0:T(8,128)(2,1)}, u32[]{:S(2)}) copy-start(bf16[1,192,2048]{2,1,0:T(8,128)(2,1)} %param.13) | copy-start | bytes 2359300
  0.6 17.3 %copy-start.16 = (bf16[1,192,2048]{2,1,0:T(8,128)(2,1)S(1)}, bf16[1,192,2048]{2,1,0:T(8,128)(2,1)}, u32[]{:S(2)}) copy-start(bf16[1,192,2048]{2,1,0:T(8,128)(2,1)} %param.14) | copy-start | bytes 2359300
  3.5 31.3 %all-to-all-start = ((bf16[32,8,1280]{2,1,0:T(8,128)(2,1)}), bf16[32,8,1280]{2,1,0:T(8,128)(2,1)S(1)}, u32[]{:S(2)}, u32[]{:S(2)}) async-start(bf16[32,8,1280]{2,1,0:T(8,128)(2,1)} %bitcast.36), calls=%async_computation | async-start | bytes 1310720 | tf_op jit(solution)/shard_map/all_to_all | solution.py:308
  20.7 40.1 %collective-permute-start.5 = (bf16[576,2048]{1,0:T(8,128)(2,1)}, bf16[576,2048]{1,0:T(8,128)(2,1)}, u32[]{:S(2)}, u32[]{:S(2)}) collective-permute-start(bf16[576,2048]{1,0:T(8,128)(2,1)} %pad_maximum_fusion.1), channel_id=1, source_target_pairs={{0,32},{32,0},{1,33},{33,1},{2,34},{34,2},{3,35},{35,3},{4,36},{36... | collective-permute-start | bytes 7077896 | tf_op jit(solution)/shard_map/ppermute | solution.py:284
  34.8 24.2 %all-to-all-start.1 = ((bf16[32,8,1280]{2,1,0:T(8,128)(2,1)}), bf16[32,8,1280]{2,1,0:T(8,128)(2,1)S(1)}, u32[]{:S(2)}, u32[]{:S(2)}) async-start(bf16[32,8,1280]{2,1,0:T(8,128)(2,1)} %bitcast.8), calls=%async_computation.1 | async-start | bytes 1310720 | tf_op jit(solution)/shard_map/all_to_all | solution.py:308
  41.2 12.2 %collective-permute-start.1 = (bf16[128,1280]{1,0:T(8,128)(2,1)}, bf16[128,1280]{1,0:T(8,128)(2,1)}, u32[]{:S(2)}, u32[]{:S(2)}) collective-permute-start(bf16[128,1280]{1,0:T(8,128)(2,1)} %get-tuple-element.105), channel_id=1, source_target_pairs={{0,64},{64,128},{128,192},{192,0},{1,65},{65,129},{129,193},{193,1... | collective-permute-start | bytes 983048 | tf_op jit(solution)/shard_map/ppermute | solution.py:284
  42.8 11.0 %collective-permute-start.4 = (bf16[128,1280]{1,0:T(8,128)(2,1)}, bf16[128,1280]{1,0:T(8,128)(2,1)}, u32[]{:S(2)}, u32[]{:S(2)}) collective-permute-start(bf16[128,1280]{1,0:T(8,128)(2,1)} %get-tuple-element.104), channel_id=1, source_target_pairs={{0,192},{64,0},{128,64},{192,128},{1,193},{65,1},{129,65},{193,129... | collective-permute-start | bytes 983048 | tf_op jit(solution)/shard_map/ppermute | solution.py:284
  44.4 15.9 %collective-permute-start.2 = (bf16[128,1280]{1,0:T(8,128)(2,1)}, bf16[128,1280]{1,0:T(8,128)(2,1)S(1)}, u32[]{:S(2)}, u32[]{:S(2)}) collective-permute-start(bf16[128,1280]{1,0:T(8,128)(2,1)} %get-tuple-element.104), channel_id=1, source_target_pairs={{0,64},{64,128},{128,192},{192,0},{1,65},{65,129},{129,193},{193,1... | collective-permute-start | bytes 983048 | tf_op jit(solution)/shard_map/ppermute | solution.py:284
  44.8 20.8 %collective-permute-start.3 = (bf16[128,1280]{1,0:T(8,128)(2,1)}, bf16[128,1280]{1,0:T(8,128)(2,1)S(1)}, u32[]{:S(2)}, u32[]{:S(2)}) collective-permute-start(bf16[128,1280]{1,0:T(8,128)(2,1)} %get-tuple-element.105), channel_id=1, source_target_pairs={{0,192},{64,0},{128,64},{192,128},{1,193},{65,1},{129,65},{193,129... | collective-permute-start | bytes 983048 | tf_op jit(solution)/shard_map/ppermute | solution.py:284
  53.4 18.4 %collective-permute-start.6 = (bf16[128,1280]{1,0:T(8,128)(2,1)}, bf16[128,1280]{1,0:T(8,128)(2,1)}, u32[]{:S(2)}, u32[]{:S(2)}) collective-permute-start(bf16[128,1280]{1,0:T(8,128)(2,1)} %collective-permute-done.1.refs_1_), channel_id=1, source_target_pairs={{0,64},{64,128},{128,192},{192,0},{1,65},{65,129},{129,193},{193,1... | collective-permute-start | bytes 983048 | tf_op jit(solution)/shard_map/ppermute | solution.py:284
  53.8 18.1 %collective-permute-start.7 = (bf16[128,1280]{1,0:T(8,128)(2,1)}, bf16[128,1280]{1,0:T(8,128)(2,1)}, u32[]{:S(2)}, u32[]{:S(2)}) collective-permute-start(bf16[128,1280]{1,0:T(8,128)(2,1)} %collective-permute-done.4.refs_4_), channel_id=1, source_target_pairs={{0,192},{64,0},{128,64},{192,128},{1,193},{65,1},{129,65},{193,129... | collective-permute-start | bytes 983048 | tf_op jit(solution)/shard_map/ppermute | solution.py:284
  60.3 5.3 %copy-start.10 = (bf16[128,1280]{1,0:T(8,128)(2,1)}, bf16[128,1280]{1,0:T(8,128)(2,1)S(1)}, u32[]{:S(2)}) copy-start(bf16[128,1280]{1,0:T(8,128)(2,1)S(1)} %collective-permute-done.2.refs_2_) | copy-start | bytes 983044
  60.3 15.0 %collective-permute-start = (bf16[128,1280]{1,0:T(8,128)(2,1)S(1)}, bf16[128,1280]{1,0:T(8,128)(2,1)S(1)}, u32[]{:S(2)}, u32[]{:S(2)}) collective-permute-start(bf16[128,1280]{1,0:T(8,128)(2,1)S(1)} %get-tuple-element.61), channel_id=1, source_target_pairs={{0,64},{64,128},{128,192},{192,0},{1,65},{65,129},{129,193},{193,1... | collective-permute-start | bytes 983048 | tf_op jit(solution)/shard_map/ppermute | solution.py:284
  60.7 14.6 %collective-permute-start.10 = (bf16[128,1280]{1,0:T(8,128)(2,1)S(1)}, bf16[128,1280]{1,0:T(8,128)(2,1)S(1)}, u32[]{:S(2)}, u32[]{:S(2)}) collective-permute-start(bf16[128,1280]{1,0:T(8,128)(2,1)S(1)} %get-tuple-element.60), channel_id=1, source_target_pairs={{0,192},{64,0},{128,64},{192,128},{1,193},{65,1},{129,65},{193,129... | collective-permute-start | bytes 983048 | tf_op jit(solution)/shard_map/ppermute | solution.py:284
  65.6 0.7 copy-start.12
  66.4 1.0 copy-start.11
  67.3 1.0 copy-start.13
  68.3 10.3 %copy-start.18 = (bf16[1,192,2048]{2,1,0:T(8,128)(2,1)S(1)}, bf16[1,192,2048]{2,1,0:T(8,128)(2,1)}, u32[]{:S(2)}) copy-start(bf16[1,192,2048]{2,1,0:T(8,128)(2,1)} %param.15) | copy-start | bytes 2359300
  71.8 33.9 %copy-start = (bf16[480,2048]{1,0:T(8,128)(2,1)}, bf16[480,2048]{1,0:T(8,128)(2,1)S(1)}, u32[]{:S(2)}) copy-start(bf16[480,2048]{1,0:T(8,128)(2,1)S(1)} %get-tuple-element.82.x1) | copy-start | bytes 5898244
  71.8 33.9 %copy-start.2 = (bf16[480,384]{1,0:T(8,128)(2,1)}, bf16[480,384]{1,0:T(8,128)(2,1)S(1)}, u32[]{:S(2)}) copy-start(bf16[480,384]{1,0:T(8,128)(2,1)S(1)} %get-tuple-element.62.refs_5_.hid1) | copy-start | bytes 1105924
  71.8 10.3 %collective-permute-start.8 = (bf16[128,1280]{1,0:T(8,128)(2,1)S(1)}, bf16[128,1280]{1,0:T(8,128)(2,1)S(1)}, u32[]{:S(2)}, u32[]{:S(2)}) collective-permute-start(bf16[128,1280]{1,0:T(8,128)(2,1)S(1)} %get-tuple-element.60), channel_id=1, source_target_pairs={{0,64},{64,128},{128,192},{192,0},{1,65},{65,129},{129,193},{193,1... | collective-permute-start | bytes 983048 | tf_op jit(solution)/shard_map/ppermute | solution.py:284
  72.1 10.1 %collective-permute-start.9 = (bf16[128,1280]{1,0:T(8,128)(2,1)S(1)}, bf16[128,1280]{1,0:T(8,128)(2,1)S(1)}, u32[]{:S(2)}, u32[]{:S(2)}) collective-permute-start(bf16[128,1280]{1,0:T(8,128)(2,1)S(1)} %get-tuple-element.61), channel_id=1, source_target_pairs={{0,192},{64,0},{128,64},{192,128},{1,193},{65,1},{129,65},{193,129... | collective-permute-start | bytes 983048 | tf_op jit(solution)/shard_map/ppermute | solution.py:284
  75.3 11.1 %collective-permute-start.11 = (bf16[128,1280]{1,0:T(8,128)(2,1)S(1)}, bf16[128,1280]{1,0:T(8,128)(2,1)S(1)}, u32[]{:S(2)}, u32[]{:S(2)}) collective-permute-start(bf16[128,1280]{1,0:T(8,128)(2,1)S(1)} %collective-permute-done.refs_1_), channel_id=1, source_target_pairs={{0,64},{64,128},{128,192},{192,0},{1,65},{65,129},{129,193},{193,1... | collective-permute-start | bytes 983048 | tf_op jit(solution)/shard_map/ppermute | solution.py:284
  75.4 11.1 %collective-permute-start.12 = (bf16[128,1280]{1,0:T(8,128)(2,1)S(1)}, bf16[128,1280]{1,0:T(8,128)(2,1)S(1)}, u32[]{:S(2)}, u32[]{:S(2)}) collective-permute-start(bf16[128,1280]{1,0:T(8,128)(2,1)S(1)} %collective-permute-done.10.refs_4_), channel_id=1, source_target_pairs={{0,192},{64,0},{128,64},{192,128},{1,193},{65,1},{129,65},{193,129... | collective-permute-start | bytes 983048 | tf_op jit(solution)/shard_map/ppermute | solution.py:284
  81.3 24.4 %copy-start.5 = (bf16[160,2048]{1,0:T(8,128)(2,1)}, bf16[160,2048]{1,0:T(8,128)(2,1)S(1)}, u32[]{:S(2)}) copy-start(bf16[160,2048]{1,0:T(8,128)(2,1)S(1)} %get-tuple-element.83.x2) | copy-start | bytes 1966084
  86.4 19.3 %copy-start.1 = (bf16[480,2048]{1,0:T(8,128)(2,1)}, bf16[480,2048]{1,0:T(8,128)(2,1)S(1)}, u32[]{:S(2)}) copy-start(bf16[480,2048]{1,0:T(8,128)(2,1)S(1)} %get-tuple-element.84.dy1) | copy-start | bytes 5898244
  86.4 19.3 %copy-start.4 = (bf16[480,768]{1,0:T(8,128)(2,1)}, bf16[480,768]{1,0:T(8,128)(2,1)S(1)}, u32[]{:S(2)}) copy-start(bf16[480,768]{1,0:T(8,128)(2,1)S(1)} %get-tuple-element.80.d1) | copy-start | bytes 2211844
  88.3 23.3 %copy-start.7 = (bf16[160,2048]{1,0:T(8,128)(2,1)}, bf16[160,2048]{1,0:T(8,128)(2,1)S(1)}, u32[]{:S(2)}) copy-start(bf16[160,2048]{1,0:T(8,128)(2,1)S(1)} %get-tuple-element.85.dy2) | copy-start | bytes 1966084
  88.3 23.2 %copy-start.8 = (bf16[160,768]{1,0:T(8,128)(2,1)}, bf16[160,768]{1,0:T(8,128)(2,1)S(1)}, u32[]{:S(2)}) copy-start(bf16[160,768]{1,0:T(8,128)(2,1)S(1)} %get-tuple-element.81.d2) | copy-start | bytes 737284
  88.4 12.6 %collective-permute-start.16 = (bf16[128,1408]{1,0:T(8,128)(2,1)S(1)}, bf16[128,1408]{1,0:T(8,128)(2,1)S(1)}, u32[]{:S(2)}, u32[]{:S(2)}) collective-permute-start(bf16[128,1408]{1,0:T(8,128)(2,1)S(1)} %get-tuple-element.78), channel_id=1, source_target_pairs={{0,64},{64,128},{128,192},{192,0},{1,65},{65,129},{129,193},{193,1... | collective-permute-start | bytes 1081352 | tf_op jit(solution)/shard_map/ppermute | solution.py:284
  89.8 21.8 %collective-permute-start.18 = (bf16[128,1408]{1,0:T(8,128)(2,1)S(1)}, bf16[128,1408]{1,0:T(8,128)(2,1)S(1)}, u32[]{:S(2)}, u32[]{:S(2)}) collective-permute-start(bf16[128,1408]{1,0:T(8,128)(2,1)S(1)} %get-tuple-element.79), channel_id=1, source_target_pairs={{0,64},{64,128},{128,192},{192,0},{1,65},{65,129},{129,193},{193,1... | collective-permute-start | bytes 1081352 | tf_op jit(solution)/shard_map/ppermute | solution.py:284
  91.3 11.4 %collective-permute-start.14 = (bf16[128,1408]{1,0:T(8,128)(2,1)S(1)}, bf16[128,1408]{1,0:T(8,128)(2,1)S(1)}, u32[]{:S(2)}, u32[]{:S(2)}) collective-permute-start(bf16[128,1408]{1,0:T(8,128)(2,1)S(1)} %get-tuple-element.76), channel_id=1, source_target_pairs={{0,192},{64,0},{128,64},{192,128},{1,193},{65,1},{129,65},{193,129... | collective-permute-start | bytes 1081352 | tf_op jit(solution)/shard_map/ppermute | solution.py:284
  93.0 18.6 %collective-permute-start.13 = (bf16[128,1408]{1,0:T(8,128)(2,1)S(1)}, bf16[128,1408]{1,0:T(8,128)(2,1)S(1)}, u32[]{:S(2)}, u32[]{:S(2)}) collective-permute-start(bf16[128,1408]{1,0:T(8,128)(2,1)S(1)} %get-tuple-element.67), channel_id=1, source_target_pairs={{0,192},{64,0},{128,64},{192,128},{1,193},{65,1},{129,65},{193,129... | collective-permute-start | bytes 1081352 | tf_op jit(solution)/shard_map/ppermute | solution.py:284
  101.1 10.5 %collective-permute-start.17 = (bf16[128,1408]{1,0:T(8,128)(2,1)S(1)}, bf16[128,1408]{1,0:T(8,128)(2,1)S(1)}, u32[]{:S(2)}, u32[]{:S(2)}) collective-permute-start(bf16[128,1408]{1,0:T(8,128)(2,1)S(1)} %add_convert_fusion.2), channel_id=1, source_target_pairs={{0,64},{64,128},{128,192},{192,0},{1,65},{65,129},{129,193},{193,1... | collective-permute-start | bytes 1081352 | tf_op jit(solution)/shard_map/ppermute | solution.py:284
  102.8 9.4 %collective-permute-start.15 = (bf16[128,1408]{1,0:T(8,128)(2,1)S(1)}, bf16[128,1408]{1,0:T(8,128)(2,1)S(1)}, u32[]{:S(2)}, u32[]{:S(2)}) collective-permute-start(bf16[128,1408]{1,0:T(8,128)(2,1)S(1)} %add_convert_fusion.3), channel_id=1, source_target_pairs={{0,192},{64,0},{128,64},{192,128},{1,193},{65,1},{129,65},{193,129... | collective-permute-start | bytes 1081352 | tf_op jit(solution)/shard_map/ppermute | solution.py:284
  111.6 11.6 %copy-start.3 = (bf16[480,384]{1,0:T(8,128)(2,1)S(1)}, bf16[480,384]{1,0:T(8,128)(2,1)}, u32[]{:S(2)}) copy-start(bf16[480,384]{1,0:T(8,128)(2,1)} %copy-done.2) | copy-start | bytes 1105924
  111.6 11.6 %copy-start.6 = (bf16[160,2048]{1,0:T(8,128)(2,1)S(1)}, bf16[160,2048]{1,0:T(8,128)(2,1)}, u32[]{:S(2)}) copy-start(bf16[160,2048]{1,0:T(8,128)(2,1)} %copy-done.5) | copy-start | bytes 1966084
  111.6 11.6 %copy-start.9 = (bf16[160,768]{1,0:T(8,128)(2,1)S(1)}, bf16[160,768]{1,0:T(8,128)(2,1)}, u32[]{:S(2)}) copy-start(bf16[160,768]{1,0:T(8,128)(2,1)} %copy-done.8) | copy-start | bytes 737284
  112.1 11.1 %collective-permute-start.19 = (bf16[576,2048]{1,0:T(8,128)(2,1)}, bf16[576,2048]{1,0:T(8,128)(2,1)}, u32[]{:S(2)}, u32[]{:S(2)}) collective-permute-start(bf16[576,2048]{1,0:T(8,128)(2,1)} %shard_map.125), channel_id=1, source_target_pairs={{0,32},{32,0},{1,33},{33,1},{2,34},{34,2},{3,35},{35,3},{4,36},{36... | collective-permute-start | bytes 7077896 | tf_op jit(solution)/shard_map/ppermute | solution.py:284
  113.3 31.5 %all-to-all-start.2 = ((bf16[32,8,1408]{2,1,0:T(8,128)(2,1)}), bf16[32,8,1408]{2,1,0:T(8,128)(2,1)S(1)}, u32[]{:S(2)}, u32[]{:S(2)}) async-start(bf16[32,8,1408]{2,1,0:T(8,128)(2,1)} %maximum_bitcast_fusion), calls=%async_computation.2 | async-start | bytes 1441792 | tf_op jit(solution)/shard_map/all_to_all | solution.py:308
  123.2 21.7 %copy-start.14 = (s32[128,1]{0,1:T(1,128)S(1)}, s32[128,1]{0,1:T(1,128)}, u32[]{:S(2)}) copy-start(s32[128,1]{0,1:T(1,128)} %param.10) | copy-start | bytes 1540
  123.2 21.7 %copy-start.15 = (bf16[128,1]{0,1:T(2,128)(2,1)S(1)}, bf16[128,1]{0,1:T(2,128)(2,1)}, u32[]{:S(2)}) copy-start(bf16[128,1]{0,1:T(2,128)(2,1)} %param.11) | copy-start | bytes 772

commit v5 on v4

--- a/solution.py
+++ b/solution.py
@@ -68,13 +68,12 @@
     def spread(target):
         return jnp.where(one_hot(rows, target), value, 0.0).astype(BF)
 
-    main = dot(spread(main_rows(expert, rank, 0)), src[:, :half])
-    main += dot(spread(main_rows(expert, rank, 1)), src[:, half:])
-    dst[:, :half] = main.astype(BF)
-    last = jnp.zeros((rows, piece), F32)
-    for k in range(8):
-        last += dot(spread(last_rows(expert, rank, k)), src[:, k * piece : (k + 1) * piece])
-    dst[:, half:] = last.astype(BF)
+    hot = jnp.concatenate([spread(main_rows(expert, rank, h)) for h in (0, 1)], axis=1)
+    stacked = jnp.concatenate([src[:, :half], src[:, half:]], axis=0)
+    dst[:, :half] = dot(hot, stacked).astype(BF)
+    hot = jnp.concatenate([spread(last_rows(expert, rank, k)) for k in range(8)], axis=1)
+    stacked = jnp.concatenate([src[:, k * piece : (k + 1) * piece] for k in range(8)], axis=0)
+    dst[:, half:] = dot(hot, stacked).astype(BF)
 
 
 def unpack_tokens(routes_ref, gates_ref, r_ref, out_ref, gate_ref):
@@ -86,11 +85,16 @@
     def spread(target):
         return jnp.where(one_hot(rows, target), 1.0, 0.0).astype(BF)
 
-    mains = [dot(spread(main_rows(expert, rank, h)), r_ref[:, :half], ACROSS) for h in (0, 1)]
+    count = out_ref.shape[0]
+    hot = jnp.concatenate([spread(main_rows(expert, rank, h)) for h in (0, 1)], axis=1)
+    mains = dot(hot, r_ref[:, :half], ACROSS)
+    hot = jnp.concatenate([spread(last_rows(expert, rank, k)) for k in range(8)], axis=1)
+    lasts = dot(hot, r_ref[:, half : half + piece], ACROSS)
     for k in range(8):
-        last = dot(spread(last_rows(expert, rank, k)), r_ref[:, half : half + piece], ACROSS)
         at = (k % 4) * piece
-        out_ref[:, k * piece : (k + 1) * piece] = (mains[k // 4][:, at : at + piece] + last).astype(BF)
+        main = mains[k // 4 * count : (k // 4 + 1) * count, at : at + piece]
+        last = lasts[k * count : (k + 1) * count]
+        out_ref[:, k * piece : (k + 1) * piece] = (main + last).astype(BF)
     lanes = r_ref[:, half + piece :]
     summed = dot(lanes, spread(expert * 8 + rank), ACROSS)
     gate_ref[...] = summed[0:1, :] / gates_ref[...].astype(F32)

time: 148 us -> 148 us (level)
  no operation moved by 1% of the time
where the time goes in v5:
time: 148 us; the launch traced here: 146 us
  starting transfers between devices  54.9 us (37%)
  waiting for transfers between devices  48.4 us (33%)
  Pallas kernels  32 us (22%)
  local copies, waits for them, and re-layouts  5.42 us (4%)
  other arithmetic  4.54 us (3%)
    all_to_all x3, waiting for transfers between devices, dispatch(): return lax.all_to_all(chunks, ('z', 'x'), 0, 0, tiled=True).reshape(v.shape)  31 us
    ppermute x20, starting transfers between devices, along(): return lax.ppermute(v, axis, [(i, (i + by) % size) for i in range(size)])  27.9 us
    all_to_all x3, starting transfers between devices, dispatch(): return lax.all_to_all(chunks, ('z', 'x'), 0, 0, tiled=True).reshape(v.shape)  27 us
    ppermute x20, waiting for transfers between devices, along(): return lax.ppermute(v, axis, [(i, (i + by) % size) for i in range(size)])  17.5 us
    pallas_call x2, Pallas kernels, call_grads(): pl.pallas_call(functools.partial(grad_block, own, bool(more), units), gri...  13.3 us
    pallas_call x2, Pallas kernels, call_x_part(): pl.pallas_call(functools.partial(x_part, [len(held) for held in xs]), out...  6.13 us
    pallas_call x2, Pallas kernels, call_dy_part(): pl.pallas_call(functools.partial(dy_part, [len(held) for held in dys]), o...  6.07 us
    pallas_call x2, Pallas kernels, pack(): pl.pallas_call(functools.partial(pack_tokens, len(operands) > 2), out_sha...  5.09 us
  transfers between devices with their start and end apart: 23, of which 9 were waited for; matrix products, arithmetic and copies ran while one was open for 5% of the time, Pallas kernels for 18%

profile of v5, /device:TPU:2, one launch (start us, length us, event | category | flops | bytes accessed | tf_op | source)
XLA Modules:
  0.0 146.2 jit_solution(5700787638019633276)
XLA Ops:
  0.7 2.6 %shard_map.119 = bf16[256,1280]{1,0:T(8,128)(2,1)} custom-call(s32[1,128]{1,0:T(1,128)} %bitcast.25, bf16[128,2048]{1,0:T(8,128)(2,1)} %refs_1_.1), custom_call_target="tpu_custom_call" | custom-call | tf_op jit(solution)/shard_map/pallas_call | solution.py:302
  3.2 11.6 %all-to-all-start = ((bf16[32,8,1280]{2,1,0:T(8,128)(2,1)}), bf16[32,8,1280]{2,1,0:T(8,128)(2,1)S(1)}, u32[]{:S(2)}, u32[]{:S(2)}) async-start(bf16[32,8,1280]{2,1,0:T(8,128)(2,1)} %bitcast.36), calls=%async_computation | async-start | bytes 1310720 | tf_op jit(solution)/shard_map/all_to_all | solution.py:312
  14.9 2.5 %shard_map.120 = bf16[256,1280]{1,0:T(8,128)(2,1)} custom-call(s32[1,128]{1,0:T(1,128)} %bitcast.26, bf16[1,128]{1,0:T(2,128)(2,1)} %bitcast.28, s32[1,128]{1,0:T(1,128)} %bitcast.37, bf16[128,2048]{1,0:T(8,128)(2,1)} %refs_3_.1), custom_call_target="tpu_custom_call" | custom-call | tf_op jit(solution)/shard_map/pallas_call | solution.py:302
  17.4 2.8 %pad_maximum_fusion.1 = bf16[576,2048]{1,0:T(8,128)(2,1)} fusion(bf16[192,2048]{1,0:T(8,128)(2,1)} %bitcast.34, bf16[192,2048]{1,0:T(8,128)(2,1)S(1)} %bitcast.30, bf16[192,2048]{1,0:T(8,128)(2,1)S(1)} %bitcast.32), kind=kLoop, calls=%fused_computation.1 | loop fusion | flops 7077888 | bytes 4718592 | tf_op jit(solution)/shard_map/concatenate | solution.py:319
  20.1 14.4 %all-to-all-done = bf16[32,8,1280]{2,1,0:T(8,128)(2,1)S(1)} async-done(((bf16[32,8,1280]{2,1,0:T(8,128)(2,1)}), bf16[32,8,1280]{2,1,0:T(8,128)(2,1)S(1)}, u32[]{:S(2)}, u32[]{:S(2)}) %all-to-all-start) | async-done | bytes 655392 | tf_op jit(solution)/shard_map/all_to_all | solution.py:312
  34.5 5.6 %all-to-all-start.1 = ((bf16[32,8,1280]{2,1,0:T(8,128)(2,1)}), bf16[32,8,1280]{2,1,0:T(8,128)(2,1)S(1)}, u32[]{:S(2)}, u32[]{:S(2)}) async-start(bf16[32,8,1280]{2,1,0:T(8,128)(2,1)} %bitcast.8), calls=%async_computation.1 | async-start | bytes 1310720 | tf_op jit(solution)/shard_map/all_to_all | solution.py:312
  40.1 0.9 fusion.1
  40.9 1.6 %collective-permute-start.1 = (bf16[128,1280]{1,0:T(8,128)(2,1)}, bf16[128,1280]{1,0:T(8,128)(2,1)}, u32[]{:S(2)}, u32[]{:S(2)}) collective-permute-start(bf16[128,1280]{1,0:T(8,128)(2,1)} %get-tuple-element.105), channel_id=1, source_target_pairs={{0,64},{64,128},{128,192},{192,0},{1,65},{65,129},{129,193},{193,1... | collective-permute-start | bytes 983048 | tf_op jit(solution)/shard_map/ppermute | solution.py:288
  42.5 1.7 %collective-permute-start.4 = (bf16[128,1280]{1,0:T(8,128)(2,1)}, bf16[128,1280]{1,0:T(8,128)(2,1)}, u32[]{:S(2)}, u32[]{:S(2)}) collective-permute-start(bf16[128,1280]{1,0:T(8,128)(2,1)} %get-tuple-element.104), channel_id=1, source_target_pairs={{0,192},{64,0},{128,64},{192,128},{1,193},{65,1},{129,65},{193,129... | collective-permute-start | bytes 983048 | tf_op jit(solution)/shard_map/ppermute | solution.py:288
  44.2 0.4 collective-permute-start.2
  44.5 2.9 %collective-permute-start.3 = (bf16[128,1280]{1,0:T(8,128)(2,1)}, bf16[128,1280]{1,0:T(8,128)(2,1)S(1)}, u32[]{:S(2)}, u32[]{:S(2)}) collective-permute-start(bf16[128,1280]{1,0:T(8,128)(2,1)} %get-tuple-element.105), channel_id=1, source_target_pairs={{0,192},{64,0},{128,64},{192,128},{1,193},{65,1},{129,65},{193,129... | collective-permute-start | bytes 983048 | tf_op jit(solution)/shard_map/ppermute | solution.py:288
  47.4 5.7 %collective-permute-done.1.refs_1_ = bf16[128,1280]{1,0:T(8,128)(2,1)} collective-permute-done((bf16[128,1280]{1,0:T(8,128)(2,1)}, bf16[128,1280]{1,0:T(8,128)(2,1)}, u32[]{:S(2)}, u32[]{:S(2)}) %collective-permute-start.1) | collective-permute-done | bytes 327712 | tf_op jit(solution)/shard_map/ppermute | solution.py:288
  53.1 0.4 collective-permute-start.6
  53.5 2.9 %collective-permute-start.7 = (bf16[128,1280]{1,0:T(8,128)(2,1)}, bf16[128,1280]{1,0:T(8,128)(2,1)}, u32[]{:S(2)}, u32[]{:S(2)}) collective-permute-start(bf16[128,1280]{1,0:T(8,128)(2,1)} %collective-permute-done.4.refs_4_), channel_id=1, source_target_pairs={{0,192},{64,0},{128,64},{192,128},{1,193},{65,1},{129,65},{193,129... | collective-permute-start | bytes 983048 | tf_op jit(solution)/shard_map/ppermute | solution.py:288
  56.4 2.4 %all-to-all-done.1 = bf16[32,8,1280]{2,1,0:T(8,128)(2,1)S(1)} async-done(((bf16[32,8,1280]{2,1,0:T(8,128)(2,1)}), bf16[32,8,1280]{2,1,0:T(8,128)(2,1)S(1)}, u32[]{:S(2)}, u32[]{:S(2)}) %all-to-all-start.1) | async-done | bytes 655392 | tf_op jit(solution)/shard_map/all_to_all | solution.py:312
  58.8 1.3 collective-permute-done.2.refs_2_
  60.0 0.4 collective-permute-start
  60.4 2.8 %collective-permute-start.10 = (bf16[128,1280]{1,0:T(8,128)(2,1)S(1)}, bf16[128,1280]{1,0:T(8,128)(2,1)S(1)}, u32[]{:S(2)}, u32[]{:S(2)}) collective-permute-start(bf16[128,1280]{1,0:T(8,128)(2,1)S(1)} %get-tuple-element.60), channel_id=1, source_target_pairs={{0,192},{64,0},{128,64},{192,128},{1,193},{65,1},{129,65},{193,129... | collective-permute-start | bytes 983048 | tf_op jit(solution)/shard_map/ppermute | solution.py:288
  63.3 1.8 %fusion = (bf16[192,2048]{1,0:T(8,128)(2,1)S(1)}, bf16[192,2048]{1,0:T(8,128)(2,1)S(1)}, bf16[192,2048]{1,0:T(8,128)(2,1)S(1)}) fusion(bf16[576,2048]{1,0:T(8,128)(2,1)} %collective-permute-done.5), kind=kLoop, calls=%fused_computation.10 | loop fusion | bytes 4718592 | tf_op jit(solution)/shard_map/slice | solution.py:320
  65.0 0.3 pad_maximum_fusion.refs_5_.refs_8_.refs_2_
  65.4 0.7 copy-done.12
  66.1 1.0 copy-done.11
  67.1 1.0 copy-done.13
  68.0 3.5 %shard_map.121 = (bf16[480,2048]{1,0:T(8,128)(2,1)S(1)}, bf16[480,384]{1,0:T(8,128)(2,1)S(1)}, f32[480,384]{1,0:T(8,128)S(1)}, f32[480,384]{1,0:T(8,128)S(1)}) custom-call(bf16[256,1280]{1,0:T(8,128)(2,1)S(1)} %bitcast.23, bf16[128,1280]{1,0:T(8,128)(2,1)} %collective-permute-done.1.refs_1_, bf16[128,1280]{1,0:T(8,128)(2,1)S(1)} %copy-done.11, ...), custom_call_target="tpu_custom_call" | custom-call | flops 1000 | bytes 1000 | tf_op jit(solution)/shard_map/pallas_call | solution.py:182
  71.7 3.2 %collective-permute-start.9 = (bf16[128,1280]{1,0:T(8,128)(2,1)S(1)}, bf16[128,1280]{1,0:T(8,128)(2,1)S(1)}, u32[]{:S(2)}, u32[]{:S(2)}) collective-permute-start(bf16[128,1280]{1,0:T(8,128)(2,1)S(1)} %get-tuple-element.61), channel_id=1, source_target_pairs={{0,192},{64,0},{128,64},{192,128},{1,193},{65,1},{129,65},{193,129... | collective-permute-start | bytes 983048 | tf_op jit(solution)/shard_map/ppermute | solution.py:288
  74.9 3.2 %collective-permute-start.12 = (bf16[128,1280]{1,0:T(8,128)(2,1)S(1)}, bf16[128,1280]{1,0:T(8,128)(2,1)S(1)}, u32[]{:S(2)}, u32[]{:S(2)}) collective-permute-start(bf16[128,1280]{1,0:T(8,128)(2,1)S(1)} %collective-permute-done.10.refs_4_), channel_id=1, source_target_pairs={{0,192},{64,0},{128,64},{192,128},{1,193},{65,1},{129,65},{193,129... | collective-permute-start | bytes 983048 | tf_op jit(solution)/shard_map/ppermute | solution.py:288
  78.1 0.1 pad_maximum_fusion.2.refs_9_.refs_6_
  78.2 2.6 %shard_map.123 = (bf16[160,2048]{1,0:T(8,128)(2,1)S(1)}, bf16[160,384]{1,0:T(8,128)(2,1)S(1)}, f32[160,384]{1,0:T(8,128)S(1)}, f32[160,384]{1,0:T(8,128)S(1)}) custom-call(bf16[128,1280]{1,0:T(8,128)(2,1)} %collective-permute-done.6.refs_0_, bf16[128,1280]{1,0:T(8,128)(2,1)} %collective-permute-done.7.refs_1_, ...), custom_call_target="tpu_custom_call" | custom-call | flops 1000 | bytes 1000 | tf_op jit(solution)/shard_map/pallas_call | solution.py:182
  80.9 1.0 collective-permute-done.8.refs_2_
  82.0 4.2 %shard_map.122 = (bf16[128,1408]{1,0:T(8,128)(2,1)S(1)}, bf16[128,1408]{1,0:T(8,128)(2,1)S(1)}, bf16[128,1408]{1,0:T(8,128)(2,1)S(1)}, bf16[128,1408]{1,0:T(8,12...) custom-call(bf16[256,1280]{1,0:T(8,128)(2,1)S(1)} %bitcast.21, ...), custom_call_target="tpu_custom_call" | custom-call | flops 1000 | bytes 1000 | tf_op jit(solution)/shard_map/pallas_call | solution.py:234
  86.2 1.9 %shard_map.124 = (bf16[128,1408]{1,0:T(8,128)(2,1)S(1)}, bf16[128,1408]{1,0:T(8,128)(2,1)S(1)}, bf16[160,2048]{1,0:T(8,128)(2,1)S(1)}, bf16[160,768]{1,0:T(8,128)(2,1)S(1)}) custom-call(bf16[128,1280]{1,0:T(8,128)(2,1)S(1)} %collective-permute-done.11.refs_0_, bf16[128,1280]{1,0:T(8,128)(2,1)S(1)} %collective-permute-done.12.refs_1_, ...), custom_call_target="tpu_custom_call" | custom-call | flops 1000 | bytes 1000 | tf_op jit(solution)/shard_map/pallas_call | solution.py:234
  88.1 1.2 collective-permute-start.16
  89.3 1.7 %collective-permute-start.18 = (bf16[128,1408]{1,0:T(8,128)(2,1)S(1)}, bf16[128,1408]{1,0:T(8,128)(2,1)S(1)}, u32[]{:S(2)}, u32[]{:S(2)}) collective-permute-start(bf16[128,1408]{1,0:T(8,128)(2,1)S(1)} %get-tuple-element.79), channel_id=1, source_target_pairs={{0,64},{64,128},{128,192},{192,0},{1,65},{65,129},{129,193},{193,1... | collective-permute-start | bytes 1081352 | tf_op jit(solution)/shard_map/ppermute | solution.py:288
  91.0 1.5 %collective-permute-start.14 = (bf16[128,1408]{1,0:T(8,128)(2,1)S(1)}, bf16[128,1408]{1,0:T(8,128)(2,1)S(1)}, u32[]{:S(2)}, u32[]{:S(2)}) collective-permute-start(bf16[128,1408]{1,0:T(8,128)(2,1)S(1)} %get-tuple-element.76), channel_id=1, source_target_pairs={{0,192},{64,0},{128,64},{192,128},{1,193},{65,1},{129,65},{193,129... | collective-permute-start | bytes 1081352 | tf_op jit(solution)/shard_map/ppermute | solution.py:288
  92.5 0.9 collective-permute-start.13
  93.4 7.3 %collective-permute-done.16 = bf16[128,1408]{1,0:T(8,128)(2,1)S(1)} collective-permute-done((bf16[128,1408]{1,0:T(8,128)(2,1)S(1)}, bf16[128,1408]{1,0:T(8,128)(2,1)S(1)}, u32[]{:S(2)}, u32[]{:S(2)}) %collective-permute-start.16) | collective-permute-done | bytes 360480 | tf_op jit(solution)/shard_map/ppermute | solution.py:288
  100.7 0.1 add_convert_fusion.2
  100.8 0.3 collective-permute-start.17
  101.1 1.3 collective-permute-done.14
  102.5 2.8 %collective-permute-start.15 = (bf16[128,1408]{1,0:T(8,128)(2,1)S(1)}, bf16[128,1408]{1,0:T(8,128)(2,1)S(1)}, u32[]{:S(2)}, u32[]{:S(2)}) collective-permute-start(bf16[128,1408]{1,0:T(8,128)(2,1)S(1)} %add_convert_fusion.3), channel_id=1, source_target_pairs={{0,192},{64,0},{128,64},{192,128},{1,193},{65,1},{129,65},{193,129... | collective-permute-start | bytes 1081352 | tf_op jit(solution)/shard_map/ppermute | solution.py:288
  105.3 5.8 %shard_map.125 = bf16[576,2048]{1,0:T(8,128)(2,1)} custom-call(bf16[480,384]{1,0:T(8,128)(2,1)S(1)} %get-tuple-element.62.refs_5_.hid1, bf16[160,384]{1,0:T(8,128)(2,1)S(1)} %get-tuple-element.73.refs_2_.hid2, bf16[480,768]{1,0:T(8,128)(2,1)S(1)} %get-tuple-element.80.d1, bf16[160,768]{1,0:T(8,128)(2,1)S(1)} %get-tuple-element.81.d2, ...), custom_call_target="tpu_custom_call" | custom-call | flops 1000 | bytes 1000 | tf_op jit(solution)/shard_map/pallas_call | solution.py:270
  111.2 0.9 collective-permute-done.15
  112.0 0.3 add_convert_fusion
  112.3 1.0 maximum_bitcast_fusion
  113.3 9.8 %all-to-all-start.2 = ((bf16[32,8,1408]{2,1,0:T(8,128)(2,1)}), bf16[32,8,1408]{2,1,0:T(8,128)(2,1)S(1)}, u32[]{:S(2)}, u32[]{:S(2)}) async-start(bf16[32,8,1408]{2,1,0:T(8,128)(2,1)} %maximum_bitcast_fusion), calls=%async_computation.2 | async-start | bytes 1441792 | tf_op jit(solution)/shard_map/all_to_all | solution.py:312
  123.2 7.4 %shard_map.126 = (bf16[192,2048]{1,0:T(8,128)(2,1)}, bf16[192,2048]{1,0:T(8,128)(2,1)}, bf16[192,2048]{1,0:T(8,128)(2,1)}) custom-call(bf16[480,384]{1,0:T(8,128)(2,1)S(1)} %copy-done.3, bf16[160,384]{1,0:T(8,128)(2,1)S(1)} %get-tuple-element.73.refs_2_.hid2, bf16[480,768]{1,0:T(8,128)(2,1)} %copy-done.4, bf16[160,768]{1,0:T(8,128)(2,1)S(1)} %copy-done.9, ...), custom_call_target="tpu_custom_call" | custom-call | flops 1000 | bytes 1000 | tf_op jit(solution)/shard_map/pallas_call | solution.py:270
  130.6 14.2 %all-to-all-done.2 = bf16[32,8,1408]{2,1,0:T(8,128)(2,1)S(1)} async-done(((bf16[32,8,1408]{2,1,0:T(8,128)(2,1)}), bf16[32,8,1408]{2,1,0:T(8,128)(2,1)S(1)}, u32[]{:S(2)}, u32[]{:S(2)}) %all-to-all-start.2) | async-done | bytes 720928 | tf_op jit(solution)/shard_map/all_to_all | solution.py:312
  144.8 1.4 shard_map.127
  (55 shorter events, 0.4 us)
Async XLA Ops:
  0.6 16.7 %copy-start.17 = (bf16[1,192,2048]{2,1,0:T(8,128)(2,1)S(1)}, bf16[1,192,2048]{2,1,0:T(8,128)(2,1)}, u32[]{:S(2)}) copy-start(bf16[1,192,2048]{2,1,0:T(8,128)(2,1)} %param.13) | copy-start | bytes 2359300
  0.6 16.7 %copy-start.16 = (bf16[1,192,2048]{2,1,0:T(8,128)(2,1)S(1)}, bf16[1,192,2048]{2,1,0:T(8,128)(2,1)}, u32[]{:S(2)}) copy-start(bf16[1,192,2048]{2,1,0:T(8,128)(2,1)} %param.14) | copy-start | bytes 2359300
  3.2 31.2 %all-to-all-start = ((bf16[32,8,1280]{2,1,0:T(8,128)(2,1)}), bf16[32,8,1280]{2,1,0:T(8,128)(2,1)S(1)}, u32[]{:S(2)}, u32[]{:S(2)}) async-start(bf16[32,8,1280]{2,1,0:T(8,128)(2,1)} %bitcast.36), calls=%async_computation | async-start | bytes 1310720 | tf_op jit(solution)/shard_map/all_to_all | solution.py:312
  20.1 40.3 %collective-permute-start.5 = (bf16[576,2048]{1,0:T(8,128)(2,1)}, bf16[576,2048]{1,0:T(8,128)(2,1)}, u32[]{:S(2)}, u32[]{:S(2)}) collective-permute-start(bf16[576,2048]{1,0:T(8,128)(2,1)} %pad_maximum_fusion.1), channel_id=1, source_target_pairs={{0,32},{32,0},{1,33},{33,1},{2,34},{34,2},{3,35},{35,3},{4,36},{36... | collective-permute-start | bytes 7077896 | tf_op jit(solution)/shard_map/ppermute | solution.py:288
  34.5 24.2 %all-to-all-start.1 = ((bf16[32,8,1280]{2,1,0:T(8,128)(2,1)}), bf16[32,8,1280]{2,1,0:T(8,128)(2,1)S(1)}, u32[]{:S(2)}, u32[]{:S(2)}) async-start(bf16[32,8,1280]{2,1,0:T(8,128)(2,1)} %bitcast.8), calls=%async_computation.1 | async-start | bytes 1310720 | tf_op jit(solution)/shard_map/all_to_all | solution.py:312
  40.9 12.2 %collective-permute-start.1 = (bf16[128,1280]{1,0:T(8,128)(2,1)}, bf16[128,1280]{1,0:T(8,128)(2,1)}, u32[]{:S(2)}, u32[]{:S(2)}) collective-permute-start(bf16[128,1280]{1,0:T(8,128)(2,1)} %get-tuple-element.105), channel_id=1, source_target_pairs={{0,64},{64,128},{128,192},{192,0},{1,65},{65,129},{129,193},{193,1... | collective-permute-start | bytes 983048 | tf_op jit(solution)/shard_map/ppermute | solution.py:288
  42.5 11.0 %collective-permute-start.4 = (bf16[128,1280]{1,0:T(8,128)(2,1)}, bf16[128,1280]{1,0:T(8,128)(2,1)}, u32[]{:S(2)}, u32[]{:S(2)}) collective-permute-start(bf16[128,1280]{1,0:T(8,128)(2,1)} %get-tuple-element.104), channel_id=1, source_target_pairs={{0,192},{64,0},{128,64},{192,128},{1,193},{65,1},{129,65},{193,129... | collective-permute-start | bytes 983048 | tf_op jit(solution)/shard_map/ppermute | solution.py:288
  44.2 15.9 %collective-permute-start.2 = (bf16[128,1280]{1,0:T(8,128)(2,1)}, bf16[128,1280]{1,0:T(8,128)(2,1)S(1)}, u32[]{:S(2)}, u32[]{:S(2)}) collective-permute-start(bf16[128,1280]{1,0:T(8,128)(2,1)} %get-tuple-element.104), channel_id=1, source_target_pairs={{0,64},{64,128},{128,192},{192,0},{1,65},{65,129},{129,193},{193,1... | collective-permute-start | bytes 983048 | tf_op jit(solution)/shard_map/ppermute | solution.py:288
  44.5 20.8 %collective-permute-start.3 = (bf16[128,1280]{1,0:T(8,128)(2,1)}, bf16[128,1280]{1,0:T(8,128)(2,1)S(1)}, u32[]{:S(2)}, u32[]{:S(2)}) collective-permute-start(bf16[128,1280]{1,0:T(8,128)(2,1)} %get-tuple-element.105), channel_id=1, source_target_pairs={{0,192},{64,0},{128,64},{192,128},{1,193},{65,1},{129,65},{193,129... | collective-permute-start | bytes 983048 | tf_op jit(solution)/shard_map/ppermute | solution.py:288
  53.1 18.4 %collective-permute-start.6 = (bf16[128,1280]{1,0:T(8,128)(2,1)}, bf16[128,1280]{1,0:T(8,128)(2,1)}, u32[]{:S(2)}, u32[]{:S(2)}) collective-permute-start(bf16[128,1280]{1,0:T(8,128)(2,1)} %collective-permute-done.1.refs_1_), channel_id=1, source_target_pairs={{0,64},{64,128},{128,192},{192,0},{1,65},{65,129},{129,193},{193,1... | collective-permute-start | bytes 983048 | tf_op jit(solution)/shard_map/ppermute | solution.py:288
  53.5 18.1 %collective-permute-start.7 = (bf16[128,1280]{1,0:T(8,128)(2,1)}, bf16[128,1280]{1,0:T(8,128)(2,1)}, u32[]{:S(2)}, u32[]{:S(2)}) collective-permute-start(bf16[128,1280]{1,0:T(8,128)(2,1)} %collective-permute-done.4.refs_4_), channel_id=1, source_target_pairs={{0,192},{64,0},{128,64},{192,128},{1,193},{65,1},{129,65},{193,129... | collective-permute-start | bytes 983048 | tf_op jit(solution)/shard_map/ppermute | solution.py:288
  60.0 5.3 %copy-start.10 = (bf16[128,1280]{1,0:T(8,128)(2,1)}, bf16[128,1280]{1,0:T(8,128)(2,1)S(1)}, u32[]{:S(2)}) copy-start(bf16[128,1280]{1,0:T(8,128)(2,1)S(1)} %collective-permute-done.2.refs_2_) | copy-start | bytes 983044
  60.0 14.9 %collective-permute-start = (bf16[128,1280]{1,0:T(8,128)(2,1)S(1)}, bf16[128,1280]{1,0:T(8,128)(2,1)S(1)}, u32[]{:S(2)}, u32[]{:S(2)}) collective-permute-start(bf16[128,1280]{1,0:T(8,128)(2,1)S(1)} %get-tuple-element.61), channel_id=1, source_target_pairs={{0,64},{64,128},{128,192},{192,0},{1,65},{65,129},{129,193},{193,1... | collective-permute-start | bytes 983048 | tf_op jit(solution)/shard_map/ppermute | solution.py:288
  60.4 14.5 %collective-permute-start.10 = (bf16[128,1280]{1,0:T(8,128)(2,1)S(1)}, bf16[128,1280]{1,0:T(8,128)(2,1)S(1)}, u32[]{:S(2)}, u32[]{:S(2)}) collective-permute-start(bf16[128,1280]{1,0:T(8,128)(2,1)S(1)} %get-tuple-element.60), channel_id=1, source_target_pairs={{0,192},{64,0},{128,64},{192,128},{1,193},{65,1},{129,65},{193,129... | collective-permute-start | bytes 983048 | tf_op jit(solution)/shard_map/ppermute | solution.py:288
  65.4 0.7 copy-start.12
  66.1 1.0 copy-start.11
  67.1 1.0 copy-start.13
  68.0 10.1 %copy-start.18 = (bf16[1,192,2048]{2,1,0:T(8,128)(2,1)S(1)}, bf16[1,192,2048]{2,1,0:T(8,128)(2,1)}, u32[]{:S(2)}) copy-start(bf16[1,192,2048]{2,1,0:T(8,128)(2,1)} %param.15) | copy-start | bytes 2359300
  71.5 33.7 %copy-start = (bf16[480,2048]{1,0:T(8,128)(2,1)}, bf16[480,2048]{1,0:T(8,128)(2,1)S(1)}, u32[]{:S(2)}) copy-start(bf16[480,2048]{1,0:T(8,128)(2,1)S(1)} %get-tuple-element.82.x1) | copy-start | bytes 5898244
  71.5 33.7 %copy-start.2 = (bf16[480,384]{1,0:T(8,128)(2,1)}, bf16[480,384]{1,0:T(8,128)(2,1)S(1)}, u32[]{:S(2)}) copy-start(bf16[480,384]{1,0:T(8,128)(2,1)S(1)} %get-tuple-element.62.refs_5_.hid1) | copy-start | bytes 1105924
  71.6 10.4 %collective-permute-start.8 = (bf16[128,1280]{1,0:T(8,128)(2,1)S(1)}, bf16[128,1280]{1,0:T(8,128)(2,1)S(1)}, u32[]{:S(2)}, u32[]{:S(2)}) collective-permute-start(bf16[128,1280]{1,0:T(8,128)(2,1)S(1)} %get-tuple-element.60), channel_id=1, source_target_pairs={{0,64},{64,128},{128,192},{192,0},{1,65},{65,129},{129,193},{193,1... | collective-permute-start | bytes 983048 | tf_op jit(solution)/shard_map/ppermute | solution.py:288
  71.7 10.3 %collective-permute-start.9 = (bf16[128,1280]{1,0:T(8,128)(2,1)S(1)}, bf16[128,1280]{1,0:T(8,128)(2,1)S(1)}, u32[]{:S(2)}, u32[]{:S(2)}) collective-permute-start(bf16[128,1280]{1,0:T(8,128)(2,1)S(1)} %get-tuple-element.61), channel_id=1, source_target_pairs={{0,192},{64,0},{128,64},{192,128},{1,193},{65,1},{129,65},{193,129... | collective-permute-start | bytes 983048 | tf_op jit(solution)/shard_map/ppermute | solution.py:288
  74.9 11.3 %collective-permute-start.11 = (bf16[128,1280]{1,0:T(8,128)(2,1)S(1)}, bf16[128,1280]{1,0:T(8,128)(2,1)S(1)}, u32[]{:S(2)}, u32[]{:S(2)}) collective-permute-start(bf16[128,1280]{1,0:T(8,128)(2,1)S(1)} %collective-permute-done.refs_1_), channel_id=1, source_target_pairs={{0,64},{64,128},{128,192},{192,0},{1,65},{65,129},{129,193},{193,1... | collective-permute-start | bytes 983048 | tf_op jit(solution)/shard_map/ppermute | solution.py:288
  74.9 11.3 %collective-permute-start.12 = (bf16[128,1280]{1,0:T(8,128)(2,1)S(1)}, bf16[128,1280]{1,0:T(8,128)(2,1)S(1)}, u32[]{:S(2)}, u32[]{:S(2)}) collective-permute-start(bf16[128,1280]{1,0:T(8,128)(2,1)S(1)} %collective-permute-done.10.refs_4_), channel_id=1, source_target_pairs={{0,192},{64,0},{128,64},{192,128},{1,193},{65,1},{129,65},{193,129... | collective-permute-start | bytes 983048 | tf_op jit(solution)/shard_map/ppermute | solution.py:288
  80.9 24.4 %copy-start.5 = (bf16[160,2048]{1,0:T(8,128)(2,1)}, bf16[160,2048]{1,0:T(8,128)(2,1)S(1)}, u32[]{:S(2)}) copy-start(bf16[160,2048]{1,0:T(8,128)(2,1)S(1)} %get-tuple-element.83.x2) | copy-start | bytes 1966084
  86.1 19.1 %copy-start.1 = (bf16[480,2048]{1,0:T(8,128)(2,1)}, bf16[480,2048]{1,0:T(8,128)(2,1)S(1)}, u32[]{:S(2)}) copy-start(bf16[480,2048]{1,0:T(8,128)(2,1)S(1)} %get-tuple-element.84.dy1) | copy-start | bytes 5898244
  86.1 19.1 %copy-start.4 = (bf16[480,768]{1,0:T(8,128)(2,1)}, bf16[480,768]{1,0:T(8,128)(2,1)S(1)}, u32[]{:S(2)}) copy-start(bf16[480,768]{1,0:T(8,128)(2,1)S(1)} %get-tuple-element.80.d1) | copy-start | bytes 2211844
  88.1 23.1 %copy-start.7 = (bf16[160,2048]{1,0:T(8,128)(2,1)}, bf16[160,2048]{1,0:T(8,128)(2,1)S(1)}, u32[]{:S(2)}) copy-start(bf16[160,2048]{1,0:T(8,128)(2,1)S(1)} %get-tuple-element.85.dy2) | copy-start | bytes 1966084
  88.1 23.1 %copy-start.8 = (bf16[160,768]{1,0:T(8,128)(2,1)}, bf16[160,768]{1,0:T(8,128)(2,1)S(1)}, u32[]{:S(2)}) copy-start(bf16[160,768]{1,0:T(8,128)(2,1)S(1)} %get-tuple-element.81.d2) | copy-start | bytes 737284
  88.1 12.6 %collective-permute-start.16 = (bf16[128,1408]{1,0:T(8,128)(2,1)S(1)}, bf16[128,1408]{1,0:T(8,128)(2,1)S(1)}, u32[]{:S(2)}, u32[]{:S(2)}) collective-permute-start(bf16[128,1408]{1,0:T(8,128)(2,1)S(1)} %get-tuple-element.78), channel_id=1, source_target_pairs={{0,64},{64,128},{128,192},{192,0},{1,65},{65,129},{129,193},{193,1... | collective-permute-start | bytes 1081352 | tf_op jit(solution)/shard_map/ppermute | solution.py:288
  89.3 21.9 %collective-permute-start.18 = (bf16[128,1408]{1,0:T(8,128)(2,1)S(1)}, bf16[128,1408]{1,0:T(8,128)(2,1)S(1)}, u32[]{:S(2)}, u32[]{:S(2)}) collective-permute-start(bf16[128,1408]{1,0:T(8,128)(2,1)S(1)} %get-tuple-element.79), channel_id=1, source_target_pairs={{0,64},{64,128},{128,192},{192,0},{1,65},{65,129},{129,193},{193,1... | collective-permute-start | bytes 1081352 | tf_op jit(solution)/shard_map/ppermute | solution.py:288
  91.0 11.4 %collective-permute-start.14 = (bf16[128,1408]{1,0:T(8,128)(2,1)S(1)}, bf16[128,1408]{1,0:T(8,128)(2,1)S(1)}, u32[]{:S(2)}, u32[]{:S(2)}) collective-permute-start(bf16[128,1408]{1,0:T(8,128)(2,1)S(1)} %get-tuple-element.76), channel_id=1, source_target_pairs={{0,192},{64,0},{128,64},{192,128},{1,193},{65,1},{129,65},{193,129... | collective-permute-start | bytes 1081352 | tf_op jit(solution)/shard_map/ppermute | solution.py:288
  92.5 18.6 %collective-permute-start.13 = (bf16[128,1408]{1,0:T(8,128)(2,1)S(1)}, bf16[128,1408]{1,0:T(8,128)(2,1)S(1)}, u32[]{:S(2)}, u32[]{:S(2)}) collective-permute-start(bf16[128,1408]{1,0:T(8,128)(2,1)S(1)} %get-tuple-element.67), channel_id=1, source_target_pairs={{0,192},{64,0},{128,64},{192,128},{1,193},{65,1},{129,65},{193,129... | collective-permute-start | bytes 1081352 | tf_op jit(solution)/shard_map/ppermute | solution.py:288
  100.8 10.4 %collective-permute-start.17 = (bf16[128,1408]{1,0:T(8,128)(2,1)S(1)}, bf16[128,1408]{1,0:T(8,128)(2,1)S(1)}, u32[]{:S(2)}, u32[]{:S(2)}) collective-permute-start(bf16[128,1408]{1,0:T(8,128)(2,1)S(1)} %add_convert_fusion.2), channel_id=1, source_target_pairs={{0,64},{64,128},{128,192},{192,0},{1,65},{65,129},{129,193},{193,1... | collective-permute-start | bytes 1081352 | tf_op jit(solution)/shard_map/ppermute | solution.py:288
  102.5 9.6 %collective-permute-start.15 = (bf16[128,1408]{1,0:T(8,128)(2,1)S(1)}, bf16[128,1408]{1,0:T(8,128)(2,1)S(1)}, u32[]{:S(2)}, u32[]{:S(2)}) collective-permute-start(bf16[128,1408]{1,0:T(8,128)(2,1)S(1)} %add_convert_fusion.3), channel_id=1, source_target_pairs={{0,192},{64,0},{128,64},{192,128},{1,193},{65,1},{129,65},{193,129... | collective-permute-start | bytes 1081352 | tf_op jit(solution)/shard_map/ppermute | solution.py:288
  111.1 12.0 %copy-start.3 = (bf16[480,384]{1,0:T(8,128)(2,1)S(1)}, bf16[480,384]{1,0:T(8,128)(2,1)}, u32[]{:S(2)}) copy-start(bf16[480,384]{1,0:T(8,128)(2,1)} %copy-done.2) | copy-start | bytes 1105924
  111.1 12.0 %copy-start.6 = (bf16[160,2048]{1,0:T(8,128)(2,1)S(1)}, bf16[160,2048]{1,0:T(8,128)(2,1)}, u32[]{:S(2)}) copy-start(bf16[160,2048]{1,0:T(8,128)(2,1)} %copy-done.5) | copy-start | bytes 1966084
  111.2 12.0 %copy-start.9 = (bf16[160,768]{1,0:T(8,128)(2,1)S(1)}, bf16[160,768]{1,0:T(8,128)(2,1)}, u32[]{:S(2)}) copy-start(bf16[160,768]{1,0:T(8,128)(2,1)} %copy-done.8) | copy-start | bytes 737284
  112.0 11.1 %collective-permute-start.19 = (bf16[576,2048]{1,0:T(8,128)(2,1)}, bf16[576,2048]{1,0:T(8,128)(2,1)}, u32[]{:S(2)}, u32[]{:S(2)}) collective-permute-start(bf16[576,2048]{1,0:T(8,128)(2,1)} %shard_map.125), channel_id=1, source_target_pairs={{0,32},{32,0},{1,33},{33,1},{2,34},{34,2},{3,35},{35,3},{4,36},{36... | collective-permute-start | bytes 7077896 | tf_op jit(solution)/shard_map/ppermute | solution.py:288
  113.3 31.5 %all-to-all-start.2 = ((bf16[32,8,1408]{2,1,0:T(8,128)(2,1)}), bf16[32,8,1408]{2,1,0:T(8,128)(2,1)S(1)}, u32[]{:S(2)}, u32[]{:S(2)}) async-start(bf16[32,8,1408]{2,1,0:T(8,128)(2,1)} %maximum_bitcast_fusion), calls=%async_computation.2 | async-start | bytes 1441792 | tf_op jit(solution)/shard_map/all_to_all | solution.py:312
  123.1 21.7 %copy-start.14 = (s32[128,1]{0,1:T(1,128)S(1)}, s32[128,1]{0,1:T(1,128)}, u32[]{:S(2)}) copy-start(s32[128,1]{0,1:T(1,128)} %param.10) | copy-start | bytes 1540
  123.1 21.7 %copy-start.15 = (bf16[128,1]{0,1:T(2,128)(2,1)S(1)}, bf16[128,1]{0,1:T(2,128)(2,1)}, u32[]{:S(2)}) copy-start(bf16[128,1]{0,1:T(2,128)(2,1)} %param.11) | copy-start | bytes 772

commit v6 on v4

--- a/solution.py
+++ b/solution.py
@@ -272,7 +272,7 @@
         + [piece(3 * units)] * len(more),
         out_specs=out_specs,
         compiler_params=params(52 if more else 14),
-        cost_estimate=pl.CostEstimate(flops=1000, bytes_accessed=1000, transcendentals=0),
+        cost_estimate=pl.CostEstimate(flops=1000 if more else 7680 * units * width, bytes_accessed=1000, transcendentals=0),
     )(*acts, *rows, *more)
 
 

time: 148 us -> 148 us (level)
  no operation moved by 1% of the time
where the time goes in v6:
time: 148 us; the launch traced here: 146 us
  starting transfers between devices  55.4 us (37%)
  waiting for transfers between devices  47.5 us (32%)
  Pallas kernels  32.5 us (22%)
  local copies, waits for them, and re-layouts  5.42 us (4%)
  other arithmetic  4.54 us (3%)
    all_to_all x3, waiting for transfers between devices, dispatch(): return lax.all_to_all(chunks, ('z', 'x'), 0, 0, tiled=True).reshape(v.shape)  30.7 us
    ppermute x20, starting transfers between devices, along(): return lax.ppermute(v, axis, [(i, (i + by) % size) for i in range(size)])  28.4 us
    all_to_all x3, starting transfers between devices, dispatch(): return lax.all_to_all(chunks, ('z', 'x'), 0, 0, tiled=True).reshape(v.shape)  27 us
    ppermute x20, waiting for transfers between devices, along(): return lax.ppermute(v, axis, [(i, (i + by) % size) for i in range(size)])  16.8 us
    pallas_call x2, Pallas kernels, call_grads(): pl.pallas_call(functools.partial(grad_block, own, bool(more), units), gri...  13.3 us
    pallas_call x2, Pallas kernels, call_x_part(): pl.pallas_call(functools.partial(x_part, [len(held) for held in xs]), out...  6.13 us
    pallas_call x2, Pallas kernels, call_dy_part(): pl.pallas_call(functools.partial(dy_part, [len(held) for held in dys]), o...  6.06 us
    pallas_call x2, Pallas kernels, pack(): pl.pallas_call(functools.partial(pack_tokens, len(operands) > 2), out_sha...  5.61 us
  transfers between devices with their start and end apart: 23, of which 9 were waited for; matrix products, arithmetic and copies ran while one was open for 5% of the time, Pallas kernels for 18%

profile of v6, /device:TPU:2, one launch (start us, length us, event | category | flops | bytes accessed | tf_op | source)
XLA Modules:
  0.0 146.3 jit_solution(14397732579726747618)
XLA Ops:
  0.7 2.8 %shard_map.119 = bf16[256,1280]{1,0:T(8,128)(2,1)} custom-call(s32[1,128]{1,0:T(1,128)} %bitcast.25, bf16[128,2048]{1,0:T(8,128)(2,1)} %refs_1_.1), custom_call_target="tpu_custom_call" | custom-call | tf_op jit(solution)/shard_map/pallas_call | solution.py:298
  3.5 11.6 %all-to-all-start = ((bf16[32,8,1280]{2,1,0:T(8,128)(2,1)}), bf16[32,8,1280]{2,1,0:T(8,128)(2,1)S(1)}, u32[]{:S(2)}, u32[]{:S(2)}) async-start(bf16[32,8,1280]{2,1,0:T(8,128)(2,1)} %bitcast.36), calls=%async_computation | async-start | bytes 1310720 | tf_op jit(solution)/shard_map/all_to_all | solution.py:308
  15.1 2.8 %shard_map.120 = bf16[256,1280]{1,0:T(8,128)(2,1)} custom-call(s32[1,128]{1,0:T(1,128)} %bitcast.26, bf16[1,128]{1,0:T(2,128)(2,1)} %bitcast.28, s32[1,128]{1,0:T(1,128)} %bitcast.37, bf16[128,2048]{1,0:T(8,128)(2,1)} %refs_3_.1), custom_call_target="tpu_custom_call" | custom-call | tf_op jit(solution)/shard_map/pallas_call | solution.py:298
  17.9 2.8 %pad_maximum_fusion.1 = bf16[576,2048]{1,0:T(8,128)(2,1)} fusion(bf16[192,2048]{1,0:T(8,128)(2,1)} %bitcast.34, bf16[192,2048]{1,0:T(8,128)(2,1)S(1)} %bitcast.30, bf16[192,2048]{1,0:T(8,128)(2,1)S(1)} %bitcast.32), kind=kLoop, calls=%fused_computation.1 | loop fusion | flops 7077888 | bytes 4718592 | tf_op jit(solution)/shard_map/concatenate | solution.py:315
  20.7 14.1 %all-to-all-done = bf16[32,8,1280]{2,1,0:T(8,128)(2,1)S(1)} async-done(((bf16[32,8,1280]{2,1,0:T(8,128)(2,1)}), bf16[32,8,1280]{2,1,0:T(8,128)(2,1)S(1)}, u32[]{:S(2)}, u32[]{:S(2)}) %all-to-all-start) | async-done | bytes 655392 | tf_op jit(solution)/shard_map/all_to_all | solution.py:308
  34.8 5.6 %all-to-all-start.1 = ((bf16[32,8,1280]{2,1,0:T(8,128)(2,1)}), bf16[32,8,1280]{2,1,0:T(8,128)(2,1)S(1)}, u32[]{:S(2)}, u32[]{:S(2)}) async-start(bf16[32,8,1280]{2,1,0:T(8,128)(2,1)} %bitcast.8), calls=%async_computation.1 | async-start | bytes 1310720 | tf_op jit(solution)/shard_map/all_to_all | solution.py:308
  40.3 0.9 fusion.1
  41.2 1.6 %collective-permute-start.1 = (bf16[128,1280]{1,0:T(8,128)(2,1)}, bf16[128,1280]{1,0:T(8,128)(2,1)}, u32[]{:S(2)}, u32[]{:S(2)}) collective-permute-start(bf16[128,1280]{1,0:T(8,128)(2,1)} %get-tuple-element.105), channel_id=1, source_target_pairs={{0,64},{64,128},{128,192},{192,0},{1,65},{65,129},{129,193},{193,1... | collective-permute-start | bytes 983048 | tf_op jit(solution)/shard_map/ppermute | solution.py:284
  42.8 1.7 %collective-permute-start.4 = (bf16[128,1280]{1,0:T(8,128)(2,1)}, bf16[128,1280]{1,0:T(8,128)(2,1)}, u32[]{:S(2)}, u32[]{:S(2)}) collective-permute-start(bf16[128,1280]{1,0:T(8,128)(2,1)} %get-tuple-element.104), channel_id=1, source_target_pairs={{0,192},{64,0},{128,64},{192,128},{1,193},{65,1},{129,65},{193,129... | collective-permute-start | bytes 983048 | tf_op jit(solution)/shard_map/ppermute | solution.py:284
  44.4 0.4 collective-permute-start.2
  44.8 2.9 %collective-permute-start.3 = (bf16[128,1280]{1,0:T(8,128)(2,1)}, bf16[128,1280]{1,0:T(8,128)(2,1)S(1)}, u32[]{:S(2)}, u32[]{:S(2)}) collective-permute-start(bf16[128,1280]{1,0:T(8,128)(2,1)} %get-tuple-element.105), channel_id=1, source_target_pairs={{0,192},{64,0},{128,64},{192,128},{1,193},{65,1},{129,65},{193,129... | collective-permute-start | bytes 983048 | tf_op jit(solution)/shard_map/ppermute | solution.py:284
  47.7 5.7 %collective-permute-done.1.refs_1_ = bf16[128,1280]{1,0:T(8,128)(2,1)} collective-permute-done((bf16[128,1280]{1,0:T(8,128)(2,1)}, bf16[128,1280]{1,0:T(8,128)(2,1)}, u32[]{:S(2)}, u32[]{:S(2)}) %collective-permute-start.1) | collective-permute-done | bytes 327712 | tf_op jit(solution)/shard_map/ppermute | solution.py:284
  53.4 0.4 collective-permute-start.6
  53.8 2.9 %collective-permute-start.7 = (bf16[128,1280]{1,0:T(8,128)(2,1)}, bf16[128,1280]{1,0:T(8,128)(2,1)}, u32[]{:S(2)}, u32[]{:S(2)}) collective-permute-start(bf16[128,1280]{1,0:T(8,128)(2,1)} %collective-permute-done.4.refs_4_), channel_id=1, source_target_pairs={{0,192},{64,0},{128,64},{192,128},{1,193},{65,1},{129,65},{193,129... | collective-permute-start | bytes 983048 | tf_op jit(solution)/shard_map/ppermute | solution.py:284
  56.6 2.4 %all-to-all-done.1 = bf16[32,8,1280]{2,1,0:T(8,128)(2,1)S(1)} async-done(((bf16[32,8,1280]{2,1,0:T(8,128)(2,1)}), bf16[32,8,1280]{2,1,0:T(8,128)(2,1)S(1)}, u32[]{:S(2)}, u32[]{:S(2)}) %all-to-all-start.1) | async-done | bytes 655392 | tf_op jit(solution)/shard_map/all_to_all | solution.py:308
  59.0 1.3 collective-permute-done.2.refs_2_
  60.3 0.4 collective-permute-start
  60.7 2.8 %collective-permute-start.10 = (bf16[128,1280]{1,0:T(8,128)(2,1)S(1)}, bf16[128,1280]{1,0:T(8,128)(2,1)S(1)}, u32[]{:S(2)}, u32[]{:S(2)}) collective-permute-start(bf16[128,1280]{1,0:T(8,128)(2,1)S(1)} %get-tuple-element.60), channel_id=1, source_target_pairs={{0,192},{64,0},{128,64},{192,128},{1,193},{65,1},{129,65},{193,129... | collective-permute-start | bytes 983048 | tf_op jit(solution)/shard_map/ppermute | solution.py:284
  63.5 1.8 %fusion = (bf16[192,2048]{1,0:T(8,128)(2,1)S(1)}, bf16[192,2048]{1,0:T(8,128)(2,1)S(1)}, bf16[192,2048]{1,0:T(8,128)(2,1)S(1)}) fusion(bf16[576,2048]{1,0:T(8,128)(2,1)} %collective-permute-done.5), kind=kLoop, calls=%fused_computation.10 | loop fusion | bytes 4718592 | tf_op jit(solution)/shard_map/slice | solution.py:316
  65.3 0.3 pad_maximum_fusion.refs_5_.refs_8_.refs_2_
  65.6 0.7 copy-done.10
  66.4 1.0 copy-done.9
  67.3 1.0 copy-done.11
  68.3 3.5 %shard_map.121 = (bf16[480,2048]{1,0:T(8,128)(2,1)S(1)}, bf16[480,384]{1,0:T(8,128)(2,1)S(1)}, f32[480,384]{1,0:T(8,128)S(1)}, f32[480,384]{1,0:T(8,128)S(1)}) custom-call(bf16[256,1280]{1,0:T(8,128)(2,1)S(1)} %bitcast.23, bf16[128,1280]{1,0:T(8,128)(2,1)} %collective-permute-done.1.refs_1_, bf16[128,1280]{1,0:T(8,128)(2,1)S(1)} %copy-done.9, ...), custom_call_target="tpu_custom_call" | custom-call | flops 1000 | bytes 1000 | tf_op jit(solution)/shard_map/pallas_call | solution.py:178
  71.8 0.3 collective-permute-start.8
  72.1 3.2 %collective-permute-start.9 = (bf16[128,1280]{1,0:T(8,128)(2,1)S(1)}, bf16[128,1280]{1,0:T(8,128)(2,1)S(1)}, u32[]{:S(2)}, u32[]{:S(2)}) collective-permute-start(bf16[128,1280]{1,0:T(8,128)(2,1)S(1)} %get-tuple-element.61), channel_id=1, source_target_pairs={{0,192},{64,0},{128,64},{192,128},{1,193},{65,1},{129,65},{193,129... | collective-permute-start | bytes 983048 | tf_op jit(solution)/shard_map/ppermute | solution.py:284
  75.4 3.2 %collective-permute-start.12 = (bf16[128,1280]{1,0:T(8,128)(2,1)S(1)}, bf16[128,1280]{1,0:T(8,128)(2,1)S(1)}, u32[]{:S(2)}, u32[]{:S(2)}) collective-permute-start(bf16[128,1280]{1,0:T(8,128)(2,1)S(1)} %collective-permute-done.10.refs_4_), channel_id=1, source_target_pairs={{0,192},{64,0},{128,64},{192,128},{1,193},{65,1},{129,65},{193,129... | collective-permute-start | bytes 983048 | tf_op jit(solution)/shard_map/ppermute | solution.py:284
  78.6 0.1 pad_maximum_fusion.2.refs_9_.refs_6_
  78.7 2.6 %shard_map.123 = (bf16[160,2048]{1,0:T(8,128)(2,1)S(1)}, bf16[160,384]{1,0:T(8,128)(2,1)S(1)}, f32[160,384]{1,0:T(8,128)S(1)}, f32[160,384]{1,0:T(8,128)S(1)}) custom-call(bf16[128,1280]{1,0:T(8,128)(2,1)} %collective-permute-done.6.refs_0_, bf16[128,1280]{1,0:T(8,128)(2,1)} %collective-permute-done.7.refs_1_, ...), custom_call_target="tpu_custom_call" | custom-call | flops 1000 | bytes 1000 | tf_op jit(solution)/shard_map/pallas_call | solution.py:178
  81.4 0.8 collective-permute-done.8.refs_2_
  82.2 4.2 %shard_map.122 = (bf16[128,1408]{1,0:T(8,128)(2,1)S(1)}, bf16[128,1408]{1,0:T(8,128)(2,1)S(1)}, bf16[128,1408]{1,0:T(8,128)(2,1)S(1)}, bf16[128,1408]{1,0:T(8,12...) custom-call(bf16[256,1280]{1,0:T(8,128)(2,1)S(1)} %bitcast.21, ...), custom_call_target="tpu_custom_call" | custom-call | flops 1000 | bytes 1000 | tf_op jit(solution)/shard_map/pallas_call | solution.py:230
  86.4 1.9 %shard_map.124 = (bf16[128,1408]{1,0:T(8,128)(2,1)S(1)}, bf16[128,1408]{1,0:T(8,128)(2,1)S(1)}, bf16[160,2048]{1,0:T(8,128)(2,1)S(1)}, bf16[160,768]{1,0:T(8,128)(2,1)S(1)}) custom-call(bf16[128,1280]{1,0:T(8,128)(2,1)S(1)} %collective-permute-done.11.refs_0_, bf16[128,1280]{1,0:T(8,128)(2,1)S(1)} %collective-permute-done.12.refs_1_, ...), custom_call_target="tpu_custom_call" | custom-call | flops 1000 | bytes 1000 | tf_op jit(solution)/shard_map/pallas_call | solution.py:230
  88.4 1.4 collective-permute-start.16
  89.8 1.6 %collective-permute-start.18 = (bf16[128,1408]{1,0:T(8,128)(2,1)S(1)}, bf16[128,1408]{1,0:T(8,128)(2,1)S(1)}, u32[]{:S(2)}, u32[]{:S(2)}) collective-permute-start(bf16[128,1408]{1,0:T(8,128)(2,1)S(1)} %get-tuple-element.79), channel_id=1, source_target_pairs={{0,64},{64,128},{128,192},{192,0},{1,65},{65,129},{129,193},{193,1... | collective-permute-start | bytes 1081352 | tf_op jit(solution)/shard_map/ppermute | solution.py:284
  91.3 1.7 %collective-permute-start.14 = (bf16[128,1408]{1,0:T(8,128)(2,1)S(1)}, bf16[128,1408]{1,0:T(8,128)(2,1)S(1)}, u32[]{:S(2)}, u32[]{:S(2)}) collective-permute-start(bf16[128,1408]{1,0:T(8,128)(2,1)S(1)} %get-tuple-element.76), channel_id=1, source_target_pairs={{0,192},{64,0},{128,64},{192,128},{1,193},{65,1},{129,65},{193,129... | collective-permute-start | bytes 1081352 | tf_op jit(solution)/shard_map/ppermute | solution.py:284
  93.0 0.7 collective-permute-start.13
  93.7 7.3 %collective-permute-done.16 = bf16[128,1408]{1,0:T(8,128)(2,1)S(1)} collective-permute-done((bf16[128,1408]{1,0:T(8,128)(2,1)S(1)}, bf16[128,1408]{1,0:T(8,128)(2,1)S(1)}, u32[]{:S(2)}, u32[]{:S(2)}) %collective-permute-start.16) | collective-permute-done | bytes 360480 | tf_op jit(solution)/shard_map/ppermute | solution.py:284
  101.1 0.4 collective-permute-start.17
  101.5 1.2 collective-permute-done.14
  102.8 3.0 %collective-permute-start.15 = (bf16[128,1408]{1,0:T(8,128)(2,1)S(1)}, bf16[128,1408]{1,0:T(8,128)(2,1)S(1)}, u32[]{:S(2)}, u32[]{:S(2)}) collective-permute-start(bf16[128,1408]{1,0:T(8,128)(2,1)S(1)} %add_convert_fusion.3), channel_id=1, source_target_pairs={{0,192},{64,0},{128,64},{192,128},{1,193},{65,1},{129,65},{193,129... | collective-permute-start | bytes 1081352 | tf_op jit(solution)/shard_map/ppermute | solution.py:284
  105.7 5.8 %shard_map.125 = bf16[576,2048]{1,0:T(8,128)(2,1)} custom-call(bf16[480,384]{1,0:T(8,128)(2,1)S(1)} %get-tuple-element.62.refs_5_.hid1, bf16[160,384]{1,0:T(8,128)(2,1)S(1)} %get-tuple-element.73.refs_2_.hid2, bf16[480,768]{1,0:T(8,128)(2,1)S(1)} %get-tuple-element.80.d1, bf16[160,768]{1,0:T(8,128)(2,1)S(1)} %get-tuple-element.81.d2, ...), custom_call_target="tpu_custom_call" | custom-call | flops 3019898880 | bytes 1000 | tf_op jit(solution)/shard_map/pallas_call | solution.py:266
  111.6 0.5 collective-permute-done.15
  112.1 0.3 add_convert_fusion
  112.4 1.0 maximum_bitcast_fusion
  113.3 9.8 %all-to-all-start.2 = ((bf16[32,8,1408]{2,1,0:T(8,128)(2,1)}), bf16[32,8,1408]{2,1,0:T(8,128)(2,1)S(1)}, u32[]{:S(2)}, u32[]{:S(2)}) async-start(bf16[32,8,1408]{2,1,0:T(8,128)(2,1)} %maximum_bitcast_fusion), calls=%async_computation.2 | async-start | bytes 1441792 | tf_op jit(solution)/shard_map/all_to_all | solution.py:308
  123.2 7.4 %shard_map.126 = (bf16[192,2048]{1,0:T(8,128)(2,1)}, bf16[192,2048]{1,0:T(8,128)(2,1)}, bf16[192,2048]{1,0:T(8,128)(2,1)}) custom-call(bf16[480,384]{1,0:T(8,128)(2,1)S(1)} %copy-done.3, bf16[160,384]{1,0:T(8,128)(2,1)S(1)} %get-tuple-element.73.refs_2_.hid2, bf16[480,768]{1,0:T(8,128)(2,1)} %copy-done.4, bf16[160,768]{1,0:T(8,128)(2,1)S(1)} %copy-done.13, ...), custom_call_target="tpu_custom_call" | custom-call | flops 1000 | bytes 1000 | tf_op jit(solution)/shard_map/pallas_call | solution.py:266
  130.7 14.2 %all-to-all-done.2 = bf16[32,8,1408]{2,1,0:T(8,128)(2,1)S(1)} async-done(((bf16[32,8,1408]{2,1,0:T(8,128)(2,1)}), bf16[32,8,1408]{2,1,0:T(8,128)(2,1)S(1)}, u32[]{:S(2)}, u32[]{:S(2)}) %all-to-all-start.2) | async-done | bytes 720928 | tf_op jit(solution)/shard_map/all_to_all | solution.py:308
  144.9 1.4 shard_map.127
  (55 shorter events, 0.4 us)
Async XLA Ops:
  0.6 17.3 %copy-start.17 = (bf16[1,192,2048]{2,1,0:T(8,128)(2,1)S(1)}, bf16[1,192,2048]{2,1,0:T(8,128)(2,1)}, u32[]{:S(2)}) copy-start(bf16[1,192,2048]{2,1,0:T(8,128)(2,1)} %param.13) | copy-start | bytes 2359300
  0.6 17.3 %copy-start.16 = (bf16[1,192,2048]{2,1,0:T(8,128)(2,1)S(1)}, bf16[1,192,2048]{2,1,0:T(8,128)(2,1)}, u32[]{:S(2)}) copy-start(bf16[1,192,2048]{2,1,0:T(8,128)(2,1)} %param.14) | copy-start | bytes 2359300
  3.5 31.3 %all-to-all-start = ((bf16[32,8,1280]{2,1,0:T(8,128)(2,1)}), bf16[32,8,1280]{2,1,0:T(8,128)(2,1)S(1)}, u32[]{:S(2)}, u32[]{:S(2)}) async-start(bf16[32,8,1280]{2,1,0:T(8,128)(2,1)} %bitcast.36), calls=%async_computation | async-start | bytes 1310720 | tf_op jit(solution)/shard_map/all_to_all | solution.py:308
  20.7 40.1 %collective-permute-start.5 = (bf16[576,2048]{1,0:T(8,128)(2,1)}, bf16[576,2048]{1,0:T(8,128)(2,1)}, u32[]{:S(2)}, u32[]{:S(2)}) collective-permute-start(bf16[576,2048]{1,0:T(8,128)(2,1)} %pad_maximum_fusion.1), channel_id=1, source_target_pairs={{0,32},{32,0},{1,33},{33,1},{2,34},{34,2},{3,35},{35,3},{4,36},{36... | collective-permute-start | bytes 7077896 | tf_op jit(solution)/shard_map/ppermute | solution.py:284
  34.8 24.2 %all-to-all-start.1 = ((bf16[32,8,1280]{2,1,0:T(8,128)(2,1)}), bf16[32,8,1280]{2,1,0:T(8,128)(2,1)S(1)}, u32[]{:S(2)}, u32[]{:S(2)}) async-start(bf16[32,8,1280]{2,1,0:T(8,128)(2,1)} %bitcast.8), calls=%async_computation.1 | async-start | bytes 1310720 | tf_op jit(solution)/shard_map/all_to_all | solution.py:308
  41.2 12.2 %collective-permute-start.1 = (bf16[128,1280]{1,0:T(8,128)(2,1)}, bf16[128,1280]{1,0:T(8,128)(2,1)}, u32[]{:S(2)}, u32[]{:S(2)}) collective-permute-start(bf16[128,1280]{1,0:T(8,128)(2,1)} %get-tuple-element.105), channel_id=1, source_target_pairs={{0,64},{64,128},{128,192},{192,0},{1,65},{65,129},{129,193},{193,1... | collective-permute-start | bytes 983048 | tf_op jit(solution)/shard_map/ppermute | solution.py:284
  42.8 11.0 %collective-permute-start.4 = (bf16[128,1280]{1,0:T(8,128)(2,1)}, bf16[128,1280]{1,0:T(8,128)(2,1)}, u32[]{:S(2)}, u32[]{:S(2)}) collective-permute-start(bf16[128,1280]{1,0:T(8,128)(2,1)} %get-tuple-element.104), channel_id=1, source_target_pairs={{0,192},{64,0},{128,64},{192,128},{1,193},{65,1},{129,65},{193,129... | collective-permute-start | bytes 983048 | tf_op jit(solution)/shard_map/ppermute | solution.py:284
  44.4 15.9 %collective-permute-start.2 = (bf16[128,1280]{1,0:T(8,128)(2,1)}, bf16[128,1280]{1,0:T(8,128)(2,1)S(1)}, u32[]{:S(2)}, u32[]{:S(2)}) collective-permute-start(bf16[128,1280]{1,0:T(8,128)(2,1)} %get-tuple-element.104), channel_id=1, source_target_pairs={{0,64},{64,128},{128,192},{192,0},{1,65},{65,129},{129,193},{193,1... | collective-permute-start | bytes 983048 | tf_op jit(solution)/shard_map/ppermute | solution.py:284
  44.8 20.8 %collective-permute-start.3 = (bf16[128,1280]{1,0:T(8,128)(2,1)}, bf16[128,1280]{1,0:T(8,128)(2,1)S(1)}, u32[]{:S(2)}, u32[]{:S(2)}) collective-permute-start(bf16[128,1280]{1,0:T(8,128)(2,1)} %get-tuple-element.105), channel_id=1, source_target_pairs={{0,192},{64,0},{128,64},{192,128},{1,193},{65,1},{129,65},{193,129... | collective-permute-start | bytes 983048 | tf_op jit(solution)/shard_map/ppermute | solution.py:284
  53.4 18.4 %collective-permute-start.6 = (bf16[128,1280]{1,0:T(8,128)(2,1)}, bf16[128,1280]{1,0:T(8,128)(2,1)}, u32[]{:S(2)}, u32[]{:S(2)}) collective-permute-start(bf16[128,1280]{1,0:T(8,128)(2,1)} %collective-permute-done.1.refs_1_), channel_id=1, source_target_pairs={{0,64},{64,128},{128,192},{192,0},{1,65},{65,129},{129,193},{193,1... | collective-permute-start | bytes 983048 | tf_op jit(solution)/shard_map/ppermute | solution.py:284
  53.8 18.1 %collective-permute-start.7 = (bf16[128,1280]{1,0:T(8,128)(2,1)}, bf16[128,1280]{1,0:T(8,128)(2,1)}, u32[]{:S(2)}, u32[]{:S(2)}) collective-permute-start(bf16[128,1280]{1,0:T(8,128)(2,1)} %collective-permute-done.4.refs_4_), channel_id=1, source_target_pairs={{0,192},{64,0},{128,64},{192,128},{1,193},{65,1},{129,65},{193,129... | collective-permute-start | bytes 983048 | tf_op jit(solution)/shard_map/ppermute | solution.py:284
  60.3 5.3 %copy-start.8 = (bf16[128,1280]{1,0:T(8,128)(2,1)}, bf16[128,1280]{1,0:T(8,128)(2,1)S(1)}, u32[]{:S(2)}) copy-start(bf16[128,1280]{1,0:T(8,128)(2,1)S(1)} %collective-permute-done.2.refs_2_) | copy-start | bytes 983044
  60.3 15.0 %collective-permute-start = (bf16[128,1280]{1,0:T(8,128)(2,1)S(1)}, bf16[128,1280]{1,0:T(8,128)(2,1)S(1)}, u32[]{:S(2)}, u32[]{:S(2)}) collective-permute-start(bf16[128,1280]{1,0:T(8,128)(2,1)S(1)} %get-tuple-element.61), channel_id=1, source_target_pairs={{0,64},{64,128},{128,192},{192,0},{1,65},{65,129},{129,193},{193,1... | collective-permute-start | bytes 983048 | tf_op jit(solution)/shard_map/ppermute | solution.py:284
  60.7 14.6 %collective-permute-start.10 = (bf16[128,1280]{1,0:T(8,128)(2,1)S(1)}, bf16[128,1280]{1,0:T(8,128)(2,1)S(1)}, u32[]{:S(2)}, u32[]{:S(2)}) collective-permute-start(bf16[128,1280]{1,0:T(8,128)(2,1)S(1)} %get-tuple-element.60), channel_id=1, source_target_pairs={{0,192},{64,0},{128,64},{192,128},{1,193},{65,1},{129,65},{193,129... | collective-permute-start | bytes 983048 | tf_op jit(solution)/shard_map/ppermute | solution.py:284
  65.6 0.7 copy-start.10
  66.4 1.0 copy-start.9
  67.3 1.0 copy-start.11
  68.3 10.3 %copy-start.18 = (bf16[1,192,2048]{2,1,0:T(8,128)(2,1)S(1)}, bf16[1,192,2048]{2,1,0:T(8,128)(2,1)}, u32[]{:S(2)}) copy-start(bf16[1,192,2048]{2,1,0:T(8,128)(2,1)} %param.15) | copy-start | bytes 2359300
  71.8 33.9 %copy-start = (bf16[480,2048]{1,0:T(8,128)(2,1)}, bf16[480,2048]{1,0:T(8,128)(2,1)S(1)}, u32[]{:S(2)}) copy-start(bf16[480,2048]{1,0:T(8,128)(2,1)S(1)} %get-tuple-element.82.x1) | copy-start | bytes 5898244
  71.8 33.9 %copy-start.2 = (bf16[480,384]{1,0:T(8,128)(2,1)}, bf16[480,384]{1,0:T(8,128)(2,1)S(1)}, u32[]{:S(2)}) copy-start(bf16[480,384]{1,0:T(8,128)(2,1)S(1)} %get-tuple-element.62.refs_5_.hid1) | copy-start | bytes 1105924
  71.8 10.3 %collective-permute-start.8 = (bf16[128,1280]{1,0:T(8,128)(2,1)S(1)}, bf16[128,1280]{1,0:T(8,128)(2,1)S(1)}, u32[]{:S(2)}, u32[]{:S(2)}) collective-permute-start(bf16[128,1280]{1,0:T(8,128)(2,1)S(1)} %get-tuple-element.60), channel_id=1, source_target_pairs={{0,64},{64,128},{128,192},{192,0},{1,65},{65,129},{129,193},{193,1... | collective-permute-start | bytes 983048 | tf_op jit(solution)/shard_map/ppermute | solution.py:284
  72.1 10.1 %collective-permute-start.9 = (bf16[128,1280]{1,0:T(8,128)(2,1)S(1)}, bf16[128,1280]{1,0:T(8,128)(2,1)S(1)}, u32[]{:S(2)}, u32[]{:S(2)}) collective-permute-start(bf16[128,1280]{1,0:T(8,128)(2,1)S(1)} %get-tuple-element.61), channel_id=1, source_target_pairs={{0,192},{64,0},{128,64},{192,128},{1,193},{65,1},{129,65},{193,129... | collective-permute-start | bytes 983048 | tf_op jit(solution)/shard_map/ppermute | solution.py:284
  75.3 11.1 %collective-permute-start.11 = (bf16[128,1280]{1,0:T(8,128)(2,1)S(1)}, bf16[128,1280]{1,0:T(8,128)(2,1)S(1)}, u32[]{:S(2)}, u32[]{:S(2)}) collective-permute-start(bf16[128,1280]{1,0:T(8,128)(2,1)S(1)} %collective-permute-done.refs_1_), channel_id=1, source_target_pairs={{0,64},{64,128},{128,192},{192,0},{1,65},{65,129},{129,193},{193,1... | collective-permute-start | bytes 983048 | tf_op jit(solution)/shard_map/ppermute | solution.py:284
  75.4 11.1 %collective-permute-start.12 = (bf16[128,1280]{1,0:T(8,128)(2,1)S(1)}, bf16[128,1280]{1,0:T(8,128)(2,1)S(1)}, u32[]{:S(2)}, u32[]{:S(2)}) collective-permute-start(bf16[128,1280]{1,0:T(8,128)(2,1)S(1)} %collective-permute-done.10.refs_4_), channel_id=1, source_target_pairs={{0,192},{64,0},{128,64},{192,128},{1,193},{65,1},{129,65},{193,129... | collective-permute-start | bytes 983048 | tf_op jit(solution)/shard_map/ppermute | solution.py:284
  81.3 24.4 %copy-start.5 = (bf16[160,2048]{1,0:T(8,128)(2,1)}, bf16[160,2048]{1,0:T(8,128)(2,1)S(1)}, u32[]{:S(2)}) copy-start(bf16[160,2048]{1,0:T(8,128)(2,1)S(1)} %get-tuple-element.83.x2) | copy-start | bytes 1966084
  86.4 19.3 %copy-start.1 = (bf16[480,2048]{1,0:T(8,128)(2,1)}, bf16[480,2048]{1,0:T(8,128)(2,1)S(1)}, u32[]{:S(2)}) copy-start(bf16[480,2048]{1,0:T(8,128)(2,1)S(1)} %get-tuple-element.84.dy1) | copy-start | bytes 5898244
  86.4 19.3 %copy-start.4 = (bf16[480,768]{1,0:T(8,128)(2,1)}, bf16[480,768]{1,0:T(8,128)(2,1)S(1)}, u32[]{:S(2)}) copy-start(bf16[480,768]{1,0:T(8,128)(2,1)S(1)} %get-tuple-element.80.d1) | copy-start | bytes 2211844
  88.3 23.3 %copy-start.7 = (bf16[160,2048]{1,0:T(8,128)(2,1)}, bf16[160,2048]{1,0:T(8,128)(2,1)S(1)}, u32[]{:S(2)}) copy-start(bf16[160,2048]{1,0:T(8,128)(2,1)S(1)} %get-tuple-element.85.dy2) | copy-start | bytes 1966084
  88.3 23.2 %copy-start.12 = (bf16[160,768]{1,0:T(8,128)(2,1)}, bf16[160,768]{1,0:T(8,128)(2,1)S(1)}, u32[]{:S(2)}) copy-start(bf16[160,768]{1,0:T(8,128)(2,1)S(1)} %get-tuple-element.81.d2) | copy-start | bytes 737284
  88.4 12.6 %collective-permute-start.16 = (bf16[128,1408]{1,0:T(8,128)(2,1)S(1)}, bf16[128,1408]{1,0:T(8,128)(2,1)S(1)}, u32[]{:S(2)}, u32[]{:S(2)}) collective-permute-start(bf16[128,1408]{1,0:T(8,128)(2,1)S(1)} %get-tuple-element.78), channel_id=1, source_target_pairs={{0,64},{64,128},{128,192},{192,0},{1,65},{65,129},{129,193},{193,1... | collective-permute-start | bytes 1081352 | tf_op jit(solution)/shard_map/ppermute | solution.py:284
  89.8 21.8 %collective-permute-start.18 = (bf16[128,1408]{1,0:T(8,128)(2,1)S(1)}, bf16[128,1408]{1,0:T(8,128)(2,1)S(1)}, u32[]{:S(2)}, u32[]{:S(2)}) collective-permute-start(bf16[128,1408]{1,0:T(8,128)(2,1)S(1)} %get-tuple-element.79), channel_id=1, source_target_pairs={{0,64},{64,128},{128,192},{192,0},{1,65},{65,129},{129,193},{193,1... | collective-permute-start | bytes 1081352 | tf_op jit(solution)/shard_map/ppermute | solution.py:284
  91.3 11.4 %collective-permute-start.14 = (bf16[128,1408]{1,0:T(8,128)(2,1)S(1)}, bf16[128,1408]{1,0:T(8,128)(2,1)S(1)}, u32[]{:S(2)}, u32[]{:S(2)}) collective-permute-start(bf16[128,1408]{1,0:T(8,128)(2,1)S(1)} %get-tuple-element.76), channel_id=1, source_target_pairs={{0,192},{64,0},{128,64},{192,128},{1,193},{65,1},{129,65},{193,129... | collective-permute-start | bytes 1081352 | tf_op jit(solution)/shard_map/ppermute | solution.py:284
  93.0 18.6 %collective-permute-start.13 = (bf16[128,1408]{1,0:T(8,128)(2,1)S(1)}, bf16[128,1408]{1,0:T(8,128)(2,1)S(1)}, u32[]{:S(2)}, u32[]{:S(2)}) collective-permute-start(bf16[128,1408]{1,0:T(8,128)(2,1)S(1)} %get-tuple-element.67), channel_id=1, source_target_pairs={{0,192},{64,0},{128,64},{192,128},{1,193},{65,1},{129,65},{193,129... | collective-permute-start | bytes 1081352 | tf_op jit(solution)/shard_map/ppermute | solution.py:284
  101.1 10.5 %collective-permute-start.17 = (bf16[128,1408]{1,0:T(8,128)(2,1)S(1)}, bf16[128,1408]{1,0:T(8,128)(2,1)S(1)}, u32[]{:S(2)}, u32[]{:S(2)}) collective-permute-start(bf16[128,1408]{1,0:T(8,128)(2,1)S(1)} %add_convert_fusion.2), channel_id=1, source_target_pairs={{0,64},{64,128},{128,192},{192,0},{1,65},{65,129},{129,193},{193,1... | collective-permute-start | bytes 1081352 | tf_op jit(solution)/shard_map/ppermute | solution.py:284
  102.8 9.4 %collective-permute-start.15 = (bf16[128,1408]{1,0:T(8,128)(2,1)S(1)}, bf16[128,1408]{1,0:T(8,128)(2,1)S(1)}, u32[]{:S(2)}, u32[]{:S(2)}) collective-permute-start(bf16[128,1408]{1,0:T(8,128)(2,1)S(1)} %add_convert_fusion.3), channel_id=1, source_target_pairs={{0,192},{64,0},{128,64},{192,128},{1,193},{65,1},{129,65},{193,129... | collective-permute-start | bytes 1081352 | tf_op jit(solution)/shard_map/ppermute | solution.py:284
  111.6 11.6 %copy-start.3 = (bf16[480,384]{1,0:T(8,128)(2,1)S(1)}, bf16[480,384]{1,0:T(8,128)(2,1)}, u32[]{:S(2)}) copy-start(bf16[480,384]{1,0:T(8,128)(2,1)} %copy-done.2) | copy-start | bytes 1105924
  111.6 11.6 %copy-start.6 = (bf16[160,2048]{1,0:T(8,128)(2,1)S(1)}, bf16[160,2048]{1,0:T(8,128)(2,1)}, u32[]{:S(2)}) copy-start(bf16[160,2048]{1,0:T(8,128)(2,1)} %copy-done.5) | copy-start | bytes 1966084
  111.6 11.6 %copy-start.13 = (bf16[160,768]{1,0:T(8,128)(2,1)S(1)}, bf16[160,768]{1,0:T(8,128)(2,1)}, u32[]{:S(2)}) copy-start(bf16[160,768]{1,0:T(8,128)(2,1)} %copy-done.12) | copy-start | bytes 737284
  112.1 11.1 %collective-permute-start.19 = (bf16[576,2048]{1,0:T(8,128)(2,1)}, bf16[576,2048]{1,0:T(8,128)(2,1)}, u32[]{:S(2)}, u32[]{:S(2)}) collective-permute-start(bf16[576,2048]{1,0:T(8,128)(2,1)} %shard_map.125), channel_id=1, source_target_pairs={{0,32},{32,0},{1,33},{33,1},{2,34},{34,2},{3,35},{35,3},{4,36},{36... | collective-permute-start | bytes 7077896 | tf_op jit(solution)/shard_map/ppermute | solution.py:284
  113.3 31.5 %all-to-all-start.2 = ((bf16[32,8,1408]{2,1,0:T(8,128)(2,1)}), bf16[32,8,1408]{2,1,0:T(8,128)(2,1)S(1)}, u32[]{:S(2)}, u32[]{:S(2)}) async-start(bf16[32,8,1408]{2,1,0:T(8,128)(2,1)} %maximum_bitcast_fusion), calls=%async_computation.2 | async-start | bytes 1441792 | tf_op jit(solution)/shard_map/all_to_all | solution.py:308
  123.2 21.7 %copy-start.14 = (s32[128,1]{0,1:T(1,128)S(1)}, s32[128,1]{0,1:T(1,128)}, u32[]{:S(2)}) copy-start(s32[128,1]{0,1:T(1,128)} %param.10) | copy-start | bytes 1540
  123.2 21.7 %copy-start.15 = (bf16[128,1]{0,1:T(2,128)(2,1)S(1)}, bf16[128,1]{0,1:T(2,128)(2,1)}, u32[]{:S(2)}) copy-start(bf16[128,1]{0,1:T(2,128)(2,1)} %param.11) | copy-start | bytes 772
